TPU v7x, 32 devices: a whole 2x2x4 slice. The times are simulated.
32 devices in a mesh: box: 2 (over y), gy: 4 (over z), gz: 4 (over x, core).
Axes of the slice: x: 2, y: 2, z: 4, core: 2. Of those that a mesh axis runs over, the one named last changes fastest.
Arguments:
- velocity: float32 [2, 3, 32, 64, 512], P('box', None, 'gz', 'gy'), may hold values from -6 to 6
- turbine_cells: int32 [4, 4, 512], P('gz', 'gy'), may hold values from 0 to 65535, as said below
- turbine_count: int32 [4, 4], P('gz', 'gy'), may hold values from 0 to 512, as said below
- fringe_start: int32 [1], replicated, may hold values from 0 to 384
Outputs:
- advanced: float32 [2, 3, 32, 64, 512], P('box', None, 'gz', 'gy')
Inputs may be any that keep to these rules, and one draw needn't show every extreme that they name: `turbine_cells`: flat indices into one device's block of 8 x 16 x 512 cells; cells may repeat. `turbine_count`: some device block has all 512 slots live; others have any number.
All inputs are finite; a program needn't handle non-finite values.
Results may differ from a plain program's by a relative error of at most 0.0003.
Values sent between devices are 32-bit elements; how exact they have to be, the bound alone decides.
No kernel may reach another device: no remote copies, remote signals or barrier semaphores. Data moves between devices by JAX's collectives and lax.ppermute only.
A program may use at most 64 MiB of HBM per device.

v0:
```python
import jax
import jax.numpy as jnp
from jax import lax
from jax.sharding import PartitionSpec as P

FW = 128


smag_coef = 0.1024
drag_coef = 0.665
time_step = 0.2
tau_table = ((0, 3, 4), (3, 1, 5), (4, 5, 2))
pair_table = ((0, 0), (1, 1), (2, 2), (0, 1), (0, 2), (1, 2))


def extended(block, sides, width, periodic):
    for axis, dim in sides:
        count = lax.axis_size(axis)
        forward = [(i, i + 1) for i in range(count - 1)]
        if periodic:
            forward.append((count - 1, 0))
        backward = [(target, source) for source, target in forward]
        low = lax.ppermute(
            lax.slice_in_dim(block, block.shape[dim] - width, None, axis=dim), axis, forward
        )
        high = lax.ppermute(lax.slice_in_dim(block, 0, width, axis=dim), axis, backward)
        block = jnp.concatenate([low, block, high], axis=dim)
    return block


def shifted(value, axis, by):
    devices = lax.axis_size(axis)
    pairs = [(i, i + by) for i in range(devices) if 0 <= i + by < devices]
    return lax.ppermute(value, axis, pairs)


def xdiff(field):
    return (jnp.roll(field, -1, -1) - jnp.roll(field, 1, -1)) * 0.5


def sdiff(field, axis):
    count = field.shape[axis]
    return (
        lax.slice_in_dim(field, 2, count, axis=axis)
        - lax.slice_in_dim(field, 0, count - 2, axis=axis)
    ) * 0.5


def stress(grads):
    rates = [0.5 * (grads[j][i] + grads[i][j]) for i, j in pair_table]
    squares = rates[0] * rates[0] + rates[1] * rates[1] + rates[2] * rates[2]
    squares = squares + 2.0 * (rates[3] * rates[3] + rates[4] * rates[4] + rates[5] * rates[5])
    visc = smag_coef * jnp.sqrt(2.0 * squares)
    return jnp.stack([2.0 * visc * rate for rate in rates])


def divergence(tau_x, tau_y, tau_z):
    parts = []
    for i in range(3):
        term = xdiff(tau_x[tau_table[i][0]])
        term = term + sdiff(tau_y[tau_table[i][1]], 1)
        term = term + sdiff(tau_z[tau_table[i][2]], 0)
        parts.append(term)
    return jnp.stack(parts)


def advection(center, grads):
    return center[0] * grads[0] + center[1] * grads[1] + center[2] * grads[2]


def drag_force(ux, cells, count, is_main):
    flat = ux.reshape(-1)
    vals = flat[cells]
    live = jnp.arange(cells.shape[0]) < count
    force = jnp.where(live, -drag_coef * vals * jnp.abs(vals), 0.0)
    spread = jnp.zeros_like(flat).at[cells].add(force).reshape(ux.shape)
    return spread * is_main


def section_rates(field, cells, count, is_main):
    depth = field.shape[1]
    wide = extended(field, (("gy", 2),), 2, True)
    whole = extended(wide, (("gz", 1),), 2, False)
    inner = whole[:, 1:-1, 1:-1]
    grads = [xdiff(inner), sdiff(whole[:, 1:-1], 2), sdiff(whole[:, :, 1:-1], 1)]
    tau = stress(grads)
    height = depth * lax.axis_size("gz")
    levels = lax.axis_index("gz") * depth - 1 + jnp.arange(depth + 2)
    inside = ((levels >= 0) & (levels < height)).astype(jnp.float32)
    tau = tau * inside[None, :, None, None]
    div = divergence(tau[:, 1:-1, 1:-1], tau[:, 1:-1, :], tau[:, :, 1:-1])
    center_grads = [grad[:, 1:-1, 1:-1] for grad in grads]
    result = div - advection(field, center_grads)
    return result.at[0].add(drag_force(field[0], cells, count, is_main))


def blend(field, start, is_main):
    width = FW
    arrived = shifted(field, "box", 1)
    cols = jnp.arange(field.shape[3])
    inside = (cols >= start) & (cols < start + width) & (is_main > 0.5)
    return jnp.where(inside, 0.5 * (field + arrived), field)


def per_device(velocity, turbine_cells, turbine_count, fringe_start):
    field = velocity[0]
    cells = turbine_cells.reshape(-1)
    count = turbine_count.reshape(())
    start = fringe_start[0]
    is_main = (lax.axis_index("box") == 1).astype(jnp.float32)
    first = blend(field + time_step * section_rates(field, cells, count, is_main), start, is_main)
    second = blend(
        0.75 * field + 0.25 * (first + time_step * section_rates(first, cells, count, is_main)),
        start,
        is_main,
    )
    third = 1.0 / 3.0 * field + 2.0 / 3.0 * (
        second + time_step * section_rates(second, cells, count, is_main)
    )
    return blend(third, start, is_main)[None]


def solution(mesh):
    placed = (P("box", None, "gz", "gy", None), P("gz", "gy", None), P("gz", "gy"), P())
    return jax.shard_map(
        per_device,
        mesh=mesh,
        in_specs=placed,
        out_specs=P("box", None, "gz", "gy", None),
        check_vma=False,
    )
```

profile of v0, /device:TPU:5, one launch (start us, length us, event | category | flops | bytes accessed | tf_op | source)
XLA Modules:
  0.0 144.5 jit_solution(2624824530739770969)
XLA Ops:
  0.0 1.2 fusion.106
  1.2 1.3 collective-permute-start
  2.6 2.1 %collective-permute-start.1 = (f32[3,8,2,512]{3,2,1,0:T(2,128)S(1)}, f32[3,8,2,512]{3,2,1,0:T(2,128)S(1)}, u32[]{:S(2)}, u32[]{:S(2)}) collective-permute-start(f32[3,8,2,512]{3,2,1,0:T(2,128)S(1)} %get-tuple-element.106), channel_id=1, source_target_pairs={{4,0},{8,4},{12,8},{0,12},{5,1},{9,5},{13,9},{1,13},{6,2},{10,6},{... | collective-permute-start | bytes 294920 | tf_op jit(solution)/shard_map/ppermute | solution.py:26
  4.7 1.2 fusion.105
  6.7 3.1 %gather_fusion = f32[512]{0:T(512)S(1)} fusion(f32[65536]{0:T(1024)S(1)} %bitcast.170, s32[1024]{0:T(1024)S(1)} %pad_clamp_fusion), kind=kCustom, calls=%fused_computation | custom fusion | bytes 6144 | tf_op jit(solution)/shard_map/gather | solution.py:73
  9.9 3.3 %scatter_custom_fusion = f32[65536]{0:T(1024)S(1)} fusion(s32[512]{0:T(512)S(1)} %bitcast.177, f32[512]{0:T(512)S(1)} %multiply_select_fusion.4, f32[]{:T(128)} %constant.113.clone.1), kind=kCustom, calls=%fused_computation.247 | custom fusion | flops 512 | bytes 262148 | tf_op jit(solution)/shard_map/scatter-add | solution.py:76
  13.4 4.1 %collective-permute-start.2 = (f32[3,2,20,512]{3,2,1,0:T(8,128)S(1)}, f32[3,2,20,512]{3,2,1,0:T(8,128)S(1)}, u32[]{:S(2)}, u32[]{:S(2)}) collective-permute-start(f32[3,2,20,512]{3,2,1,0:T(8,128)S(1)} %get-tuple-element.88), channel_id=1, source_target_pairs={{0,1},{1,2},{2,3},{4,5},{5,6},{6,7},{8,9},{9,10},{10,11},{12,13},{... | collective-permute-start | bytes 737288 | tf_op jit(solution)/shard_map/ppermute | solution.py:23
  17.5 1.9 %collective-permute-start.3 = (f32[3,2,20,512]{3,2,1,0:T(8,128)S(1)}, f32[3,2,20,512]{3,2,1,0:T(8,128)S(1)}, u32[]{:S(2)}, u32[]{:S(2)}) collective-permute-start(f32[3,2,20,512]{3,2,1,0:T(8,128)S(1)} %get-tuple-element.87), channel_id=1, source_target_pairs={{1,0},{2,1},{3,2},{5,4},{6,5},{7,6},{9,8},{10,9},{11,10},{13,12},{... | collective-permute-start | bytes 737288 | tf_op jit(solution)/shard_map/ppermute | solution.py:26
  19.5 1.6 %collective-permute-done.2 = f32[3,2,20,512]{3,2,1,0:T(8,128)S(1)} collective-permute-done((f32[3,2,20,512]{3,2,1,0:T(8,128)S(1)}, f32[3,2,20,512]{3,2,1,0:T(8,128)S(1)}, u32[]{:S(2)}, u32[]{:S(2)}) %collective-permute-start.2) | collective-permute-done | bytes 245792 | tf_op jit(solution)/shard_map/ppermute | solution.py:23
  21.1 4.4 %collective-permute-done.3 = f32[3,2,20,512]{3,2,1,0:T(8,128)S(1)} collective-permute-done((f32[3,2,20,512]{3,2,1,0:T(8,128)S(1)}, f32[3,2,20,512]{3,2,1,0:T(8,128)S(1)}, u32[]{:S(2)}, u32[]{:S(2)}) %collective-permute-start.3) | collective-permute-done | bytes 245792 | tf_op jit(solution)/shard_map/ppermute | solution.py:26
  25.8 0.7 fusion.100
  27.3 0.7 fusion.7
  27.9 0.6 multiply_dynamic-update-slice_fusion.17
  29.1 0.6 broadcast_multiply_fusion.2
  31.2 0.7 fusion.19
  32.1 1.3 collective-permute-start.4
  34.1 15.4 %collective-permute-done.4 = f32[3,8,16,512]{3,2,1,0:T(8,128)S(1)} collective-permute-done((f32[3,8,16,512]{3,2,1,0:T(8,128)S(1)}, f32[3,8,16,512]{3,2,1,0:T(8,128)S(1)}, u32[]{:S(2)}, u32[]{:S(2)}) %collective-permute-start.4) | collective-permute-done | bytes 786464 | tf_op jit(solution)/shard_map/ppermute | solution.py:34
  50.0 3.3 %collective-permute-start.6 = (f32[3,8,2,512]{3,2,1,0:T(2,128)S(1)}, f32[3,8,2,512]{3,2,1,0:T(2,128)S(1)}, u32[]{:S(2)}, u32[]{:S(2)}) collective-permute-start(f32[3,8,2,512]{3,2,1,0:T(2,128)S(1)} %get-tuple-element.100), channel_id=1, source_target_pairs={{4,0},{8,4},{12,8},{0,12},{5,1},{9,5},{13,9},{1,13},{6,2},{10,6},{... | collective-permute-start | bytes 294920 | tf_op jit(solution)/shard_map/ppermute | solution.py:26
  53.3 3.1 %gather_fusion.1 = f32[512]{0:T(512)S(1)} fusion(f32[65536]{0:T(1024)S(1)} %bitcast.172, s32[1024]{0:T(1024)S(1)} %pad_clamp_fusion), kind=kCustom, calls=%fused_computation.1 | custom fusion | bytes 6144 | tf_op jit(solution)/shard_map/gather | solution.py:73
  56.5 3.3 %scatter_custom_fusion.1 = f32[65536]{0:T(1024)S(1)} fusion(s32[512]{0:T(512)S(1)} %bitcast.178, f32[512]{0:T(512)S(1)} %multiply_select_fusion.3, f32[]{:T(128)} %constant.113.clone.1), kind=kCustom, calls=%fused_computation.245 | custom fusion | flops 512 | bytes 262148 | tf_op jit(solution)/shard_map/scatter-add | solution.py:76
  59.9 0.9 pad_maximum_fusion.24
  60.8 2.0 %collective-permute-start.7 = (f32[3,2,20,512]{3,2,1,0:T(8,128)}, f32[3,2,20,512]{3,2,1,0:T(8,128)S(1)}, u32[]{:S(2)}, u32[]{:S(2)}) collective-permute-start(f32[3,2,20,512]{3,2,1,0:T(8,128)} %get-tuple-element.86), channel_id=1, source_target_pairs={{0,1},{1,2},{2,3},{4,5},{5,6},{6,7},{8,9},{9,10},{10,11},{12,13},{... | collective-permute-start | bytes 737288 | tf_op jit(solution)/shard_map/ppermute | solution.py:23
  62.8 2.5 %collective-permute-start.8 = (f32[3,2,20,512]{3,2,1,0:T(8,128)}, f32[3,2,20,512]{3,2,1,0:T(8,128)S(1)}, u32[]{:S(2)}, u32[]{:S(2)}) collective-permute-start(f32[3,2,20,512]{3,2,1,0:T(8,128)} %get-tuple-element.85), channel_id=1, source_target_pairs={{1,0},{2,1},{3,2},{5,4},{6,5},{7,6},{9,8},{10,9},{11,10},{13,12},{... | collective-permute-start | bytes 737288 | tf_op jit(solution)/shard_map/ppermute | solution.py:26
  65.4 1.4 collective-permute-done.7
  66.8 4.3 %collective-permute-done.8 = f32[3,2,20,512]{3,2,1,0:T(8,128)S(1)} collective-permute-done((f32[3,2,20,512]{3,2,1,0:T(8,128)}, f32[3,2,20,512]{3,2,1,0:T(8,128)S(1)}, u32[]{:S(2)}, u32[]{:S(2)}) %collective-permute-start.8) | collective-permute-done | bytes 245792 | tf_op jit(solution)/shard_map/ppermute | solution.py:26
  71.1 1.2 pad_maximum_fusion.1
  72.3 0.7 fusion.98
  74.7 0.6 multiply_dynamic-update-slice_fusion.11
  75.9 0.6 broadcast_multiply_fusion.1
  78.0 0.7 fusion.16
  79.0 1.3 collective-permute-start.9
  80.3 16.2 %collective-permute-done.9 = f32[3,8,16,512]{3,2,1,0:T(8,128)S(1)} collective-permute-done((f32[3,8,16,512]{3,2,1,0:T(8,128)S(1)}, f32[3,8,16,512]{3,2,1,0:T(8,128)S(1)}, u32[]{:S(2)}, u32[]{:S(2)}) %collective-permute-start.9) | collective-permute-done | bytes 786464 | tf_op jit(solution)/shard_map/ppermute | solution.py:34
  96.9 3.3 %collective-permute-start.11 = (f32[3,8,2,512]{3,2,1,0:T(2,128)S(1)}, f32[3,8,2,512]{3,2,1,0:T(2,128)S(1)}, u32[]{:S(2)}, u32[]{:S(2)}) collective-permute-start(f32[3,8,2,512]{3,2,1,0:T(2,128)S(1)} %get-tuple-element.94), channel_id=1, source_target_pairs={{4,0},{8,4},{12,8},{0,12},{5,1},{9,5},{13,9},{1,13},{6,2},{10,6},{... | collective-permute-start | bytes 294920 | tf_op jit(solution)/shard_map/ppermute | solution.py:26
  100.2 3.1 %gather_fusion.2 = f32[512]{0:T(512)S(1)} fusion(f32[65536]{0:T(1024)S(1)} %bitcast.171, s32[1024]{0:T(1024)S(1)} %pad_clamp_fusion), kind=kCustom, calls=%fused_computation.2 | custom fusion | bytes 6144 | tf_op jit(solution)/shard_map/gather | solution.py:73
  103.4 3.3 %scatter_custom_fusion.2 = f32[65536]{0:T(1024)S(1)} fusion(s32[512]{0:T(512)S(1)} %bitcast.179, f32[512]{0:T(512)S(1)} %multiply_select_fusion.2, f32[]{:T(128)} %constant.113.clone.1), kind=kCustom, calls=%fused_computation.243 | custom fusion | flops 512 | bytes 262148 | tf_op jit(solution)/shard_map/scatter-add | solution.py:76
  106.8 0.9 pad_maximum_fusion.21
  107.7 1.9 %collective-permute-start.12 = (f32[3,2,20,512]{3,2,1,0:T(8,128)}, f32[3,2,20,512]{3,2,1,0:T(8,128)S(1)}, u32[]{:S(2)}, u32[]{:S(2)}) collective-permute-start(f32[3,2,20,512]{3,2,1,0:T(8,128)} %get-tuple-element.84), channel_id=1, source_target_pairs={{0,1},{1,2},{2,3},{4,5},{5,6},{6,7},{8,9},{9,10},{10,11},{12,13},{... | collective-permute-start | bytes 737288 | tf_op jit(solution)/shard_map/ppermute | solution.py:23
  109.7 2.6 %collective-permute-start.13 = (f32[3,2,20,512]{3,2,1,0:T(8,128)}, f32[3,2,20,512]{3,2,1,0:T(8,128)S(1)}, u32[]{:S(2)}, u32[]{:S(2)}) collective-permute-start(f32[3,2,20,512]{3,2,1,0:T(8,128)} %get-tuple-element.83), channel_id=1, source_target_pairs={{1,0},{2,1},{3,2},{5,4},{6,5},{7,6},{9,8},{10,9},{11,10},{13,12},{... | collective-permute-start | bytes 737288 | tf_op jit(solution)/shard_map/ppermute | solution.py:26
  112.4 1.2 collective-permute-done.12
  113.6 4.3 %collective-permute-done.13 = f32[3,2,20,512]{3,2,1,0:T(8,128)S(1)} collective-permute-done((f32[3,2,20,512]{3,2,1,0:T(8,128)}, f32[3,2,20,512]{3,2,1,0:T(8,128)S(1)}, u32[]{:S(2)}, u32[]{:S(2)}) %collective-permute-start.13) | collective-permute-done | bytes 245792 | tf_op jit(solution)/shard_map/ppermute | solution.py:26
  117.9 1.2 pad_maximum_fusion.2
  119.1 0.7 fusion.96
  121.5 0.6 multiply_dynamic-update-slice_fusion.5
  122.8 0.6 broadcast_multiply_fusion
  124.8 0.7 fusion.13
  125.9 1.3 collective-permute-start.14
  127.2 16.3 %collective-permute-done.14 = f32[3,8,16,512]{3,2,1,0:T(8,128)S(1)} collective-permute-done((f32[3,8,16,512]{3,2,1,0:T(8,128)S(1)}, f32[3,8,16,512]{3,2,1,0:T(8,128)S(1)}, u32[]{:S(2)}, u32[]{:S(2)}) %collective-permute-start.14) | collective-permute-done | bytes 786464 | tf_op jit(solution)/shard_map/ppermute | solution.py:34
  143.4 1.0 select_bitcast_fusion
  (113 shorter events, 12.9 us)
Async XLA Ops:
  0.0 5.9 %copy-start.9 = (s32[1,1,512]{2,1,0:T(1,128)S(1)}, s32[1,1,512]{2,1,0:T(1,128)}, u32[]{:S(2)}) copy-start(s32[1,1,512]{2,1,0:T(1,128)} %param.11) | copy-start | bytes 6148
  1.2 12.0 %collective-permute-start = (f32[3,8,2,512]{3,2,1,0:T(2,128)S(1)}, f32[3,8,2,512]{3,2,1,0:T(2,128)S(1)}, u32[]{:S(2)}, u32[]{:S(2)}) collective-permute-start(f32[3,8,2,512]{3,2,1,0:T(2,128)S(1)} %get-tuple-element.105), channel_id=1, source_target_pairs={{0,4},{4,8},{8,12},{12,0},{1,5},{5,9},{9,13},{13,1},{2,6},{6,10},{... | collective-permute-start | bytes 294920 | tf_op jit(solution)/shard_map/ppermute | solution.py:23
  2.6 10.7 %collective-permute-start.1 = (f32[3,8,2,512]{3,2,1,0:T(2,128)S(1)}, f32[3,8,2,512]{3,2,1,0:T(2,128)S(1)}, u32[]{:S(2)}, u32[]{:S(2)}) collective-permute-start(f32[3,8,2,512]{3,2,1,0:T(2,128)S(1)} %get-tuple-element.106), channel_id=1, source_target_pairs={{4,0},{8,4},{12,8},{0,12},{5,1},{9,5},{13,9},{1,13},{6,2},{10,6},{... | collective-permute-start | bytes 294920 | tf_op jit(solution)/shard_map/ppermute | solution.py:26
  5.9 7.3 %copy-start = (f32[1,3,8,16,512]{4,3,2,1,0:T(8,128)S(1)}, f32[1,3,8,16,512]{4,3,2,1,0:T(8,128)}, u32[]{:S(2)}) copy-start(f32[1,3,8,16,512]{4,3,2,1,0:T(8,128)} %param.10) | copy-start | bytes 2359300
  13.4 7.8 %collective-permute-start.2 = (f32[3,2,20,512]{3,2,1,0:T(8,128)S(1)}, f32[3,2,20,512]{3,2,1,0:T(8,128)S(1)}, u32[]{:S(2)}, u32[]{:S(2)}) collective-permute-start(f32[3,2,20,512]{3,2,1,0:T(8,128)S(1)} %get-tuple-element.88), channel_id=1, source_target_pairs={{0,1},{1,2},{2,3},{4,5},{5,6},{6,7},{8,9},{9,10},{10,11},{12,13},{... | collective-permute-start | bytes 737288 | tf_op jit(solution)/shard_map/ppermute | solution.py:23
  17.5 8.0 %collective-permute-start.3 = (f32[3,2,20,512]{3,2,1,0:T(8,128)S(1)}, f32[3,2,20,512]{3,2,1,0:T(8,128)S(1)}, u32[]{:S(2)}, u32[]{:S(2)}) collective-permute-start(f32[3,2,20,512]{3,2,1,0:T(8,128)S(1)} %get-tuple-element.87), channel_id=1, source_target_pairs={{1,0},{2,1},{3,2},{5,4},{6,5},{7,6},{9,8},{10,9},{11,10},{13,12},{... | collective-permute-start | bytes 737288 | tf_op jit(solution)/shard_map/ppermute | solution.py:26
  32.1 17.4 %collective-permute-start.4 = (f32[3,8,16,512]{3,2,1,0:T(8,128)S(1)}, f32[3,8,16,512]{3,2,1,0:T(8,128)S(1)}, u32[]{:S(2)}, u32[]{:S(2)}) collective-permute-start(f32[3,8,16,512]{3,2,1,0:T(8,128)S(1)} %multiply_add_fusion.2), channel_id=1, source_target_pairs={{0,16},{1,17},{2,18},{3,19},{4,20},{5,21},{6,22},{7,23},{8,24},{9,... | collective-permute-start | bytes 2359304 | tf_op jit(solution)/shard_map/ppermute | solution.py:34
  49.9 9.9 %collective-permute-start.5 = (f32[3,8,2,512]{3,2,1,0:T(2,128)S(1)}, f32[3,8,2,512]{3,2,1,0:T(2,128)S(1)}, u32[]{:S(2)}, u32[]{:S(2)}) collective-permute-start(f32[3,8,2,512]{3,2,1,0:T(2,128)S(1)} %get-tuple-element.99), channel_id=1, source_target_pairs={{0,4},{4,8},{8,12},{12,0},{1,5},{5,9},{9,13},{13,1},{2,6},{6,10},{... | collective-permute-start | bytes 294920 | tf_op jit(solution)/shard_map/ppermute | solution.py:23
  50.0 9.8 %collective-permute-start.6 = (f32[3,8,2,512]{3,2,1,0:T(2,128)S(1)}, f32[3,8,2,512]{3,2,1,0:T(2,128)S(1)}, u32[]{:S(2)}, u32[]{:S(2)}) collective-permute-start(f32[3,8,2,512]{3,2,1,0:T(2,128)S(1)} %get-tuple-element.100), channel_id=1, source_target_pairs={{4,0},{8,4},{12,8},{0,12},{5,1},{9,5},{13,9},{1,13},{6,2},{10,6},{... | collective-permute-start | bytes 294920 | tf_op jit(solution)/shard_map/ppermute | solution.py:26
  59.8 1.0 copy-start.5
  59.8 1.0 copy-start.7
  60.8 6.0 %collective-permute-start.7 = (f32[3,2,20,512]{3,2,1,0:T(8,128)}, f32[3,2,20,512]{3,2,1,0:T(8,128)S(1)}, u32[]{:S(2)}, u32[]{:S(2)}) collective-permute-start(f32[3,2,20,512]{3,2,1,0:T(8,128)} %get-tuple-element.86), channel_id=1, source_target_pairs={{0,1},{1,2},{2,3},{4,5},{5,6},{6,7},{8,9},{9,10},{10,11},{12,13},{... | collective-permute-start | bytes 737288 | tf_op jit(solution)/shard_map/ppermute | solution.py:23
  62.8 8.3 %collective-permute-start.8 = (f32[3,2,20,512]{3,2,1,0:T(8,128)}, f32[3,2,20,512]{3,2,1,0:T(8,128)S(1)}, u32[]{:S(2)}, u32[]{:S(2)}) collective-permute-start(f32[3,2,20,512]{3,2,1,0:T(8,128)} %get-tuple-element.85), channel_id=1, source_target_pairs={{1,0},{2,1},{3,2},{5,4},{6,5},{7,6},{9,8},{10,9},{11,10},{13,12},{... | collective-permute-start | bytes 737288 | tf_op jit(solution)/shard_map/ppermute | solution.py:26
  73.4 0.9 copy-start.6
  73.4 0.9 copy-start.8
  79.0 17.5 %collective-permute-start.9 = (f32[3,8,16,512]{3,2,1,0:T(8,128)S(1)}, f32[3,8,16,512]{3,2,1,0:T(8,128)S(1)}, u32[]{:S(2)}, u32[]{:S(2)}) collective-permute-start(f32[3,8,16,512]{3,2,1,0:T(8,128)S(1)} %multiply_add_fusion.1), channel_id=1, source_target_pairs={{0,16},{1,17},{2,18},{3,19},{4,20},{5,21},{6,22},{7,23},{8,24},{9,... | collective-permute-start | bytes 2359304 | tf_op jit(solution)/shard_map/ppermute | solution.py:34
  96.9 9.9 %collective-permute-start.10 = (f32[3,8,2,512]{3,2,1,0:T(2,128)S(1)}, f32[3,8,2,512]{3,2,1,0:T(2,128)S(1)}, u32[]{:S(2)}, u32[]{:S(2)}) collective-permute-start(f32[3,8,2,512]{3,2,1,0:T(2,128)S(1)} %get-tuple-element.93), channel_id=1, source_target_pairs={{0,4},{4,8},{8,12},{12,0},{1,5},{5,9},{9,13},{13,1},{2,6},{6,10},{... | collective-permute-start | bytes 294920 | tf_op jit(solution)/shard_map/ppermute | solution.py:23
  96.9 9.8 %collective-permute-start.11 = (f32[3,8,2,512]{3,2,1,0:T(2,128)S(1)}, f32[3,8,2,512]{3,2,1,0:T(2,128)S(1)}, u32[]{:S(2)}, u32[]{:S(2)}) collective-permute-start(f32[3,8,2,512]{3,2,1,0:T(2,128)S(1)} %get-tuple-element.94), channel_id=1, source_target_pairs={{4,0},{8,4},{12,8},{0,12},{5,1},{9,5},{13,9},{1,13},{6,2},{10,6},{... | collective-permute-start | bytes 294920 | tf_op jit(solution)/shard_map/ppermute | solution.py:26
  106.8 1.0 copy-start.1
  106.8 1.0 copy-start.3
  107.7 5.9 %collective-permute-start.12 = (f32[3,2,20,512]{3,2,1,0:T(8,128)}, f32[3,2,20,512]{3,2,1,0:T(8,128)S(1)}, u32[]{:S(2)}, u32[]{:S(2)}) collective-permute-start(f32[3,2,20,512]{3,2,1,0:T(8,128)} %get-tuple-element.84), channel_id=1, source_target_pairs={{0,1},{1,2},{2,3},{4,5},{5,6},{6,7},{8,9},{9,10},{10,11},{12,13},{... | collective-permute-start | bytes 737288 | tf_op jit(solution)/shard_map/ppermute | solution.py:23
  109.7 8.3 %collective-permute-start.13 = (f32[3,2,20,512]{3,2,1,0:T(8,128)}, f32[3,2,20,512]{3,2,1,0:T(8,128)S(1)}, u32[]{:S(2)}, u32[]{:S(2)}) collective-permute-start(f32[3,2,20,512]{3,2,1,0:T(8,128)} %get-tuple-element.83), channel_id=1, source_target_pairs={{1,0},{2,1},{3,2},{5,4},{6,5},{7,6},{9,8},{10,9},{11,10},{13,12},{... | collective-permute-start | bytes 737288 | tf_op jit(solution)/shard_map/ppermute | solution.py:26
  120.3 0.9 copy-start.2
  120.3 0.9 copy-start.4
  125.9 17.6 %collective-permute-start.14 = (f32[3,8,16,512]{3,2,1,0:T(8,128)S(1)}, f32[3,8,16,512]{3,2,1,0:T(8,128)S(1)}, u32[]{:S(2)}, u32[]{:S(2)}) collective-permute-start(f32[3,8,16,512]{3,2,1,0:T(8,128)S(1)} %multiply_add_fusion), channel_id=1, source_target_pairs={{0,16},{1,17},{2,18},{3,19},{4,20},{5,21},{6,22},{7,23},{8,24},{9,... | collective-permute-start | bytes 2359304 | tf_op jit(solution)/shard_map/ppermute | solution.py:34
where the time goes:
time: 145 us; the launch traced here: 144 us
  waiting for transfers between devices  65.1 us (45%)
  other arithmetic  29.5 us (20%)
  starting transfers between devices  29 us (20%)
  local copies, waits for them, and re-layouts  18.6 us (13%)
  between operations  2.28 us (2%)
    ppermute x3, waiting for transfers between devices, shifted(): return lax.ppermute(value, axis, pairs)  47.8 us
    ppermute x6, starting transfers between devices, extended(): lax.ppermute(lax.slice_in_dim(block, 0, width, axis=dim), axis, backward)  15.6 us
    ppermute x6, waiting for transfers between devices, extended(): lax.ppermute(lax.slice_in_dim(block, 0, width, axis=dim), axis, backward)  13 us
    scatter-add x3, other arithmetic, drag_force(): spread = jnp.zeros_like(flat).at[cells].add(force).reshape(ux.shape)  9.99 us
    ppermute x6, starting transfers between devices, extended(): lax.ppermute(lax.slice_in_dim(block, block.shape[dim] - width, None, axis...  9.52 us
    gather x3, local copies, waits for them, and re-layouts, drag_force(): vals = flat[cells]  9.43 us
    slice x24, local copies, waits for them, and re-layouts, xdiff(): return (jnp.roll(field, -1, -1) - jnp.roll(field, 1, -1)) * 0.5  4.65 us
    concatenate x6, other arithmetic, extended(): block = jnp.concatenate([low, block, high], axis=dim)  4.59 us
  transfers between devices with their start and end apart: 15, of which 9 were waited for; matrix products, arithmetic and copies ran while one was open for 15% of the time, Pallas kernels for 0%

commit v1 on v0

v1 whole, which is shorter than its diff:
```python
import functools

import jax
import jax.numpy as jnp
from jax import lax
from jax.experimental import pallas as pl
from jax.experimental.pallas import tpu as pltpu
from jax.sharding import PartitionSpec as P

FW = 128
LANES = 128
HALO = 6
YOFF = 8
MARGIN = 64

smag_coef = 0.1024
drag_coef = 0.665
time_step = 0.2
VMEM_LIMIT = 60 * 1024 * 1024


def corner_rows():
    offset, table = 0, []
    for distance in range(1, HALO):
        table.append((distance, HALO - distance, offset))
        offset += HALO - distance
    return table, offset


def whole_vmem(count):
    return [pl.BlockSpec(memory_space=pltpu.VMEM)] * count


def call(kernel, outs, ins, smem, scratch=()):
    specs = [
        pl.BlockSpec(memory_space=pltpu.SMEM if i < smem else pltpu.VMEM) for i in range(len(ins))
    ]
    return pl.pallas_call(
        kernel,
        out_shape=[jax.ShapeDtypeStruct(shape, jnp.float32) for shape in outs],
        in_specs=specs,
        out_specs=whole_vmem(len(outs)),
        scratch_shapes=list(scratch),
        compiler_params=pltpu.CompilerParams(vmem_limit_bytes=VMEM_LIMIT),
    )(*ins)


def pack_own(dims, scal, u, fringe, up, down):
    tiles, depth, width = dims
    first = scal[0]
    lane0 = scal[1]
    lane = lax.broadcasted_iota(jnp.int32, (width, LANES), 1)
    picked = [lax.rem(first + k, tiles) for k in range(3)]
    for c in range(3):
        for z in range(depth):
            rows = [u[c, z, :, pl.ds(pl.multiple_of(p * LANES, LANES), LANES)] for p in picked]
            for k in range(2):
                at = ((c * 2 + k) * depth + z) * width
                fringe[pl.ds(at, width), :] = jnp.where(lane >= lane0, rows[k], rows[k + 1])
    for c in range(3):
        for t in range(tiles):
            for z in range(depth):
                at = ((c * tiles + t) * depth + z) * HALO
                cols = pl.ds(t * LANES, LANES)
                up[pl.ds(at, HALO), :] = u[c, z, width - HALO :, cols]
                down[pl.ds(at, HALO), :] = u[c, z, :HALO, cols]


def pack_second(dims, u, fringe, fup, fdown, above, below):
    tiles, depth, width = dims
    for c in range(3):
        for k in range(2):
            for z in range(depth):
                at = ((c * 2 + k) * depth + z) * HALO
                src = ((c * 2 + k) * depth + z) * width
                fup[pl.ds(at, HALO), :] = fringe[pl.ds(src + width - HALO, HALO), :]
                fdown[pl.ds(at, HALO), :] = fringe[pl.ds(src, HALO), :]
        for t in range(tiles + 2):
            for h in range(HALO):
                at = ((c * (tiles + 2) + t) * HALO + h) * width
                for out, z in ((above, depth - HALO + h), (below, h)):
                    if t < tiles:
                        value = u[c, z, :, pl.ds(t * LANES, LANES)]
                    else:
                        value = fringe[pl.ds(((c * 2 + t - tiles) * depth + z) * width, width), :]
                    out[pl.ds(at, width), :] = value


def pack_corners(dims, left, right, fleft, fright, above, below):
    tiles, depth, _ = dims
    table, total = corner_rows()
    for c in range(3):
        for t in range(tiles + 2):
            for side in range(2):
                for distance, rows, offset in table:
                    at = ((c * (tiles + 2) + t) * 2 + side) * total + offset
                    for out, z in ((above, depth - distance), (below, distance - 1)):
                        if t < tiles:
                            src, row = (left, right)[side], ((c * tiles + t) * depth + z) * HALO
                        else:
                            src, row = (fleft, fright)[side], ((c * 2 + t - tiles) * depth + z) * HALO
                        row = row + (HALO - rows if side == 0 else 0)
                        out[pl.ds(at, rows), :] = src[pl.ds(row, rows), :]


def multiplicity(dims, lists, out):
    tiles, depth, width = dims
    slots = lists.shape[1]
    reach = HALO - 2
    rows = width + 2 * reach
    levels = depth + 2 * reach
    columns = tiles * LANES
    row_iota = lax.broadcasted_iota(jnp.int32, (levels * rows, slots), 0)
    col_iota = lax.broadcasted_iota(jnp.int32, (columns, slots), 0)
    total = jnp.zeros((levels * rows, columns), jnp.float32)
    for index in range(9):
        oz, oy = index // 3 - 1, index % 3 - 1
        cell = lists[index : index + 1, :]
        x = cell % columns
        y = cell // columns % width + oy * width + reach
        z = cell // (columns * width) + oz * depth + reach
        fits = (cell >= 0) & (y >= 0) & (y < rows) & (z >= 0) & (z < levels)
        row = jnp.where(fits, z * rows + y, -1)
        one = (row_iota == row).astype(jnp.float32).astype(jnp.bfloat16)
        two = (col_iota == x).astype(jnp.float32).astype(jnp.bfloat16)
        total = total + lax.dot_general(
            one, two, (((1,), (1,)), ((), ())), preferred_element_type=jnp.float32
        )
    for t in range(tiles):
        out[t] = total[:, t * LANES : (t + 1) * LANES].reshape(levels, rows, LANES)


def xdiff(value, first, last, nleft, nright):
    ahead = pltpu.roll(value, LANES - 1, 2)
    behind = pltpu.roll(value, 1, 2)
    parts = []
    for i in range(value.shape[0]):
        right = jnp.where(last, ahead[nright[i]], ahead[i])
        left = jnp.where(first, behind[nleft[i]], behind[i])
        parts.append(right - left)
    return jnp.stack(parts)


def tau_tile(src, tau, part, z, y0, span, seam, inside, keep_part):
    first, last, nleft, nright = seam
    here = pl.ds(y0, 8)
    u = [src[c, span, z, here, :] for c in range(3)]
    gx = [xdiff(v, first, last, nleft, nright) for v in u]
    gy = [
        src[c, span, z, pl.ds(y0 + 1, 8), :] - src[c, span, z, pl.ds(y0 - 1, 8), :]
        for c in range(3)
    ]
    gz = [src[c, span, z + 1, here, :] - src[c, span, z - 1, here, :] for c in range(3)]
    xy = gx[1] + gy[0]
    xz = gx[2] + gz[0]
    yz = gy[2] + gz[1]
    diag = gx[0] * gx[0] + gy[1] * gy[1] + gz[2] * gz[2]
    off = xy * xy + xz * xz + yz * yz
    visc = jnp.sqrt(0.5 * diag + 0.25 * off) * inside
    half = visc * 0.5
    for k, value in enumerate(
        (visc * gx[0], visc * gy[1], visc * gz[2], half * xy, half * xz, half * yz)
    ):
        tau[k, span, z, here, :] = value
    if keep_part:
        scaled = [v * (-0.5 * time_step) for v in u]
        for c in range(3):
            part[c, span, z, here, :] = u[c] + (
                scaled[0] * gx[c] + scaled[1] * gy[c] + scaled[2] * gz[c]
            )


TAU = ((0, 3, 4), (3, 1, 5), (4, 5, 2))


def out_tile(src, base, tau, part, z, y0, span, seam, weights):
    first, last, nleft, nright = seam
    here = pl.ds(y0, 8)
    keep, take = weights
    results = []
    for c in range(3):
        div = xdiff(tau[TAU[c][0], span, z, here, :], first, last, nleft, nright)
        div = div + (
            tau[TAU[c][1], span, z, pl.ds(y0 + 1, 8), :]
            - tau[TAU[c][1], span, z, pl.ds(y0 - 1, 8), :]
        )
        div = div + (tau[TAU[c][2], span, z + 1, here, :] - tau[TAU[c][2], span, z - 1, here, :])
        value = part[c, span, z, here, :] * take + div * (take * time_step * 0.5 * smag_coef)
        if keep:
            value = value + keep * base[c, span, z, here, :]
        results.append(value)
    return results


def step_kernel(
    dims, scal, u, left, right, fringe, fleft, fright, under, over, cunder, cover, count, out,
    u0, u1, u2, tau, part,
):
    tiles, depth, width = dims
    start, lane0, main, bottom, top = (scal[i] for i in (2, 1, 3, 4, 5))
    table, total = corner_rows()
    all_tiles = tiles + 2
    for c in range(3):
        for t in range(tiles):
            cols = pl.ds(t * LANES, LANES)
            for z in range(depth):
                at = ((c * tiles + t) * depth + z) * HALO
                u0[c, t, z + HALO, pl.ds(YOFF, width), :] = u[c, z, :, cols]
                u0[c, t, z + HALO, pl.ds(YOFF - HALO, HALO), :] = left[pl.ds(at, HALO), :]
                u0[c, t, z + HALO, pl.ds(YOFF + width, HALO), :] = right[pl.ds(at, HALO), :]
        for k in range(2):
            for z in range(depth):
                at = (c * 2 + k) * depth + z
                rows = pl.ds(at * HALO, HALO)
                u0[c, tiles + k, z + HALO, pl.ds(YOFF, width), :] = fringe[pl.ds(at * width, width), :]
                u0[c, tiles + k, z + HALO, pl.ds(YOFF - HALO, HALO), :] = fleft[rows, :]
                u0[c, tiles + k, z + HALO, pl.ds(YOFF + width, HALO), :] = fright[rows, :]
        for t in range(all_tiles):
            for h in range(HALO):
                rows = pl.ds(((c * all_tiles + t) * HALO + h) * width, width)
                u0[c, t, h, pl.ds(YOFF, width), :] = under[rows, :]
                u0[c, t, HALO + depth + h, pl.ds(YOFF, width), :] = over[rows, :]
            for side in range(2):
                for distance, rows, offset in table:
                    at = ((c * all_tiles + t) * 2 + side) * total + offset
                    y = YOFF - rows if side == 0 else YOFF + width
                    u0[c, t, HALO - distance, pl.ds(y, rows), :] = cunder[pl.ds(at, rows), :]
                    u0[c, t, HALO + depth + distance - 1, pl.ds(y, rows), :] = cover[pl.ds(at, rows), :]

    def clear(z):
        for c in range(3):
            u0[c, :, z] = jnp.zeros(u0.shape[1:2] + u0.shape[3:], jnp.float32)

    @pl.when(bottom == 1)
    def _():
        lax.fori_loop(0, HALO, lambda i, _: clear(i), None)

    @pl.when(top == 1)
    def _():
        lax.fori_loop(0, HALO, lambda i, _: clear(HALO + depth + i), None)

    lane = lax.broadcasted_iota(jnp.int32, (8, LANES), 1)
    order = list(range(tiles))
    main_seam = (lane == 0, lane == LANES - 1, order[-1:] + order[:-1], order[1:] + order[:1])
    window_seam = (lane == lane0, lane == lax.rem(lane0 + LANES - 1, LANES), [1, 0], [1, 0])
    main_span, window_span = slice(0, tiles), slice(tiles, tiles + 2)

    def inside_of(z):
        below = (z < HALO) & (bottom == 1)
        above = (z >= HALO + depth) & (top == 1)
        return jnp.where(below | above, 0.0, 1.0)

    def loop(low, high, body):
        def step(z, _):
            body(z)

        lax.fori_loop(low, high, step, None)

    def tau_stage(src, margin, span, seam):
        rows = list(range(YOFF - margin, YOFF + width + margin - 8, 8)) + [YOFF + width + margin - 8]
        fewer = list(range(YOFF - margin + 1, YOFF + width + margin - 9, 8)) + [YOFF + width + margin - 9]

        def body(starts, z):
            for y0 in starts:
                tau_tile(src, tau, part, z, y0, span, seam, inside_of(z), True)

        loop(HALO, HALO + depth, functools.partial(body, rows))
        loop(HALO - margin, HALO, functools.partial(body, fewer))
        loop(HALO + depth, HALO + depth + margin, functools.partial(body, fewer))

    def out_stage(src, dst, margin, weights, span, seam, blended):
        rows = list(range(YOFF - margin, YOFF + width + margin - 8, 8)) + [YOFF + width + margin - 8]
        reach = HALO - 2

        def body(z):
            inside = inside_of(z)
            for y0 in rows:
                here = pl.ds(y0, 8)
                values = out_tile(src, u0, tau, part, z, y0, span, seam, weights)
                if blended:
                    ux = src[0, span, z, here, :]
                    times = count[:, z - HALO + reach, pl.ds(y0 - YOFF + reach, 8), :]
                    factor = jnp.where(main == 1, -drag_coef * time_step * weights[1], 0.0)
                    values[0] = values[0] + (times * factor) * (ux * jnp.abs(ux))
                for c in range(3):
                    value = values[c]
                    if blended:
                        near = dst[c, tiles, z, here, :]
                        far = dst[c, tiles + 1, z, here, :]
                        parts = []
                        for t in range(tiles):
                            col = lane + t * LANES
                            mask = (col >= start) & (col < start + FW) & (main == 1)
                            other = jnp.where(col < start + MARGIN, near, far)
                            parts.append(jnp.where(mask, 0.5 * (value[t] + other), value[t]))
                        value = jnp.stack(parts)
                    dst[c, span, z, here, :] = value * inside

        loop(HALO - margin, HALO + depth + margin, body)

    stages = (
        (u0, u1, HALO - 1, (0.0, 1.0)),
        (u1, u2, HALO - 3, (0.75, 0.25)),
        (u2, u1, HALO - 5, (1.0 / 3.0, 2.0 / 3.0)),
    )
    for src, dst, margin, weights in stages:

        @pl.when(main == 1)
        def _():
            tau_stage(src, margin, window_span, window_seam)
            out_stage(src, dst, margin - 1, weights, window_span, window_seam, False)

        tau_stage(src, margin, main_span, main_seam)
        out_stage(src, dst, margin - 1, weights, main_span, main_seam, True)
    for c in range(3):
        for t in range(tiles):
            for z in range(depth):
                out[c, z, :, pl.ds(t * LANES, LANES)] = u1[c, t, z + HALO, pl.ds(YOFF, width), :]


def around(axis, by):
    count = lax.axis_size(axis)
    return [(i, (i + by) % count) for i in range(count)]


def per_device(velocity, turbine_cells, turbine_count, fringe_start):
    u = velocity[0]
    _, depth, width, columns = u.shape
    tiles = columns // LANES
    dims = (tiles, depth, width)
    start = fringe_start[0]
    origin = (start + columns - MARGIN) % columns
    gz, gy = lax.axis_index("gz"), lax.axis_index("gy")
    nz, ny = lax.axis_size("gz"), lax.axis_size("gy")
    scal = jnp.stack(
        [
            origin // LANES,
            origin % LANES,
            start,
            (lax.axis_index("box") == 1).astype(jnp.int32),
            (gz == 0).astype(jnp.int32),
            (gz == nz - 1).astype(jnp.int32),
        ]
    ).astype(jnp.int32)

    slots = turbine_cells.shape[-1]
    cells = turbine_cells.reshape(slots)
    cells = jnp.where(jnp.arange(slots) < turbine_count.reshape(()), cells, -1)
    every = lax.all_gather(cells, ("gy", "gz"))
    lists = []
    for oz in (-1, 0, 1):
        for oy in (-1, 0, 1):
            z = gz + oz
            row = lax.dynamic_index_in_dim(
                every, (gy + oy) % ny * nz + jnp.clip(z, 0, nz - 1), keepdims=False
            )
            lists.append(jnp.where((z >= 0) & (z < nz), row, -1))
    lists = jnp.stack(lists)

    halo_rows = 3 * tiles * depth * HALO
    window_rows = 3 * 2 * depth * HALO
    level_rows = 3 * (tiles + 2) * HALO * width
    corner = 3 * (tiles + 2) * 2 * corner_rows()[1]
    corner = (corner + 7) // 8 * 8

    fringe, up, down = call(
        functools.partial(pack_own, dims),
        [(3 * 2 * depth * width, LANES), (halo_rows, LANES), (halo_rows, LANES)],
        (scal, u),
        1,
    )
    fringe = lax.ppermute(fringe, "box", [(0, 1), (1, 0)])
    left = lax.ppermute(up, "gy", around("gy", 1))
    right = lax.ppermute(down, "gy", around("gy", -1))
    fup, fdown, above, below = call(
        functools.partial(pack_second, dims),
        [(window_rows, LANES), (window_rows, LANES), (level_rows, LANES), (level_rows, LANES)],
        (u, fringe),
        0,
    )
    fleft = lax.ppermute(fup, "gy", around("gy", 1))
    fright = lax.ppermute(fdown, "gy", around("gy", -1))
    under = lax.ppermute(above, "gz", around("gz", 1))
    over = lax.ppermute(below, "gz", around("gz", -1))
    cabove, cbelow = call(
        functools.partial(pack_corners, dims),
        [(corner, LANES), (corner, LANES)],
        (left, right, fleft, fright),
        0,
    )
    cunder = lax.ppermute(cabove, "gz", around("gz", 1))
    cover = lax.ppermute(cbelow, "gz", around("gz", -1))

    reach = HALO - 2
    (count,) = call(
        functools.partial(multiplicity, dims),
        [(tiles, depth + 2 * reach, width + 2 * reach, LANES)],
        (lists,),
        0,
    )
    ext = (tiles + 2, depth + 2 * HALO, width + 2 * YOFF, LANES)
    (out,) = call(
        functools.partial(step_kernel, dims),
        [u.shape],
        (scal, u, left, right, fringe, fleft, fright, under, over, cunder, cover, count),
        1,
        [pltpu.VMEM((n,) + ext, jnp.float32) for n in (3, 3, 3, 6, 3)],
    )
    return out[None]


def solution(mesh):
    placed = (P("box", None, "gz", "gy", None), P("gz", "gy", None), P("gz", "gy"), P())
    return jax.shard_map(
        per_device,
        mesh=mesh,
        in_specs=placed,
        out_specs=P("box", None, "gz", "gy", None),
        check_vma=False,
    )
```

time: 145 us -> 106 us (0.73)
  Pallas kernels: 0 us -> 38.9 us
  waiting for transfers between devices: 65.1 us -> 26.7 us
  other arithmetic: 29.5 us -> 0.03 us
  blocking collectives: 0 us -> 23.3 us
  starting transfers between devices: 29 us -> 10.2 us
  local copies, waits for them, and re-layouts: 18.6 us -> 5.3 us
    pallas_call x0 -> x5, Pallas kernels: none -> 38.9 us  [call(): pl.pallas_call(kernel, out_shape=[jax.ShapeDtypeStruct(shape, jnp.float32...]
    ppermute x15 -> x9, waiting for transfers between devices: 65.1 us -> 26.7 us  [the longest x1 10.2 us: per_device(): fringe = lax.ppermute(fringe, 'box', [(0, 1), (1, 0)])]
    all_gather x0 -> x1, blocking collectives: none -> 23.3 us  [per_device(): every = lax.all_gather(cells, ('gy', 'gz'))]
    ppermute x15 -> x9, starting transfers between devices: 29 us -> 10.2 us  [the longest x1 2.64 us: per_device(): under = lax.ppermute(above, 'gz', around('gz', 1))]
    scatter-add x6 -> x0, other arithmetic: 10.2 us -> none  [the longest x3 9.99 us: drag_force(): spread = jnp.zeros_like(flat).at[cells].add(force).reshape(ux.shape)]
    gather x3 -> x0, local copies, waits for them, and re-layouts: 9.43 us -> none  [drag_force(): vals = flat[cells]]
    slice x30 -> x0, local copies, waits for them, and re-layouts: 7.47 us -> none  [the longest x24 4.65 us: xdiff(): return (jnp.roll(field, -1, -1) - jnp.roll(field, 1, -1)) * 0.5]
    mul x14 -> x0, other arithmetic: 5.28 us -> none  [the longest x5 1.82 us: sdiff(): (lax.slice_in_dim(field, 2, count, axis=axis) - lax.slice_in_dim(field, 0...]
  transfers between devices with their start and end apart: 15 -> 9, of which waited for: 9 -> 5; matrix products, arithmetic and copies ran while one was open for 15% -> 1% of each run, Pallas kernels for 0% -> 5%
where the time goes in v1:
time: 106 us
  Pallas kernels  38.9 us (37%)
  waiting for transfers between devices  26.7 us (25%)
  blocking collectives  23.3 us (22%)
  starting transfers between devices  10.2 us (10%)
  local copies, waits for them, and re-layouts  5.3 us (5%)
  between operations  1.46 us (1%)
    pallas_call x5, Pallas kernels, call(): pl.pallas_call(kernel, out_shape=[jax.ShapeDtypeStruct(shape, jnp.float32...  38.9 us
    all_gather x1, blocking collectives, per_device(): every = lax.all_gather(cells, ('gy', 'gz'))  23.3 us
    ppermute x1, waiting for transfers between devices, per_device(): fringe = lax.ppermute(fringe, 'box', [(0, 1), (1, 0)])  10.2 us
    ppermute x1, waiting for transfers between devices, per_device(): left = lax.ppermute(up, 'gy', around('gy', 1))  6.48 us
    ppermute x1, waiting for transfers between devices, per_device(): right = lax.ppermute(down, 'gy', around('gy', -1))  3.81 us
    ppermute x1, waiting for transfers between devices, per_device(): fleft = lax.ppermute(fup, 'gy', around('gy', 1))  3.46 us
    unnamed x24, local copies, waits for them, and re-layouts  3.45 us
    ppermute x1, waiting for transfers between devices, per_device(): fright = lax.ppermute(fdown, 'gy', around('gy', -1))  2.79 us
  transfers between devices with their start and end apart: 9, of which 5 were waited for; matrix products, arithmetic and copies ran while one was open for 1% of the time, Pallas kernels for 5%

profile of v1, /device:TPU:5, one launch (start us, length us, event | category | flops | bytes accessed | tf_op | source)
XLA Modules:
  0.0 106.0 jit_solution(2837219148003435382)
XLA Ops:
  0.7 0.6 stack.47.scal
  1.3 2.2 %shard_map.46 = (f32[768,128]{1,0:T(8,128)}, f32[576,128]{1,0:T(8,128)}, f32[576,128]{1,0:T(8,128)}) custom-call(s32[6]{0:T(128)} %stack.47.scal, f32[3,8,16,512]{3,2,1,0:T(8,128)} %bitcast.32), custom_call_target="tpu_custom_call" | custom-call | tf_op jit(solution)/shard_map/pallas_call | solution.py:38
  3.5 0.0 copy-start.11
  3.5 0.0 copy-start.10
  3.5 0.0 collective-permute-start.2
  3.5 10.2 %collective-permute-done.2.fringe = f32[768,128]{1,0:T(8,128)S(1)} collective-permute-done((f32[768,128]{1,0:T(8,128)}, f32[768,128]{1,0:T(8,128)S(1)}, u32[]{:S(2)}, u32[]{:S(2)}) %collective-permute-start.2) | collective-permute-done | bytes 393248 | tf_op jit(solution)/shard_map/ppermute | solution.py:372
  13.7 0.0 copy-start
  13.7 0.8 copy-done
  14.5 2.6 %shard_map.47 = (f32[288,128]{1,0:T(8,128)}, f32[288,128]{1,0:T(8,128)}, f32[1728,128]{1,0:T(8,128)}, f32[1728,128]{1,0:T(8,128)}) custom-call(f32[3,8,16,512]{3,2,1,0:T(8,128)} %bitcast.33, f32[768,128]{1,0:T(8,128)} %copy-done), custom_call_target="tpu_custom_call" | custom-call | tf_op jit(solution)/shard_map/pallas_call | solution.py:38
  17.1 2.6 %collective-permute-start.5 = (f32[1728,128]{1,0:T(8,128)}, f32[1728,128]{1,0:T(8,128)S(1)}, u32[]{:S(2)}, u32[]{:S(2)}) collective-permute-start(f32[1728,128]{1,0:T(8,128)} %get-tuple-element.19), channel_id=1, source_target_pairs={{0,1},{1,2},{2,3},{3,0},{4,5},{5,6},{6,7},{7,4},{8,9},{9,10},{10,1... | collective-permute-start | bytes 2654216 | tf_op jit(solution)/shard_map/ppermute | solution.py:383
  19.8 0.0 collective-permute-start.6
  19.8 0.0 copy-done.11
  19.8 1.3 %collective-permute-start = (f32[576,128]{1,0:T(8,128)S(1)}, f32[576,128]{1,0:T(8,128)S(1)}, u32[]{:S(2)}, u32[]{:S(2)}) collective-permute-start(f32[576,128]{1,0:T(8,128)S(1)} %copy-done.11), channel_id=1, source_target_pairs={{0,4},{4,8},{8,12},{12,0},{1,5},{5,9},{9,13},{13,1},{2,6},{6,10},{... | collective-permute-start | bytes 884744 | tf_op jit(solution)/shard_map/ppermute | solution.py:373
  21.1 0.0 copy-done.10
  21.1 2.1 %collective-permute-start.1 = (f32[576,128]{1,0:T(8,128)S(1)}, f32[576,128]{1,0:T(8,128)S(1)}, u32[]{:S(2)}, u32[]{:S(2)}) collective-permute-start(f32[576,128]{1,0:T(8,128)S(1)} %copy-done.10), channel_id=1, source_target_pairs={{0,12},{4,0},{8,4},{12,8},{1,13},{5,1},{9,5},{13,9},{2,14},{6,2},{... | collective-permute-start | bytes 884744 | tf_op jit(solution)/shard_map/ppermute | solution.py:374
  23.2 0.0 collective-permute-start.3
  23.2 6.5 %collective-permute-done.left = f32[576,128]{1,0:T(8,128)S(1)} collective-permute-done((f32[576,128]{1,0:T(8,128)S(1)}, f32[576,128]{1,0:T(8,128)S(1)}, u32[]{:S(2)}, u32[]{:S(2)}) %collective-permute-start) | collective-permute-done | bytes 294944 | tf_op jit(solution)/shard_map/ppermute | solution.py:373
  29.7 0.0 copy-start.1
  29.7 1.6 %collective-permute-start.4 = (f32[288,128]{1,0:T(8,128)}, f32[288,128]{1,0:T(8,128)S(1)}, u32[]{:S(2)}, u32[]{:S(2)}) collective-permute-start(f32[288,128]{1,0:T(8,128)} %get-tuple-element.18), channel_id=1, source_target_pairs={{0,12},{4,0},{8,4},{12,8},{1,13},{5,1},{9,5},{13,9},{2,14},{6,2},{... | collective-permute-start | bytes 442376 | tf_op jit(solution)/shard_map/ppermute | solution.py:382
  31.9 3.8 %collective-permute-done.1.right = f32[576,128]{1,0:T(8,128)S(1)} collective-permute-done((f32[576,128]{1,0:T(8,128)S(1)}, f32[576,128]{1,0:T(8,128)S(1)}, u32[]{:S(2)}, u32[]{:S(2)}) %collective-permute-start.1) | collective-permute-done | bytes 294944 | tf_op jit(solution)/shard_map/ppermute | solution.py:374
  35.7 0.0 copy-start.2
  35.7 3.5 %collective-permute-done.3.fleft = f32[288,128]{1,0:T(8,128)S(1)} collective-permute-done((f32[288,128]{1,0:T(8,128)}, f32[288,128]{1,0:T(8,128)S(1)}, u32[]{:S(2)}, u32[]{:S(2)}) %collective-permute-start.3) | collective-permute-done | bytes 147488 | tf_op jit(solution)/shard_map/ppermute | solution.py:381
  39.2 0.0 copy-start.5
  39.2 2.8 %collective-permute-done.4.fright = f32[288,128]{1,0:T(8,128)S(1)} collective-permute-done((f32[288,128]{1,0:T(8,128)}, f32[288,128]{1,0:T(8,128)S(1)}, u32[]{:S(2)}, u32[]{:S(2)}) %collective-permute-start.4) | collective-permute-done | bytes 147488 | tf_op jit(solution)/shard_map/ppermute | solution.py:382
  42.0 0.0 copy-done.1
  42.0 0.0 copy-done.2
  42.0 0.0 copy-done.5
  42.0 0.0 copy-start.6
  42.0 0.7 copy-done.6
  42.7 2.1 %shard_map.48 = (f32[544,128]{1,0:T(8,128)}, f32[544,128]{1,0:T(8,128)}) custom-call(f32[576,128]{1,0:T(8,128)} %copy-done.1, f32[576,128]{1,0:T(8,128)} %copy-done.2, f32[288,128]{1,0:T(8,128)} %copy-done.5, f32[288,128]{1,0:T(8,128)} %copy-done.6), custom_call_target="tpu_custom_call" | custom-call | tf_op jit(solution)/shard_map/pallas_call | solution.py:38
  44.7 0.0 copy-start.9
  44.7 2.6 %collective-permute-start.7 = (f32[544,128]{1,0:T(8,128)}, f32[544,128]{1,0:T(8,128)S(1)}, u32[]{:S(2)}, u32[]{:S(2)}) collective-permute-start(f32[544,128]{1,0:T(8,128)} %get-tuple-element.21), channel_id=1, source_target_pairs={{0,1},{1,2},{2,3},{3,0},{4,5},{5,6},{6,7},{7,4},{8,9},{9,10},{10,1... | collective-permute-start | bytes 835592 | tf_op jit(solution)/shard_map/ppermute | solution.py:391
  47.3 0.0 collective-permute-start.8
  47.3 0.0 copy-done.9
  47.3 23.3 %all-gather = s32[16,1,512]{2,1,0:T(1,128)S(1)} all-gather(s32[1,1,512]{2,1,0:T(1,128)S(1)} %fusion.9), channel_id=1, replica_groups=mesh['box'=2,'gy'=4,'gz'=4] {'gy','gz'}, dimensions={0}, use_global_device_ids=true | all-gather | bytes 34816 | tf_op jit(solution)/shard_map/all_gather | solution.py:349
  70.7 1.2 %stack.48.lists = s32[9,512]{1,0:T(8,128)} concatenate(s32[1,512]{1,0:T(1,128)S(1)} %get-tuple-element.31, s32[1,512]{1,0:T(1,128)S(1)} %get-tuple-element.30, s32[1,512]{1,0:T(1,128)S(1)} %get-tuple-element.29, s32[1,512]{1,0:T(1,128)S(1)} %get-tuple-element.28, s32[1,512]{1,0:T(1,128)S(1)} %get-tuple-element.27, s32[1,512]{1,0:T(1,128)S(1)} %get-tuple-element.26, ...), dimensions={0} | concatenate | bytes 36864 | tf_op jit(solution)/shard_map/stack | solution.py:358
  71.9 3.7 %shard_map.49.count = f32[4,16,24,128]{3,2,1,0:T(8,128)} custom-call(s32[9,512]{1,0:T(8,128)} %stack.48.lists), custom_call_target="tpu_custom_call" | custom-call | tf_op jit(solution)/shard_map/pallas_call | solution.py:38
  75.6 0.0 collective-permute-done.7.cunder
  75.6 0.0 collective-permute-done.8.cover
  75.6 0.0 copy-start.8
  75.6 0.0 collective-permute-done.5.under
  75.6 0.0 copy-start.3
  75.6 0.0 collective-permute-done.6.over
  75.6 0.7 copy-done.7
  76.3 0.1 copy-done.8
  76.4 0.3 copy-done.3
  76.7 0.9 copy-done.4
  77.6 28.4 %shard_map.50 = f32[3,8,16,512]{3,2,1,0:T(8,128)} custom-call(s32[6]{0:T(128)} %stack.47.scal, f32[3,8,16,512]{3,2,1,0:T(8,128)} %bitcast.34, f32[576,128]{1,0:T(8,128)} %copy-done.1, f32[576,128]{1,0:T(8,128)} %copy-done.2, f32[768,128]{1,0:T(8,128)} %copy-done, f32[288,128]{1,0:T(8,128)} %copy-done.5, f32[288,128]{1,0:T(8,128)} %copy-done.6, ...), custom_call_target="tpu_custom_call" | custom-call | tf_op jit(solution)/shard_map/pallas_call | solution.py:38
  (4 shorter events, 0.0 us)
Async XLA Ops:
  3.5 16.2 %copy-start.11 = (f32[576,128]{1,0:T(8,128)S(1)}, f32[576,128]{1,0:T(8,128)}, u32[]{:S(2)}) copy-start(f32[576,128]{1,0:T(8,128)} %get-tuple-element.14) | copy-start | bytes 884740
  3.5 17.5 %copy-start.10 = (f32[576,128]{1,0:T(8,128)S(1)}, f32[576,128]{1,0:T(8,128)}, u32[]{:S(2)}) copy-start(f32[576,128]{1,0:T(8,128)} %get-tuple-element.15) | copy-start | bytes 884740
  3.5 10.2 %collective-permute-start.2 = (f32[768,128]{1,0:T(8,128)}, f32[768,128]{1,0:T(8,128)S(1)}, u32[]{:S(2)}, u32[]{:S(2)}) collective-permute-start(f32[768,128]{1,0:T(8,128)} %get-tuple-element.16), channel_id=1, source_target_pairs={{0,16},{16,0},{1,17},{17,1},{2,18},{18,2},{3,19},{19,3},{4,20},{20... | collective-permute-start | bytes 1179656 | tf_op jit(solution)/shard_map/ppermute | solution.py:372
  13.7 0.8 copy-start
  17.1 58.5 %collective-permute-start.5 = (f32[1728,128]{1,0:T(8,128)}, f32[1728,128]{1,0:T(8,128)S(1)}, u32[]{:S(2)}, u32[]{:S(2)}) collective-permute-start(f32[1728,128]{1,0:T(8,128)} %get-tuple-element.19), channel_id=1, source_target_pairs={{0,1},{1,2},{2,3},{3,0},{4,5},{5,6},{6,7},{7,4},{8,9},{9,10},{10,1... | collective-permute-start | bytes 2654216 | tf_op jit(solution)/shard_map/ppermute | solution.py:383
  19.8 55.9 %collective-permute-start.6 = (f32[1728,128]{1,0:T(8,128)}, f32[1728,128]{1,0:T(8,128)S(1)}, u32[]{:S(2)}, u32[]{:S(2)}) collective-permute-start(f32[1728,128]{1,0:T(8,128)} %get-tuple-element.20), channel_id=1, source_target_pairs={{0,3},{1,0},{2,1},{3,2},{4,7},{5,4},{6,5},{7,6},{8,11},{9,8},{10,9... | collective-permute-start | bytes 2654216 | tf_op jit(solution)/shard_map/ppermute | solution.py:384
  19.8 9.9 %collective-permute-start = (f32[576,128]{1,0:T(8,128)S(1)}, f32[576,128]{1,0:T(8,128)S(1)}, u32[]{:S(2)}, u32[]{:S(2)}) collective-permute-start(f32[576,128]{1,0:T(8,128)S(1)} %copy-done.11), channel_id=1, source_target_pairs={{0,4},{4,8},{8,12},{12,0},{1,5},{5,9},{9,13},{13,1},{2,6},{6,10},{... | collective-permute-start | bytes 884744 | tf_op jit(solution)/shard_map/ppermute | solution.py:373
  21.1 14.6 %collective-permute-start.1 = (f32[576,128]{1,0:T(8,128)S(1)}, f32[576,128]{1,0:T(8,128)S(1)}, u32[]{:S(2)}, u32[]{:S(2)}) collective-permute-start(f32[576,128]{1,0:T(8,128)S(1)} %copy-done.10), channel_id=1, source_target_pairs={{0,12},{4,0},{8,4},{12,8},{1,13},{5,1},{9,5},{13,9},{2,14},{6,2},{... | collective-permute-start | bytes 884744 | tf_op jit(solution)/shard_map/ppermute | solution.py:374
  23.2 16.0 %collective-permute-start.3 = (f32[288,128]{1,0:T(8,128)}, f32[288,128]{1,0:T(8,128)S(1)}, u32[]{:S(2)}, u32[]{:S(2)}) collective-permute-start(f32[288,128]{1,0:T(8,128)} %get-tuple-element.17), channel_id=1, source_target_pairs={{0,4},{4,8},{8,12},{12,0},{1,5},{5,9},{9,13},{13,1},{2,6},{6,10},{... | collective-permute-start | bytes 442376 | tf_op jit(solution)/shard_map/ppermute | solution.py:381
  29.7 12.3 %copy-start.1 = (f32[576,128]{1,0:T(8,128)}, f32[576,128]{1,0:T(8,128)S(1)}, u32[]{:S(2)}) copy-start(f32[576,128]{1,0:T(8,128)S(1)} %collective-permute-done.left) | copy-start | bytes 884740
  29.7 12.3 %collective-permute-start.4 = (f32[288,128]{1,0:T(8,128)}, f32[288,128]{1,0:T(8,128)S(1)}, u32[]{:S(2)}, u32[]{:S(2)}) collective-permute-start(f32[288,128]{1,0:T(8,128)} %get-tuple-element.18), channel_id=1, source_target_pairs={{0,12},{4,0},{8,4},{12,8},{1,13},{5,1},{9,5},{13,9},{2,14},{6,2},{... | collective-permute-start | bytes 442376 | tf_op jit(solution)/shard_map/ppermute | solution.py:382
  35.7 6.3 %copy-start.2 = (f32[576,128]{1,0:T(8,128)}, f32[576,128]{1,0:T(8,128)S(1)}, u32[]{:S(2)}) copy-start(f32[576,128]{1,0:T(8,128)S(1)} %collective-permute-done.1.right) | copy-start | bytes 884740
  39.2 2.8 %copy-start.5 = (f32[288,128]{1,0:T(8,128)}, f32[288,128]{1,0:T(8,128)S(1)}, u32[]{:S(2)}) copy-start(f32[288,128]{1,0:T(8,128)S(1)} %collective-permute-done.3.fleft) | copy-start | bytes 442372
  42.0 0.7 copy-start.6
  44.7 2.6 %copy-start.9 = (s32[1,1,512]{2,1,0:T(1,128)S(1)}, s32[1,1,512]{2,1,0:T(1,128)}, u32[]{:S(2)}) copy-start(s32[1,1,512]{2,1,0:T(1,128)} %param.5) | copy-start | bytes 6148
  44.7 30.9 %collective-permute-start.7 = (f32[544,128]{1,0:T(8,128)}, f32[544,128]{1,0:T(8,128)S(1)}, u32[]{:S(2)}, u32[]{:S(2)}) collective-permute-start(f32[544,128]{1,0:T(8,128)} %get-tuple-element.21), channel_id=1, source_target_pairs={{0,1},{1,2},{2,3},{3,0},{4,5},{5,6},{6,7},{7,4},{8,9},{9,10},{10,1... | collective-permute-start | bytes 835592 | tf_op jit(solution)/shard_map/ppermute | solution.py:391
  47.3 28.3 %collective-permute-start.8 = (f32[544,128]{1,0:T(8,128)}, f32[544,128]{1,0:T(8,128)S(1)}, u32[]{:S(2)}, u32[]{:S(2)}) collective-permute-start(f32[544,128]{1,0:T(8,128)} %get-tuple-element.22), channel_id=1, source_target_pairs={{0,3},{1,0},{2,1},{3,2},{4,7},{5,4},{6,5},{7,6},{8,11},{9,8},{10,9... | collective-permute-start | bytes 835592 | tf_op jit(solution)/shard_map/ppermute | solution.py:392
  75.6 0.7 copy-start.7
  75.6 0.8 copy-start.8
  75.6 1.1 %copy-start.3 = (f32[1728,128]{1,0:T(8,128)}, f32[1728,128]{1,0:T(8,128)S(1)}, u32[]{:S(2)}) copy-start(f32[1728,128]{1,0:T(8,128)S(1)} %collective-permute-done.5.under) | copy-start | bytes 2654212
  76.7 0.9 copy-start.4

commit v2 on v1

v2 whole, which is shorter than its diff:
```python
import functools

import jax
import jax.numpy as jnp
from jax import lax
from jax.experimental import pallas as pl
from jax.experimental.pallas import tpu as pltpu
from jax.sharding import PartitionSpec as P

FW = 128
LANES = 128
HALO = 6
YOFF = 8
MARGIN = 64

smag_coef = 0.1024
drag_coef = 0.665
time_step = 0.2
LISTED = 4


def corner_rows():
    offset, table = 0, []
    for distance in range(1, HALO):
        table.append((distance, HALO - distance, offset))
        offset += HALO - distance
    return table, offset


def whole_vmem(count):
    return [pl.BlockSpec(memory_space=pltpu.VMEM)] * count


def call(kernel, outs, ins, smem, limit, cost, scratch=()):
    specs = [
        pl.BlockSpec(memory_space=pltpu.SMEM if i < smem else pltpu.VMEM) for i in range(len(ins))
    ]
    return pl.pallas_call(
        kernel,
        out_shape=[jax.ShapeDtypeStruct(shape, jnp.float32) for shape in outs],
        in_specs=specs,
        out_specs=whole_vmem(len(outs)),
        scratch_shapes=list(scratch),
        compiler_params=pltpu.CompilerParams(vmem_limit_bytes=limit * 1024 * 1024),
        cost_estimate=pl.CostEstimate(flops=cost, bytes_accessed=cost, transcendentals=0),
    )(*ins)


def place(start, columns):
    origin = lax.rem(start + columns - MARGIN, columns)
    return origin // LANES, lax.rem(origin, LANES)


def pack_own(dims, start, live, cells, u, fringe, up, down, above, below):
    tiles, depth, width = dims
    first, lane0 = place(start[0], tiles * LANES)
    lane = lax.broadcasted_iota(jnp.int32, (width, LANES), 1)
    picked = [lax.rem(first + k, tiles) for k in range(3)]
    slot = lax.broadcasted_iota(jnp.int32, (1, LANES), 1)
    for k in range(LISTED):
        row = cells[0, :, pl.ds(k * LANES, LANES)]
        row = jnp.where(slot + k * LANES < live[0, 0], row, -1).astype(jnp.float32)
        for out in (above, below):
            out[pl.ds(3 * tiles * HALO * width + k, 1), :] = row
    for c in range(3):
        for t in range(tiles):
            cols = pl.ds(t * LANES, LANES)
            for z in range(depth):
                at = ((c * tiles + t) * depth + z) * HALO
                up[pl.ds(at, HALO), :] = u[c, z, width - HALO :, cols]
                down[pl.ds(at, HALO), :] = u[c, z, :HALO, cols]
            for h in range(HALO):
                at = ((c * tiles + t) * HALO + h) * width
                above[pl.ds(at, width), :] = u[c, depth - HALO + h, :, cols]
                below[pl.ds(at, width), :] = u[c, h, :, cols]
    for c in range(3):
        for z in range(depth):
            rows = [u[c, z, :, pl.ds(pl.multiple_of(p * LANES, LANES), LANES)] for p in picked]
            for k in range(2):
                at = ((c * 2 + k) * depth + z) * width
                fringe[pl.ds(at, width), :] = jnp.where(lane >= lane0, rows[k], rows[k + 1])


def pack_window(dims, own, under, over, fringe, fup, fdown, above, below):
    tiles, depth, width = dims
    listed = 3 * tiles * HALO * width
    for k, source in enumerate((under, own, over)):
        for out in (fup, fdown):
            out[pl.ds(3 * 2 * depth * HALO + k * LISTED, LISTED), :] = source[pl.ds(listed, LISTED), :]
    for c in range(3):
        for k in range(2):
            for z in range(depth):
                at = ((c * 2 + k) * depth + z) * HALO
                src = ((c * 2 + k) * depth + z) * width
                fup[pl.ds(at, HALO), :] = fringe[pl.ds(src + width - HALO, HALO), :]
                fdown[pl.ds(at, HALO), :] = fringe[pl.ds(src, HALO), :]
            for h in range(HALO):
                at = ((c * 2 + k) * HALO + h) * width
                for out, z in ((above, depth - HALO + h), (below, h)):
                    src = ((c * 2 + k) * depth + z) * width
                    out[pl.ds(at, width), :] = fringe[pl.ds(src, width), :]


def pack_corners(dims, left, right, fleft, fright, above, below):
    tiles, depth, _ = dims
    table, total = corner_rows()
    for c in range(3):
        for t in range(tiles + 2):
            for side in range(2):
                for distance, rows, offset in table:
                    at = ((c * (tiles + 2) + t) * 2 + side) * total + offset
                    for out, z in ((above, depth - distance), (below, distance - 1)):
                        if t < tiles:
                            src, row = (left, right)[side], ((c * tiles + t) * depth + z) * HALO
                        else:
                            src, row = (fleft, fright)[side], ((c * 2 + t - tiles) * depth + z) * HALO
                        row = row + (HALO - rows if side == 0 else 0)
                        out[pl.ds(at, rows), :] = src[pl.ds(row, rows), :]


def multiplicity(dims, own, under, over, fleft, fright, out):
    tiles, depth, width = dims
    reach = HALO - 2
    rows = width + 2 * reach
    levels = depth + 2 * reach
    columns = tiles * LANES
    bottom = lax.axis_index("gz") == 0
    top = lax.axis_index("gz") == lax.axis_size("gz") - 1
    row_iota = lax.broadcasted_iota(jnp.int32, (levels * rows, LANES), 0)
    col_iota = lax.broadcasted_iota(jnp.int32, (columns, LANES), 0)
    level_at, window_at = 3 * tiles * HALO * width, 3 * 2 * depth * HALO
    total = jnp.zeros((levels * rows, columns), jnp.float32)
    for index in range(9):
        oz, oy = index // 3 - 1, index % 3 - 1
        if oy == 0:
            source, at = (under, own, over)[oz + 1], level_at
        else:
            source, at = (fleft, None, fright)[oy + 1], window_at + (oz + 1) * LISTED
        for k in range(LISTED):
            cell = source[pl.ds(at + k, 1), :].astype(jnp.int32)
            x = cell % columns
            y = cell // columns % width + oy * width + reach
            z = cell // (columns * width) + oz * depth + reach
            fits = (cell >= 0) & (y >= 0) & (y < rows) & (z >= 0) & (z < levels)
            if oz < 0:
                fits = fits & jnp.logical_not(bottom)
            if oz > 0:
                fits = fits & jnp.logical_not(top)
            row = jnp.where(fits, z * rows + y, -1)
            one = (row_iota == row).astype(jnp.float32).astype(jnp.bfloat16)
            two = (col_iota == x).astype(jnp.float32).astype(jnp.bfloat16)
            total = total + lax.dot_general(
                one, two, (((1,), (1,)), ((), ())), preferred_element_type=jnp.float32
            )
    for t in range(tiles):
        out[t] = total[:, t * LANES : (t + 1) * LANES].reshape(levels, rows, LANES)


def xdiff(value, first, last, nleft, nright):
    ahead = pltpu.roll(value, LANES - 1, 2)
    behind = pltpu.roll(value, 1, 2)
    parts = []
    for i in range(value.shape[0]):
        right = jnp.where(last, ahead[nright[i]], ahead[i])
        left = jnp.where(first, behind[nleft[i]], behind[i])
        parts.append(right - left)
    return jnp.stack(parts)


def tau_tile(src, tau, part, z, y0, span, seam, inside, keep_part):
    first, last, nleft, nright = seam
    here = pl.ds(y0, 8)
    u = [src[c, span, z, here, :] for c in range(3)]
    gx = [xdiff(v, first, last, nleft, nright) for v in u]
    gy = [
        src[c, span, z, pl.ds(y0 + 1, 8), :] - src[c, span, z, pl.ds(y0 - 1, 8), :]
        for c in range(3)
    ]
    gz = [src[c, span, z + 1, here, :] - src[c, span, z - 1, here, :] for c in range(3)]
    xy = gx[1] + gy[0]
    xz = gx[2] + gz[0]
    yz = gy[2] + gz[1]
    diag = gx[0] * gx[0] + gy[1] * gy[1] + gz[2] * gz[2]
    off = xy * xy + xz * xz + yz * yz
    visc = jnp.sqrt(0.5 * diag + 0.25 * off)
    if inside is not None:
        visc = visc * inside
    half = visc * 0.5
    for k, value in enumerate(
        (visc * gx[0], visc * gy[1], visc * gz[2], half * xy, half * xz, half * yz)
    ):
        tau[k, span, z, here, :] = value
    if keep_part:
        scaled = [v * (-0.5 * time_step) for v in u]
        for c in range(3):
            part[c, span, z, here, :] = u[c] + (
                scaled[0] * gx[c] + scaled[1] * gy[c] + scaled[2] * gz[c]
            )


TAU = ((0, 3, 4), (3, 1, 5), (4, 5, 2))


def out_tile(src, base, tau, part, z, y0, span, seam, weights):
    first, last, nleft, nright = seam
    here = pl.ds(y0, 8)
    keep, take = weights
    results = []
    for c in range(3):
        div = xdiff(tau[TAU[c][0], span, z, here, :], first, last, nleft, nright)
        div = div + (
            tau[TAU[c][1], span, z, pl.ds(y0 + 1, 8), :]
            - tau[TAU[c][1], span, z, pl.ds(y0 - 1, 8), :]
        )
        div = div + (tau[TAU[c][2], span, z + 1, here, :] - tau[TAU[c][2], span, z - 1, here, :])
        value = part[c, span, z, here, :] * take + div * (take * time_step * 0.5 * smag_coef)
        if keep:
            value = value + keep * base[c, span, z, here, :]
        results.append(value)
    return results


def step_kernel(
    dims, first_column, u, left, right, fringe, fleft, fright, under, over, funder, fover,
    cunder, cover, count, out, u0, u1, u2, tau, part,
):
    tiles, depth, width = dims
    start = first_column[0]
    _, lane0 = place(start, tiles * LANES)
    main = lax.axis_index("box")
    bottom = (lax.axis_index("gz") == 0).astype(jnp.int32)
    top = (lax.axis_index("gz") == lax.axis_size("gz") - 1).astype(jnp.int32)
    table, total = corner_rows()
    all_tiles = tiles + 2
    for c in range(3):
        for t in range(tiles):
            cols = pl.ds(t * LANES, LANES)
            for z in range(depth):
                at = ((c * tiles + t) * depth + z) * HALO
                u0[c, t, z + HALO, pl.ds(YOFF, width), :] = u[c, z, :, cols]
                u0[c, t, z + HALO, pl.ds(YOFF - HALO, HALO), :] = left[pl.ds(at, HALO), :]
                u0[c, t, z + HALO, pl.ds(YOFF + width, HALO), :] = right[pl.ds(at, HALO), :]
        for k in range(2):
            for z in range(depth):
                at = (c * 2 + k) * depth + z
                rows = pl.ds(at * HALO, HALO)
                u0[c, tiles + k, z + HALO, pl.ds(YOFF, width), :] = fringe[pl.ds(at * width, width), :]
                u0[c, tiles + k, z + HALO, pl.ds(YOFF - HALO, HALO), :] = fleft[rows, :]
                u0[c, tiles + k, z + HALO, pl.ds(YOFF + width, HALO), :] = fright[rows, :]
        for t in range(all_tiles):
            for h in range(HALO):
                lower, upper, at = under, over, (c * tiles + t) * HALO + h
                if t >= tiles:
                    lower, upper, at = funder, fover, (c * 2 + t - tiles) * HALO + h
                rows = pl.ds(at * width, width)
                u0[c, t, h, pl.ds(YOFF, width), :] = lower[rows, :]
                u0[c, t, HALO + depth + h, pl.ds(YOFF, width), :] = upper[rows, :]
            for side in range(2):
                for distance, rows, offset in table:
                    at = ((c * all_tiles + t) * 2 + side) * total + offset
                    y = YOFF - rows if side == 0 else YOFF + width
                    u0[c, t, HALO - distance, pl.ds(y, rows), :] = cunder[pl.ds(at, rows), :]
                    u0[c, t, HALO + depth + distance - 1, pl.ds(y, rows), :] = cover[pl.ds(at, rows), :]

    def clear(z):
        for c in range(3):
            u0[c, :, z] = jnp.zeros(u0.shape[1:2] + u0.shape[3:], jnp.float32)

    @pl.when(bottom == 1)
    def _():
        lax.fori_loop(0, HALO, lambda i, _: clear(i), None)

    @pl.when(top == 1)
    def _():
        lax.fori_loop(0, HALO, lambda i, _: clear(HALO + depth + i), None)

    lane = lax.broadcasted_iota(jnp.int32, (8, LANES), 1)
    order = list(range(tiles))
    main_seam = (lane == 0, lane == LANES - 1, order[-1:] + order[:-1], order[1:] + order[:1])
    window_seam = (lane == lane0, lane == lax.rem(lane0 + LANES - 1, LANES), [1, 0], [1, 0])
    main_span, window_span = slice(0, tiles), slice(tiles, tiles + 2)

    def inside_of(z):
        if HALO <= z < HALO + depth:
            return None
        return 1.0 - (bottom if z < HALO else top).astype(jnp.float32)

    def sweep(margin, body):
        for z in range(HALO - margin, HALO + depth + margin):
            reach = margin - max(HALO - z, z - (HALO + depth - 1), 0)
            stop = YOFF + width + reach - 8
            for y0 in list(range(YOFF - reach, stop, 8)) + [stop]:
                body(z, y0)

    def tau_stage(src, margin, span, seam):
        def body(z, y0):
            tau_tile(src, tau, part, z, y0, span, seam, inside_of(z), True)

        sweep(margin, body)

    def out_stage(src, dst, margin, weights, span, seam, blended):
        reach = HALO - 2

        def body(z, y0):
            here = pl.ds(y0, 8)
            values = out_tile(src, u0, tau, part, z, y0, span, seam, weights)
            if blended:
                ux = src[0, span, z, here, :]
                times = count[:, z - HALO + reach, pl.ds(y0 - YOFF + reach, 8), :]
                factor = jnp.where(main == 1, -drag_coef * time_step * weights[1], 0.0)
                values[0] = values[0] + (times * factor) * (ux * jnp.abs(ux))
            for c in range(3):
                value = values[c]
                if blended:
                    near = dst[c, tiles, z, here, :]
                    far = dst[c, tiles + 1, z, here, :]
                    parts = []
                    for t in range(tiles):
                        col = lane + t * LANES
                        mask = (col >= start) & (col < start + FW) & (main == 1)
                        other = jnp.where(col < start + MARGIN, near, far)
                        parts.append(jnp.where(mask, 0.5 * (value[t] + other), value[t]))
                    value = jnp.stack(parts)
                if inside_of(z) is not None:
                    value = value * inside_of(z)
                dst[c, span, z, here, :] = value

        sweep(margin, body)

    stages = (
        (u0, u1, HALO - 1, (0.0, 1.0)),
        (u1, u2, HALO - 3, (0.75, 0.25)),
        (u2, u1, HALO - 5, (1.0 / 3.0, 2.0 / 3.0)),
    )
    for src, dst, margin, weights in stages:

        @pl.when(main == 1)
        def _():
            tau_stage(src, margin, window_span, window_seam)
            out_stage(src, dst, margin - 1, weights, window_span, window_seam, False)

        tau_stage(src, margin, main_span, main_seam)
        out_stage(src, dst, margin - 1, weights, main_span, main_seam, True)
    for c in range(3):
        for t in range(tiles):
            for z in range(depth):
                out[c, z, :, pl.ds(t * LANES, LANES)] = u1[c, t, z + HALO, pl.ds(YOFF, width), :]


def around(axis, by):
    count = lax.axis_size(axis)
    return [(i, (i + by) % count) for i in range(count)]


def per_device(velocity, turbine_cells, turbine_count, fringe_start):
    u = velocity[0]
    _, depth, width, columns = u.shape
    tiles = columns // LANES
    dims = (tiles, depth, width)

    halo_rows = 3 * tiles * depth * HALO
    level_rows = 3 * tiles * HALO * width + 8
    window_halo_rows = 3 * 2 * depth * HALO + 16
    window_level_rows = 3 * 2 * HALO * width
    corner = 3 * (tiles + 2) * 2 * corner_rows()[1]
    corner = (corner + 7) // 8 * 8

    fringe, up, down, above, below = call(
        functools.partial(pack_own, dims),
        [
            (3 * 2 * depth * width, LANES),
            (halo_rows, LANES),
            (halo_rows, LANES),
            (level_rows, LANES),
            (level_rows, LANES),
        ],
        (fringe_start, turbine_count, turbine_cells, u),
        2,
        12,
        1,
    )
    left = lax.ppermute(up, "gy", around("gy", 1))
    right = lax.ppermute(down, "gy", around("gy", -1))
    under = lax.ppermute(above, "gz", around("gz", 1))
    over = lax.ppermute(below, "gz", around("gz", -1))
    fringe = lax.ppermute(fringe, "box", [(0, 1), (1, 0)])
    fup, fdown, fabove, fbelow = call(
        functools.partial(pack_window, dims),
        [
            (window_halo_rows, LANES),
            (window_halo_rows, LANES),
            (window_level_rows, LANES),
            (window_level_rows, LANES),
        ],
        (above, under, over, fringe),
        0,
        12,
        1,
    )
    fleft = lax.ppermute(fup, "gy", around("gy", 1))
    fright = lax.ppermute(fdown, "gy", around("gy", -1))
    funder = lax.ppermute(fabove, "gz", around("gz", 1))
    fover = lax.ppermute(fbelow, "gz", around("gz", -1))
    cabove, cbelow = call(
        functools.partial(pack_corners, dims),
        [(corner, LANES), (corner, LANES)],
        (left, right, fleft, fright),
        0,
        8,
        1,
    )
    cunder = lax.ppermute(cabove, "gz", around("gz", 1))
    cover = lax.ppermute(cbelow, "gz", around("gz", -1))

    reach = HALO - 2
    (count,) = call(
        functools.partial(multiplicity, dims),
        [(tiles, depth + 2 * reach, width + 2 * reach, LANES)],
        (above, under, over, fleft, fright),
        0,
        12,
        8_000_000,
    )
    ext = (tiles + 2, depth + 2 * HALO, width + 2 * YOFF, LANES)
    (out,) = call(
        functools.partial(step_kernel, dims),
        [u.shape],
        (fringe_start, u, left, right, fringe, fleft, fright, under, over, funder, fover, cunder, cover, count),
        1,
        48,
        8_000_000,
        [pltpu.VMEM((n,) + ext, jnp.float32) for n in (3, 3, 3, 6, 3)],
    )
    return out[None]


def solution(mesh):
    placed = (P("box", None, "gz", "gy", None), P("gz", "gy", None), P("gz", "gy"), P())
    return jax.shard_map(
        per_device,
        mesh=mesh,
        in_specs=placed,
        out_specs=P("box", None, "gz", "gy", None),
        check_vma=False,
    )
```

time: 106 us -> 56.2 us (0.53)
  the two profiles are of different devices: /device:TPU:5 before, /device:TPU:7 now
where the time goes in v2:
time: 56.2 us; the launch traced here: 56 us
  Pallas kernels  21.6 us (38%)
  waiting for transfers between devices  20.8 us (37%)
  starting transfers between devices  11.1 us (20%)
  between operations  1.38 us (2%)
  local copies, waits for them, and re-layouts  1.15 us (2%)
    pallas_call x5, Pallas kernels, call(): pl.pallas_call(kernel, out_shape=[jax.ShapeDtypeStruct(shape, jnp.float32...  21.6 us
    ppermute x1, waiting for transfers between devices, per_device(): fringe = lax.ppermute(fringe, 'box', [(0, 1), (1, 0)])  7.48 us
    ppermute x1, waiting for transfers between devices, per_device(): cover = lax.ppermute(cbelow, 'gz', around('gz', -1))  4.59 us
    ppermute x1, waiting for transfers between devices, per_device(): over = lax.ppermute(below, 'gz', around('gz', -1))  3.17 us
    ppermute x1, waiting for transfers between devices, per_device(): fright = lax.ppermute(fdown, 'gy', around('gy', -1))  2.86 us
    ppermute x1, waiting for transfers between devices, per_device(): fleft = lax.ppermute(fup, 'gy', around('gy', 1))  2.67 us
    ppermute x1, starting transfers between devices, per_device(): fright = lax.ppermute(fdown, 'gy', around('gy', -1))  2.09 us
    ppermute x1, starting transfers between devices, per_device(): right = lax.ppermute(down, 'gy', around('gy', -1))  2.03 us
  transfers between devices with their start and end apart: 11, of which 5 were waited for; matrix products, arithmetic and copies ran while one was open for 0% of the time, Pallas kernels for 7%

profile of v2, /device:TPU:7, one launch (start us, length us, event | category | flops | bytes accessed | tf_op | source)
XLA Modules:
  0.0 56.0 jit_solution(17284410424056222085)
XLA Ops:
  0.7 0.0 copy-start.2
  1.3 0.0 copy-done.2
  1.3 0.0 copy-start
  1.3 1.1 %copy-done = f32[1,3,8,16,512]{4,3,2,1,0:T(8,128)S(1)} copy-done((f32[1,3,8,16,512]{4,3,2,1,0:T(8,128)S(1)}, f32[1,3,8,16,512]{4,3,2,1,0:T(8,128)}, u32[]{:S(2)}) %copy-start) | copy-done | bytes 786456
  2.5 0.2 shard_map.46
  2.7 0.7 %collective-permute-start.4 = (f32[1160,128]{1,0:T(8,128)S(1)}, f32[1160,128]{1,0:T(8,128)S(1)}, u32[]{:S(2)}, u32[]{:S(2)}) collective-permute-start(f32[1160,128]{1,0:T(8,128)S(1)} %get-tuple-element.20), channel_id=1, source_target_pairs={{0,3},{1,0},{2,1},{3,2},{4,7},{5,4},{6,5},{7,6},{8,11},{9,8},{10,9... | collective-permute-start | bytes 1781768 | tf_op jit(solution)/shard_map/ppermute | solution.py:385
  3.4 1.1 %collective-permute-start.3 = (f32[1160,128]{1,0:T(8,128)S(1)}, f32[1160,128]{1,0:T(8,128)S(1)}, u32[]{:S(2)}, u32[]{:S(2)}) collective-permute-start(f32[1160,128]{1,0:T(8,128)S(1)} %get-tuple-element.19.own), channel_id=1, source_target_pairs={{0,1},{1,2},{2,3},{3,0},{4,5},{5,6},{6,7},{7,4},{8,9},{9,10},{10,1... | collective-permute-start | bytes 1781768 | tf_op jit(solution)/shard_map/ppermute | solution.py:384
  4.5 0.2 collective-permute-start.2
  4.7 1.3 %collective-permute-start = (f32[576,128]{1,0:T(8,128)S(1)}, f32[576,128]{1,0:T(8,128)S(1)}, u32[]{:S(2)}, u32[]{:S(2)}) collective-permute-start(f32[576,128]{1,0:T(8,128)S(1)} %get-tuple-element.16), channel_id=1, source_target_pairs={{0,4},{4,8},{8,12},{12,0},{1,5},{5,9},{9,13},{13,1},{2,6},{6,10},{... | collective-permute-start | bytes 884744 | tf_op jit(solution)/shard_map/ppermute | solution.py:382
  6.0 2.0 %collective-permute-start.1 = (f32[576,128]{1,0:T(8,128)S(1)}, f32[576,128]{1,0:T(8,128)S(1)}, u32[]{:S(2)}, u32[]{:S(2)}) collective-permute-start(f32[576,128]{1,0:T(8,128)S(1)} %get-tuple-element.17), channel_id=1, source_target_pairs={{0,12},{4,0},{8,4},{12,8},{1,13},{5,1},{9,5},{13,9},{2,14},{6,2},{... | collective-permute-start | bytes 884744 | tf_op jit(solution)/shard_map/ppermute | solution.py:383
  8.0 7.5 %collective-permute-done.2.fringe = f32[768,128]{1,0:T(8,128)S(1)} collective-permute-done((f32[768,128]{1,0:T(8,128)S(1)}, f32[768,128]{1,0:T(8,128)S(1)}, u32[]{:S(2)}, u32[]{:S(2)}) %collective-permute-start.2) | collective-permute-done | bytes 393248 | tf_op jit(solution)/shard_map/ppermute | solution.py:386
  15.5 3.2 %collective-permute-done.4.over = f32[1160,128]{1,0:T(8,128)S(1)} collective-permute-done((f32[1160,128]{1,0:T(8,128)S(1)}, f32[1160,128]{1,0:T(8,128)S(1)}, u32[]{:S(2)}, u32[]{:S(2)}) %collective-permute-start.4) | collective-permute-done | bytes 593952 | tf_op jit(solution)/shard_map/ppermute | solution.py:385
  18.7 0.0 collective-permute-done.3.under
  18.7 0.1 shard_map.47
  18.7 1.3 %collective-permute-start.5 = (f32[304,128]{1,0:T(8,128)S(1)}, f32[304,128]{1,0:T(8,128)S(1)}, u32[]{:S(2)}, u32[]{:S(2)}) collective-permute-start(f32[304,128]{1,0:T(8,128)S(1)} %get-tuple-element.21), channel_id=1, source_target_pairs={{0,4},{4,8},{8,12},{12,0},{1,5},{5,9},{9,13},{13,1},{2,6},{6,10},{... | collective-permute-start | bytes 466952 | tf_op jit(solution)/shard_map/ppermute | solution.py:400
  20.1 2.1 %collective-permute-start.6 = (f32[304,128]{1,0:T(8,128)S(1)}, f32[304,128]{1,0:T(8,128)S(1)}, u32[]{:S(2)}, u32[]{:S(2)}) collective-permute-start(f32[304,128]{1,0:T(8,128)S(1)} %get-tuple-element.22), channel_id=1, source_target_pairs={{0,12},{4,0},{8,4},{12,8},{1,13},{5,1},{9,5},{13,9},{2,14},{6,2},{... | collective-permute-start | bytes 466952 | tf_op jit(solution)/shard_map/ppermute | solution.py:401
  22.2 1.1 %collective-permute-start.7 = (f32[576,128]{1,0:T(8,128)S(1)}, f32[576,128]{1,0:T(8,128)S(1)}, u32[]{:S(2)}, u32[]{:S(2)}) collective-permute-start(f32[576,128]{1,0:T(8,128)S(1)} %get-tuple-element.23), channel_id=1, source_target_pairs={{0,1},{1,2},{2,3},{3,0},{4,5},{5,6},{6,7},{7,4},{8,9},{9,10},{10,1... | collective-permute-start | bytes 884744 | tf_op jit(solution)/shard_map/ppermute | solution.py:402
  23.2 0.0 collective-permute-done.left
  23.2 0.0 collective-permute-start.8
  23.2 0.0 collective-permute-done.1.right
  23.3 2.7 %collective-permute-done.5.fleft = f32[304,128]{1,0:T(8,128)S(1)} collective-permute-done((f32[304,128]{1,0:T(8,128)S(1)}, f32[304,128]{1,0:T(8,128)S(1)}, u32[]{:S(2)}, u32[]{:S(2)}) %collective-permute-start.5) | collective-permute-done | bytes 155680 | tf_op jit(solution)/shard_map/ppermute | solution.py:400
  25.9 2.9 %collective-permute-done.6.fright = f32[304,128]{1,0:T(8,128)S(1)} collective-permute-done((f32[304,128]{1,0:T(8,128)S(1)}, f32[304,128]{1,0:T(8,128)S(1)}, u32[]{:S(2)}, u32[]{:S(2)}) %collective-permute-start.6) | collective-permute-done | bytes 155680 | tf_op jit(solution)/shard_map/ppermute | solution.py:401
  28.8 0.1 shard_map.48
  28.9 0.5 collective-permute-start.9
  29.4 0.0 copy-start.1
  29.4 0.7 %collective-permute-start.10 = (f32[544,128]{1,0:T(8,128)S(1)}, f32[544,128]{1,0:T(8,128)S(1)}, u32[]{:S(2)}, u32[]{:S(2)}) collective-permute-start(f32[544,128]{1,0:T(8,128)S(1)} %get-tuple-element.26), channel_id=1, source_target_pairs={{0,3},{1,0},{2,1},{3,2},{4,7},{5,4},{6,5},{7,6},{8,11},{9,8},{10,9... | collective-permute-start | bytes 835592 | tf_op jit(solution)/shard_map/ppermute | solution.py:413
  30.1 3.8 %shard_map.49.count = f32[4,16,24,128]{3,2,1,0:T(8,128)S(1)} custom-call(f32[1160,128]{1,0:T(8,128)S(1)} %get-tuple-element.19.own, f32[1160,128]{1,0:T(8,128)S(1)} %collective-permute-done.3.under, f32[1160,128]{1,0:T(8,128)S(1)} %collective-permute-done.4.over, f32[304,128]{1,0:T(8,128)S(1)} %collective-permute-done.5.fleft, ...), custom_call_target="tpu_custom_call" | custom-call | flops 8000000 | bytes 8000000 | tf_op jit(solution)/shard_map/pallas_call | solution.py:38
  33.9 0.0 collective-permute-done.7.funder
  34.0 0.0 collective-permute-done.8.fover
  34.0 0.0 collective-permute-done.9.cunder
  34.0 4.6 %collective-permute-done.10.cover = f32[544,128]{1,0:T(8,128)S(1)} collective-permute-done((f32[544,128]{1,0:T(8,128)S(1)}, f32[544,128]{1,0:T(8,128)S(1)}, u32[]{:S(2)}, u32[]{:S(2)}) %collective-permute-start.10) | collective-permute-done | bytes 278560 | tf_op jit(solution)/shard_map/ppermute | solution.py:413
  38.6 0.0 copy-done.1
  38.6 17.4 %shard_map.50 = f32[3,8,16,512]{3,2,1,0:T(8,128)} custom-call(s32[1]{0:T(128)S(6)} %copy.6.start.first_column, f32[3,8,16,512]{3,2,1,0:T(8,128)S(1)} %bitcast.3, f32[576,128]{1,0:T(8,128)S(1)} %collective-permute-done.left, f32[576,128]{1,0:T(8,128)S(1)} %collective-permute-done.1.right, f32[768,128]{1,0:T(8,128)S(1)} %collective-permute-done.2.fringe, ...), custom_call_target="tpu_custom_call" | custom-call | flops 8000000 | bytes 8000000 | tf_op jit(solution)/shard_map/pallas_call | solution.py:38
Async XLA Ops:
  0.7 0.7 %copy-start.2 = (s32[1,1,512]{2,1,0:T(1,128)S(1)}, s32[1,1,512]{2,1,0:T(1,128)}, u32[]{:S(2)}) copy-start(s32[1,1,512]{2,1,0:T(1,128)} %cells.1) | copy-start | bytes 6148
  1.3 1.1 %copy-start = (f32[1,3,8,16,512]{4,3,2,1,0:T(8,128)S(1)}, f32[1,3,8,16,512]{4,3,2,1,0:T(8,128)}, u32[]{:S(2)}) copy-start(f32[1,3,8,16,512]{4,3,2,1,0:T(8,128)} %param.4) | copy-start | bytes 2359300
  2.7 16.0 %collective-permute-start.4 = (f32[1160,128]{1,0:T(8,128)S(1)}, f32[1160,128]{1,0:T(8,128)S(1)}, u32[]{:S(2)}, u32[]{:S(2)}) collective-permute-start(f32[1160,128]{1,0:T(8,128)S(1)} %get-tuple-element.20), channel_id=1, source_target_pairs={{0,3},{1,0},{2,1},{3,2},{4,7},{5,4},{6,5},{7,6},{8,11},{9,8},{10,9... | collective-permute-start | bytes 1781768 | tf_op jit(solution)/shard_map/ppermute | solution.py:385
  3.4 15.3 %collective-permute-start.3 = (f32[1160,128]{1,0:T(8,128)S(1)}, f32[1160,128]{1,0:T(8,128)S(1)}, u32[]{:S(2)}, u32[]{:S(2)}) collective-permute-start(f32[1160,128]{1,0:T(8,128)S(1)} %get-tuple-element.19.own), channel_id=1, source_target_pairs={{0,1},{1,2},{2,3},{3,0},{4,5},{5,6},{6,7},{7,4},{8,9},{9,10},{10,1... | collective-permute-start | bytes 1781768 | tf_op jit(solution)/shard_map/ppermute | solution.py:384
  4.5 11.0 %collective-permute-start.2 = (f32[768,128]{1,0:T(8,128)S(1)}, f32[768,128]{1,0:T(8,128)S(1)}, u32[]{:S(2)}, u32[]{:S(2)}) collective-permute-start(f32[768,128]{1,0:T(8,128)S(1)} %get-tuple-element.18), channel_id=1, source_target_pairs={{0,16},{16,0},{1,17},{17,1},{2,18},{18,2},{3,19},{19,3},{4,20},{20... | collective-permute-start | bytes 1179656 | tf_op jit(solution)/shard_map/ppermute | solution.py:386
  4.7 18.6 %collective-permute-start = (f32[576,128]{1,0:T(8,128)S(1)}, f32[576,128]{1,0:T(8,128)S(1)}, u32[]{:S(2)}, u32[]{:S(2)}) collective-permute-start(f32[576,128]{1,0:T(8,128)S(1)} %get-tuple-element.16), channel_id=1, source_target_pairs={{0,4},{4,8},{8,12},{12,0},{1,5},{5,9},{9,13},{13,1},{2,6},{6,10},{... | collective-permute-start | bytes 884744 | tf_op jit(solution)/shard_map/ppermute | solution.py:382
  6.0 17.3 %collective-permute-start.1 = (f32[576,128]{1,0:T(8,128)S(1)}, f32[576,128]{1,0:T(8,128)S(1)}, u32[]{:S(2)}, u32[]{:S(2)}) collective-permute-start(f32[576,128]{1,0:T(8,128)S(1)} %get-tuple-element.17), channel_id=1, source_target_pairs={{0,12},{4,0},{8,4},{12,8},{1,13},{5,1},{9,5},{13,9},{2,14},{6,2},{... | collective-permute-start | bytes 884744 | tf_op jit(solution)/shard_map/ppermute | solution.py:383
  18.7 7.2 %collective-permute-start.5 = (f32[304,128]{1,0:T(8,128)S(1)}, f32[304,128]{1,0:T(8,128)S(1)}, u32[]{:S(2)}, u32[]{:S(2)}) collective-permute-start(f32[304,128]{1,0:T(8,128)S(1)} %get-tuple-element.21), channel_id=1, source_target_pairs={{0,4},{4,8},{8,12},{12,0},{1,5},{5,9},{9,13},{13,1},{2,6},{6,10},{... | collective-permute-start | bytes 466952 | tf_op jit(solution)/shard_map/ppermute | solution.py:400
  20.1 8.7 %collective-permute-start.6 = (f32[304,128]{1,0:T(8,128)S(1)}, f32[304,128]{1,0:T(8,128)S(1)}, u32[]{:S(2)}, u32[]{:S(2)}) collective-permute-start(f32[304,128]{1,0:T(8,128)S(1)} %get-tuple-element.22), channel_id=1, source_target_pairs={{0,12},{4,0},{8,4},{12,8},{1,13},{5,1},{9,5},{13,9},{2,14},{6,2},{... | collective-permute-start | bytes 466952 | tf_op jit(solution)/shard_map/ppermute | solution.py:401
  22.2 11.8 %collective-permute-start.7 = (f32[576,128]{1,0:T(8,128)S(1)}, f32[576,128]{1,0:T(8,128)S(1)}, u32[]{:S(2)}, u32[]{:S(2)}) collective-permute-start(f32[576,128]{1,0:T(8,128)S(1)} %get-tuple-element.23), channel_id=1, source_target_pairs={{0,1},{1,2},{2,3},{3,0},{4,5},{5,6},{6,7},{7,4},{8,9},{9,10},{10,1... | collective-permute-start | bytes 884744 | tf_op jit(solution)/shard_map/ppermute | solution.py:402
  23.2 10.7 %collective-permute-start.8 = (f32[576,128]{1,0:T(8,128)S(1)}, f32[576,128]{1,0:T(8,128)S(1)}, u32[]{:S(2)}, u32[]{:S(2)}) collective-permute-start(f32[576,128]{1,0:T(8,128)S(1)} %get-tuple-element.24), channel_id=1, source_target_pairs={{0,3},{1,0},{2,1},{3,2},{4,7},{5,4},{6,5},{7,6},{8,11},{9,8},{10,9... | collective-permute-start | bytes 884744 | tf_op jit(solution)/shard_map/ppermute | solution.py:403
  28.9 5.1 %collective-permute-start.9 = (f32[544,128]{1,0:T(8,128)S(1)}, f32[544,128]{1,0:T(8,128)S(1)}, u32[]{:S(2)}, u32[]{:S(2)}) collective-permute-start(f32[544,128]{1,0:T(8,128)S(1)} %get-tuple-element.25), channel_id=1, source_target_pairs={{0,1},{1,2},{2,3},{3,0},{4,5},{5,6},{6,7},{7,4},{8,9},{9,10},{10,1... | collective-permute-start | bytes 835592 | tf_op jit(solution)/shard_map/ppermute | solution.py:412
  29.4 9.2 %copy-start.1 = (f32[1,3,8,16,512]{4,3,2,1,0:T(8,128)S(1)}, f32[1,3,8,16,512]{4,3,2,1,0:T(8,128)}, u32[]{:S(2)}) copy-start(f32[1,3,8,16,512]{4,3,2,1,0:T(8,128)} %param.4) | copy-start | bytes 2359300
  29.4 9.2 %collective-permute-start.10 = (f32[544,128]{1,0:T(8,128)S(1)}, f32[544,128]{1,0:T(8,128)S(1)}, u32[]{:S(2)}, u32[]{:S(2)}) collective-permute-start(f32[544,128]{1,0:T(8,128)S(1)} %get-tuple-element.26), channel_id=1, source_target_pairs={{0,3},{1,0},{2,1},{3,2},{4,7},{5,4},{6,5},{7,6},{8,11},{9,8},{10,9... | collective-permute-start | bytes 835592 | tf_op jit(solution)/shard_map/ppermute | solution.py:413

commit v3 on v2

v3 whole, which is shorter than its diff:
```python
import functools

import jax
import jax.numpy as jnp
from jax import lax
from jax.experimental import pallas as pl
from jax.experimental.pallas import tpu as pltpu
from jax.sharding import PartitionSpec as P

FW = 128
LANES = 128
HALO = 6
RING = HALO - 2
GROUP = 16

smag_coef = 0.1024
drag_coef = 0.665
time_step = 0.2
LISTED = 4


def corner_rows():
    offset, table = 0, []
    for distance in range(1, HALO):
        table.append((distance, HALO - distance, offset))
        offset += HALO - distance
    return table, offset


def whole_vmem(count):
    return [pl.BlockSpec(memory_space=pltpu.VMEM)] * count


def call(kernel, outs, ins, smem, limit, cost, scratch=()):
    specs = [
        pl.BlockSpec(memory_space=pltpu.SMEM if i < smem else pltpu.VMEM) for i in range(len(ins))
    ]
    return pl.pallas_call(
        kernel,
        out_shape=[jax.ShapeDtypeStruct(shape, jnp.float32) for shape in outs],
        in_specs=specs,
        out_specs=whole_vmem(len(outs)),
        scratch_shapes=list(scratch),
        compiler_params=pltpu.CompilerParams(vmem_limit_bytes=limit * 1024 * 1024),
        cost_estimate=pl.CostEstimate(flops=cost, bytes_accessed=cost, transcendentals=0),
    )(*ins)


def place(start, columns):
    origin = lax.rem(start + columns - HALO, columns)
    return origin // LANES, lax.rem(origin, LANES)


def parity(body):
    even = lax.rem(lax.axis_index("gz"), 2) == 0
    pl.when(even)(functools.partial(body, True))
    pl.when(jnp.logical_not(even))(functools.partial(body, False))


def pack_own(dims, start, live, cells, u, fringe, up, down, first, second):
    tiles, depth, width = dims
    tile0, lane0 = place(start[0], tiles * LANES)
    lane = lax.broadcasted_iota(jnp.int32, (width, LANES), 1)
    offset = lax.rem(lane - lane0 + LANES, LANES)
    picked = [
        pl.ds(pl.multiple_of(lax.rem(tile0 + k, tiles) * LANES, LANES), LANES) for k in range(3)
    ]
    slot = lax.broadcasted_iota(jnp.int32, (1, LANES), 1)
    half = depth // 2
    for zz in range(half):
        packed = None
        for c in range(3):
            for part in range(2):
                z = zz + part * half
                rows = [u[c, z, :, p] for p in picked]
                at = (c * depth + z) * width
                fringe[pl.ds(at, width), :] = jnp.where(lane >= lane0, rows[0], rows[1])
                last = jnp.where(lane >= lane0, rows[1], rows[2])
                group = GROUP * (c * 2 + part)
                if packed is None:
                    packed = last
                else:
                    packed = jnp.where(offset >= group, pltpu.roll(last, group, 1), packed)
        fringe[pl.ds((3 * depth + zz) * width, width), :] = packed
    for c in range(3):
        for t in range(tiles):
            cols = pl.ds(t * LANES, LANES)
            for z in range(depth):
                at = ((c * tiles + t) * depth + z) * HALO
                up[pl.ds(at, HALO), :] = u[c, z, width - HALO :, cols]
                down[pl.ds(at, HALO), :] = u[c, z, :HALO, cols]
    for k in range(LISTED):
        row = cells[0, :, pl.ds(k * LANES, LANES)]
        row = jnp.where(slot + k * LANES < live[0, 0], row, -1).astype(jnp.float32)
        for out in (first, second):
            out[pl.ds(3 * tiles * HALO * width + k, 1), :] = row

    def levels(even):
        above, below = (first, second) if even else (second, first)
        for c in range(3):
            for t in range(tiles):
                cols = pl.ds(t * LANES, LANES)
                for h in range(HALO):
                    at = ((c * tiles + t) * HALO + h) * width
                    above[pl.ds(at, width), :] = u[c, depth - HALO + h, :, cols]
                    below[pl.ds(at, width), :] = u[c, h, :, cols]

    parity(levels)


def pack_window(dims, own, near, far, fringe, fup, fdown, first, second):
    tiles, depth, width = dims
    half = depth // 2
    listed, list_at = 3 * tiles * HALO * width, (3 * depth + half) * HALO
    for k, source in enumerate((near, own, far)):
        for out in (fup, fdown):
            out[pl.ds(list_at + k * LISTED, LISTED), :] = source[pl.ds(listed, LISTED), :]
    for at in range(3 * depth + half):
        fup[pl.ds(at * HALO, HALO), :] = fringe[pl.ds(at * width + width - HALO, HALO), :]
        fdown[pl.ds(at * HALO, HALO), :] = fringe[pl.ds(at * width, HALO), :]
    for out in (first, second):
        for zz in range(half):
            out[pl.ds((3 * HALO + zz) * width, width), :] = fringe[
                pl.ds((3 * depth + zz) * width, width), :
            ]

    def levels(even):
        above, below = (first, second) if even else (second, first)
        for c in range(3):
            for h in range(HALO):
                at = pl.ds((c * HALO + h) * width, width)
                above[at, :] = fringe[pl.ds((c * depth + depth - HALO + h) * width, width), :]
                below[at, :] = fringe[pl.ds((c * depth + h) * width, width), :]

    parity(levels)


def pack_corners(dims, left, right, fleft, fright, fnear, ffar, first, second):
    tiles, depth, _ = dims
    table, total = corner_rows()
    half = depth // 2
    tail = 3 * (tiles + 1) * 2 * total
    for out in (first, second):
        for side, source in enumerate((fleft, fright)):
            out[pl.ds(tail + side * half * HALO, half * HALO), :] = source[
                pl.ds(3 * depth * HALO, half * HALO), :
            ]

    def corners(even):
        above, below = (first, second) if even else (second, first)
        for c in range(3):
            for t in range(tiles + 1):
                for side in range(2):
                    for distance, rows, offset in table:
                        if t < tiles:
                            at = (c * tiles + t) * 2 + side
                            source, row = (left, right)[side], (c * tiles + t) * depth
                        else:
                            at = (3 * tiles + c) * 2 + side
                            source, row = (fleft, fright)[side], c * depth
                        skip = HALO - rows if side == 0 else 0
                        for out, z in ((above, depth - distance), (below, distance - 1)):
                            out[pl.ds(at * total + offset, rows), :] = source[
                                pl.ds((row + z) * HALO + skip, rows), :
                            ]

    parity(corners)


def multiplicity(dims, own, near, far, fleft, fright, out):
    tiles, depth, width = dims
    rows, levels, columns = width + 2 * RING, depth + 2 * RING, tiles * LANES
    place_z, count_z = lax.axis_index("gz"), lax.axis_size("gz")
    step = 1 - 2 * lax.rem(place_z, 2)
    row_iota = lax.broadcasted_iota(jnp.int32, (levels * rows, LANES), 0)
    col_iota = lax.broadcasted_iota(jnp.int32, (columns, LANES), 0)
    level_at, window_at = 3 * tiles * HALO * width, (3 * depth + depth // 2) * HALO
    total = jnp.zeros((levels * rows, columns), jnp.float32)
    for index in range(9):
        which, oy = index // 3, index % 3 - 1
        oz = (step, 0, -step)[which]
        if oy == 0:
            source, at = (near, own, far)[which], level_at
        else:
            source, at = (fleft, None, fright)[oy + 1], window_at + which * LISTED
        one, two = [], []
        for k in range(LISTED):
            cell = source[pl.ds(at + k, 1), :].astype(jnp.int32)
            x = cell % columns
            y = cell // columns % width + oy * width + RING
            z = cell // (columns * width) + oz * depth + RING
            fits = (cell >= 0) & (y >= 0) & (y < rows) & (z >= 0) & (z < levels)
            row = jnp.where(fits, z * rows + y % 3 * 8 + y // 3, -1)
            if which != 1:
                other = place_z + oz
                row = jnp.where((other >= 0) & (other < count_z), row, -1)
            one.append((row_iota == row).astype(jnp.float32).astype(jnp.bfloat16))
            two.append((col_iota == x).astype(jnp.float32).astype(jnp.bfloat16))
        total = total + lax.dot_general(
            jnp.concatenate(one, 1),
            jnp.concatenate(two, 1),
            (((1,), (1,)), ((), ())),
            preferred_element_type=jnp.float32,
        )
    for t in range(tiles):
        out[t] = total[:, t * LANES : (t + 1) * LANES].reshape(levels, rows, LANES)


def xdiff(value, first, last, nleft, nright):
    ahead = pltpu.roll(value, LANES - 1, 2)
    behind = pltpu.roll(value, 1, 2)
    parts = []
    for i in range(value.shape[0]):
        right = jnp.where(last, ahead[nright[i]], ahead[i])
        left = jnp.where(first, behind[nleft[i]], behind[i])
        parts.append(right - left)
    return jnp.stack(parts)


def rows_of(k):
    return pl.ds(8 * k, 8)


def ydiff(ring, count):
    row = lax.broadcasted_iota(jnp.int32, (8, LANES), 0)
    n = len(ring)
    if n == count == 3:
        return [
            ring[1] - pltpu.roll(ring[2], 1, 1),
            ring[2] - ring[0],
            pltpu.roll(ring[0], 7, 1) - ring[1],
        ]
    edge = ring[3]
    parts = [
        ring[1] - pltpu.roll(jnp.where(row == 7, edge, ring[2]), 1, 1),
        ring[2] - ring[0],
        pltpu.roll(jnp.where(row == 0, edge, ring[0]), 7, 1) - ring[1],
    ]
    if count == 4:
        parts.append(
            pltpu.roll(jnp.where(row == 0, ring[0], edge), 7, 1)
            - pltpu.roll(jnp.where(row == 7, ring[2], edge), 1, 1)
        )
    return parts


TAU = ((0, 3, 4), (3, 1, 5), (4, 5, 2))


def tau_level(src, tau, part, z, inner, ring, count, span, seam, inside, outermost):
    first, last, nleft, nright = seam
    u = [[src[c, span, z, rows_of(k), :] for k in range(ring)] for c in range(3)]
    dy = [ydiff(v, count) for v in u]
    for k in range(count):
        here = rows_of(k)
        gx = [xdiff(u[c][k], first, last, nleft, nright) for c in range(3)]
        gy = [dy[c][k] for c in range(3)]
        gz = [src[c, span, z + 1, here, :] - src[c, span, z - 1, here, :] for c in range(3)]
        xy = gx[1] + gy[0]
        xz = gx[2] + gz[0]
        yz = gy[2] + gz[1]
        diag = gx[0] * gx[0] + gy[1] * gy[1] + gz[2] * gz[2]
        off = xy * xy + xz * xz + yz * yz
        visc = jnp.sqrt(0.5 * diag + 0.25 * off)
        if inside is not None:
            visc = visc * inside
        half = visc * 0.5
        parts = ((visc, gx[0]), (visc, gy[1]), (visc, gz[2]), (half, xy), (half, xz), (half, yz))
        edge = k == inner
        for i, (scale, rate) in enumerate(parts):
            if (outermost and i not in TAU[2]) or (edge and i not in TAU[1]):
                continue
            tau[i, span, z, here, :] = scale * rate
        if outermost or edge:
            continue
        scaled = [u[c][k] * (-0.5 * time_step) for c in range(3)]
        for c in range(3):
            part[c, span, z, here, :] = u[c][k] + (
                scaled[0] * gx[c] + scaled[1] * gy[c] + scaled[2] * gz[c]
            )


def out_level(base, tau, part, z, ring, count, span, seam, weights):
    first, last, nleft, nright = seam
    keep, take = weights
    results = [[] for _ in range(count)]
    for c in range(3):
        dy = ydiff([tau[TAU[c][1], span, z, rows_of(k), :] for k in range(ring)], count)
        for k in range(count):
            here = rows_of(k)
            div = xdiff(tau[TAU[c][0], span, z, here, :], first, last, nleft, nright) + dy[k]
            div = div + (
                tau[TAU[c][2], span, z + 1, here, :] - tau[TAU[c][2], span, z - 1, here, :]
            )
            value = part[c, span, z, here, :] * take + div * (take * time_step * 0.5 * smag_coef)
            if keep:
                value = value + keep * base[c, span, z, here, :]
            results[k].append(value)
    return results


def assemble(dims, u, left, right, fringe, fleft, fright, near, far, fnear, ffar, cnear, cfar, u0):
    tiles, depth, width = dims
    table, total = corner_rows()
    half, rows = depth // 2, width + 2 * RING
    own = pl.ds(RING, width)

    def side_rows(dst, side, value):
        n = value.shape[0]
        if side == 1:
            dst[pl.ds(RING + width, n), :] = value
        else:
            keep = min(n, RING)
            dst[pl.ds(RING - keep, keep), :] = value[n - keep :]
            if n > RING:
                dst[pl.ds(rows + 8 - (n - RING), n - RING), :] = value[: n - RING]

    def unpacked(source, at, n, group):
        value = source[pl.ds(at, n), :]
        return pltpu.roll(value, LANES - GROUP * group, 1) if group else value

    for c in range(3):
        for z in range(depth):
            for t in range(tiles):
                dst = u0.at[c, t, z + HALO]
                dst[own, :] = u[c, z, :, pl.ds(t * LANES, LANES)]
                at = pl.ds(((c * tiles + t) * depth + z) * HALO, HALO)
                side_rows(dst, 0, left[at, :])
                side_rows(dst, 1, right[at, :])
            dst = u0.at[c, tiles, z + HALO]
            at = c * depth + z
            dst[own, :] = fringe[pl.ds(at * width, width), :]
            side_rows(dst, 0, fleft[pl.ds(at * HALO, HALO), :])
            side_rows(dst, 1, fright[pl.ds(at * HALO, HALO), :])
            dst = u0.at[c, tiles + 1, z + HALO]
            group, at = c * 2 + z // half, 3 * depth + z % half
            dst[own, :] = unpacked(fringe, at * width, width, group)
            side_rows(dst, 0, unpacked(fleft, at * HALO, HALO, group))
            side_rows(dst, 1, unpacked(fright, at * HALO, HALO, group))

    def vertical(even):
        for over, levels, window, corners in (
            (even, near, fnear, cnear),
            (not even, far, ffar, cfar),
        ):
            for c in range(3):
                for h in range(HALO):
                    z = HALO + depth + h if over else h
                    for t in range(tiles):
                        at = ((c * tiles + t) * HALO + h) * width
                        u0[c, t, z, own, :] = levels[pl.ds(at, width), :]
                    u0[c, tiles, z, own, :] = window[pl.ds((c * HALO + h) * width, width), :]
                    level = h if over else depth - HALO + h
                    at = (3 * HALO + level % half) * width
                    u0[c, tiles + 1, z, own, :] = unpacked(window, at, width, c * 2 + level // half)
                for distance, n, offset in table:
                    z = HALO + depth + distance - 1 if over else HALO - distance
                    for side in range(2):
                        for t in range(tiles + 1):
                            at = (c * tiles + t) if t < tiles else 3 * tiles + c
                            at = (at * 2 + side) * total + offset
                            side_rows(u0.at[c, t, z], side, corners[pl.ds(at, n), :])
                        level = distance - 1 if over else depth - distance
                        at = 3 * (tiles + 1) * 2 * total + (side * half + level % half) * HALO
                        at = at + (HALO - n if side == 0 else 0)
                        value = unpacked(corners, at, n, c * 2 + level // half)
                        side_rows(u0.at[c, tiles + 1, z], side, value)

    parity(vertical)


def step_kernel(
    dims, first_column, u, left, right, fringe, fleft, fright, near, far, fnear, ffar,
    cnear, cfar, count, out, u0, u1, u2, tau, part,
):
    tiles, depth, width = dims
    start = first_column[0]
    _, lane0 = place(start, tiles * LANES)
    main = lax.axis_index("box")
    bottom = (lax.axis_index("gz") == 0).astype(jnp.int32)
    top = (lax.axis_index("gz") == lax.axis_size("gz") - 1).astype(jnp.int32)
    assemble(dims, u, left, right, fringe, fleft, fright, near, far, fnear, ffar, cnear, cfar, u0)

    def clear(z):
        for c in range(3):
            u0[c, :, z] = jnp.zeros(u0.shape[1:2] + u0.shape[3:], jnp.float32)

    @pl.when(bottom == 1)
    def _():
        lax.fori_loop(0, HALO, lambda i, _: clear(i), None)

    @pl.when(top == 1)
    def _():
        lax.fori_loop(0, HALO, lambda i, _: clear(HALO + depth + i), None)

    def interleave(z, carry):
        for c in range(3):
            for t in range(tiles + 2):
                values = [u0[c, t, z, pl.ds(k, 8, stride=3), :] for k in range(3)]
                for k in range(3):
                    u0[c, t, z, rows_of(k), :] = values[k]
        return carry

    lax.fori_loop(0, depth + 2 * HALO, interleave, 0)

    lane = lax.broadcasted_iota(jnp.int32, (8, LANES), 1)
    order = list(range(tiles))
    main_seam = (lane == 0, lane == LANES - 1, order[-1:] + order[:-1], order[1:] + order[:1])
    window_seam = (lane == lane0, lane == lax.rem(lane0 + LANES - 1, LANES), [1, 0], [1, 0])
    main_span, window_span = slice(0, tiles), slice(tiles, tiles + 2)
    inner = (width + 2 * RING) // 8

    def inside_of(z):
        if HALO <= z < HALO + depth:
            return None
        return 1.0 - (bottom if z < HALO else top).astype(jnp.float32)

    def outside(z):
        return max(HALO - z, z - (HALO + depth - 1), 0)

    def stage(src, dst, margin, weights, span, seam, blended):
        low, high = HALO - margin, HALO + depth + margin
        for z in range(low, high):
            reach = margin - outside(z)
            ring = inner + 1 if reach > RING - 1 else inner
            tiles_here = inner + 1 if reach > RING else inner
            tau_level(
                src, tau, part, z, inner, ring, tiles_here, span, seam, inside_of(z), reach == 0
            )
            if z > low + 1:
                new_level(src, dst, margin - 1, weights, span, seam, blended, z - 1)

    def new_level(src, dst, margin, weights, span, seam, blended, z):
        if True:
            ring = inner + 1 if margin - outside(z) >= RING else inner
            level = out_level(u0, tau, part, z, ring, inner, span, seam, weights)
            for k in range(inner):
                here = rows_of(k)
                values = level[k]
                if blended:
                    ux = src[0, span, z, here, :]
                    times = count[:, z - HALO + RING, here, :]
                    factor = jnp.where(main == 1, -drag_coef * time_step * weights[1], 0.0)
                    values[0] = values[0] + (times * factor) * (ux * jnp.abs(ux))
                for c in range(3):
                    value = values[c]
                    if blended:
                        near_part = dst[c, tiles, z, here, :]
                        far_part = dst[c, tiles + 1, z, here, :]
                        parts = []
                        for t in range(tiles):
                            col = lane + t * LANES
                            mask = (col >= start) & (col < start + FW) & (main == 1)
                            other = jnp.where(col < start + LANES - HALO, near_part, far_part)
                            parts.append(jnp.where(mask, 0.5 * (value[t] + other), value[t]))
                        value = jnp.stack(parts)
                    if inside_of(z) is not None:
                        value = value * inside_of(z)
                    dst[c, span, z, here, :] = value

    stages = (
        (u0, u1, HALO - 1, (0.0, 1.0)),
        (u1, u2, HALO - 3, (0.75, 0.25)),
        (u2, u1, HALO - 5, (1.0 / 3.0, 2.0 / 3.0)),
    )
    for src, dst, margin, weights in stages:

        @pl.when(main == 1)
        def _():
            stage(src, dst, margin, weights, window_span, window_seam, False)

        stage(src, dst, margin, weights, main_span, main_seam, True)
    for c in range(3):
        for t in range(tiles):
            for z in range(HALO, HALO + depth):
                for k in range(3):
                    u2[c, t, z, pl.ds(k, 8, stride=3), :] = u1[c, t, z, rows_of(k), :]
                out[c, z - HALO, :, pl.ds(t * LANES, LANES)] = u2[c, t, z, pl.ds(RING, width), :]


def around(axis, by):
    count = lax.axis_size(axis)
    return [(i, (i + by) % count) for i in range(count)]


def swaps(axis, phase):
    count = lax.axis_size(axis)
    partners = [i + 1 if i % 2 == phase else i - 1 for i in range(count)]
    return [(i, p if 0 <= p < count else i) for i, p in enumerate(partners)]


def per_device(velocity, turbine_cells, turbine_count, fringe_start):
    u = velocity[0]
    _, depth, width, columns = u.shape
    tiles = columns // LANES
    dims = (tiles, depth, width)
    half = depth // 2

    def shapes(*rows):
        return [((r + 7) // 8 * 8, LANES) for r in rows]

    window = (3 * depth + half) * width
    halo = 3 * tiles * depth * HALO
    level = 3 * tiles * HALO * width + LISTED
    window_halo = (3 * depth + half) * HALO + 3 * LISTED
    window_level = (3 * HALO + half) * width
    corner = 3 * (tiles + 1) * 2 * corner_rows()[1] + 2 * half * HALO

    fringe, up, down, first, second = call(
        functools.partial(pack_own, dims),
        shapes(window, halo, halo, level, level),
        (fringe_start, turbine_count, turbine_cells, u),
        2,
        12,
        1,
    )
    fringe = lax.ppermute(fringe, "box", [(0, 1), (1, 0)])
    left = lax.ppermute(up, "gy", around("gy", 1))
    right = lax.ppermute(down, "gy", around("gy", -1))
    near = lax.ppermute(first, "gz", swaps("gz", 0))
    far = lax.ppermute(second, "gz", swaps("gz", 1))
    fup, fdown, ffirst, fsecond = call(
        functools.partial(pack_window, dims),
        shapes(window_halo, window_halo, window_level, window_level),
        (first, near, far, fringe),
        0,
        12,
        1,
    )
    fleft = lax.ppermute(fup, "gy", around("gy", 1))
    fright = lax.ppermute(fdown, "gy", around("gy", -1))
    fnear = lax.ppermute(ffirst, "gz", swaps("gz", 0))
    ffar = lax.ppermute(fsecond, "gz", swaps("gz", 1))
    cfirst, csecond = call(
        functools.partial(pack_corners, dims),
        shapes(corner, corner),
        (left, right, fleft, fright, fnear, ffar),
        0,
        10,
        1,
    )
    cfar = lax.ppermute(csecond, "gz", swaps("gz", 1))
    cnear = lax.ppermute(cfirst, "gz", swaps("gz", 0))

    (count,) = call(
        functools.partial(multiplicity, dims),
        [(tiles, depth + 2 * RING, width + 2 * RING, LANES)],
        (first, near, far, fleft, fright),
        0,
        12,
        8_000_000,
    )
    ext = (tiles + 2, depth + 2 * HALO, width + 2 * RING + 8, LANES)
    (out,) = call(
        functools.partial(step_kernel, dims),
        [u.shape],
        (fringe_start, u, left, right, fringe, fleft, fright, near, far, fnear, ffar, cnear, cfar, count),
        1,
        48,
        8_000_000,
        [pltpu.VMEM((n,) + ext, jnp.float32) for n in (3, 3, 3, 6, 3)],
    )
    return out[None]


def solution(mesh):
    placed = (P("box", None, "gz", "gy", None), P("gz", "gy", None), P("gz", "gy"), P())
    return jax.shard_map(
        per_device,
        mesh=mesh,
        in_specs=placed,
        out_specs=P("box", None, "gz", "gy", None),
        check_vma=False,
    )
```

time: 56.2 us -> 51.1 us (0.909)
  the two profiles are of different devices: /device:TPU:7 before, /device:TPU:5 now
where the time goes in v3:
time: 51.1 us; the launch traced here: 50.9 us
  starting transfers between devices  17.9 us (35%)
  Pallas kernels  17.5 us (34%)
  waiting for transfers between devices  12.9 us (25%)
  between operations  1.4 us (3%)
  local copies, waits for them, and re-layouts  1.15 us (2%)
    pallas_call x5, Pallas kernels, call(): pl.pallas_call(kernel, out_shape=[jax.ShapeDtypeStruct(shape, jnp.float32...  17.5 us
    ppermute x1, waiting for transfers between devices, per_device(): cfar = lax.ppermute(csecond, 'gz', swaps('gz', 1))  3.66 us
    ppermute x1, starting transfers between devices, per_device(): far = lax.ppermute(second, 'gz', swaps('gz', 1))  3.64 us
    ppermute x1, waiting for transfers between devices, per_device(): fringe = lax.ppermute(fringe, 'box', [(0, 1), (1, 0)])  3.19 us
    ppermute x1, starting transfers between devices, per_device(): ffar = lax.ppermute(fsecond, 'gz', swaps('gz', 1))  3.08 us
    ppermute x1, starting transfers between devices, per_device(): fright = lax.ppermute(fdown, 'gy', around('gy', -1))  2.1 us
    ppermute x1, starting transfers between devices, per_device(): cfar = lax.ppermute(csecond, 'gz', swaps('gz', 1))  2.04 us
    ppermute x1, starting transfers between devices, per_device(): right = lax.ppermute(down, 'gy', around('gy', -1))  2.03 us
  transfers between devices with their start and end apart: 11, of which 6 were waited for; matrix products, arithmetic and copies ran while one was open for 0% of the time, Pallas kernels for 4%

profile of v3, /device:TPU:5, one launch (start us, length us, event | category | flops | bytes accessed | tf_op | source)
XLA Modules:
  0.0 50.9 jit_solution(17615131238840017702)
XLA Ops:
  0.7 0.0 copy-start.2
  1.3 0.0 copy-done.2
  1.3 0.0 copy-start
  1.3 1.1 %copy-done = f32[1,3,8,16,512]{4,3,2,1,0:T(8,128)S(1)} copy-done((f32[1,3,8,16,512]{4,3,2,1,0:T(8,128)S(1)}, f32[1,3,8,16,512]{4,3,2,1,0:T(8,128)}, u32[]{:S(2)}) %copy-start) | copy-done | bytes 786456
  2.5 0.3 shard_map.46
  2.8 3.6 %collective-permute-start.4 = (f32[1160,128]{1,0:T(8,128)S(1)}, f32[1160,128]{1,0:T(8,128)S(1)}, u32[]{:S(2)}, u32[]{:S(2)}) collective-permute-start(f32[1160,128]{1,0:T(8,128)S(1)} %get-tuple-element.20), channel_id=1, source_target_pairs={{0,0},{1,2},{2,1},{3,3},{4,4},{5,6},{6,5},{7,7},{8,8},{9,10},{10,9... | collective-permute-start | bytes 1781768 | tf_op jit(solution)/shard_map/ppermute | solution.py:521
  6.4 0.1 collective-permute-start.3
  6.5 0.3 collective-permute-start.2
  6.8 1.3 %collective-permute-start = (f32[576,128]{1,0:T(8,128)S(1)}, f32[576,128]{1,0:T(8,128)S(1)}, u32[]{:S(2)}, u32[]{:S(2)}) collective-permute-start(f32[576,128]{1,0:T(8,128)S(1)} %get-tuple-element.16), channel_id=1, source_target_pairs={{0,4},{4,8},{8,12},{12,0},{1,5},{5,9},{9,13},{13,1},{2,6},{6,10},{... | collective-permute-start | bytes 884744 | tf_op jit(solution)/shard_map/ppermute | solution.py:518
  8.1 2.0 %collective-permute-start.1 = (f32[576,128]{1,0:T(8,128)S(1)}, f32[576,128]{1,0:T(8,128)S(1)}, u32[]{:S(2)}, u32[]{:S(2)}) collective-permute-start(f32[576,128]{1,0:T(8,128)S(1)} %get-tuple-element.17), channel_id=1, source_target_pairs={{0,12},{4,0},{8,4},{12,8},{1,13},{5,1},{9,5},{13,9},{2,14},{6,2},{... | collective-permute-start | bytes 884744 | tf_op jit(solution)/shard_map/ppermute | solution.py:519
  10.1 3.2 %collective-permute-done.2.fringe = f32[448,128]{1,0:T(8,128)S(1)} collective-permute-done((f32[448,128]{1,0:T(8,128)S(1)}, f32[448,128]{1,0:T(8,128)S(1)}, u32[]{:S(2)}, u32[]{:S(2)}) %collective-permute-start.2) | collective-permute-done | bytes 229408 | tf_op jit(solution)/shard_map/ppermute | solution.py:517
  13.3 1.0 %collective-permute-done.4.far = f32[1160,128]{1,0:T(8,128)S(1)} collective-permute-done((f32[1160,128]{1,0:T(8,128)S(1)}, f32[1160,128]{1,0:T(8,128)S(1)}, u32[]{:S(2)}, u32[]{:S(2)}) %collective-permute-start.4) | collective-permute-done | bytes 593952 | tf_op jit(solution)/shard_map/ppermute | solution.py:521
  14.3 0.0 collective-permute-done.3.near
  14.3 0.1 shard_map.47
  14.4 0.3 collective-permute-start.7
  14.7 3.1 %collective-permute-start.8 = (f32[352,128]{1,0:T(8,128)S(1)}, f32[352,128]{1,0:T(8,128)S(1)}, u32[]{:S(2)}, u32[]{:S(2)}) collective-permute-start(f32[352,128]{1,0:T(8,128)S(1)} %get-tuple-element.24), channel_id=1, source_target_pairs={{0,0},{1,2},{2,1},{3,3},{4,4},{5,6},{6,5},{7,7},{8,8},{9,10},{10,9... | collective-permute-start | bytes 540680 | tf_op jit(solution)/shard_map/ppermute | solution.py:533
  17.8 1.3 %collective-permute-start.5 = (f32[184,128]{1,0:T(8,128)S(1)}, f32[184,128]{1,0:T(8,128)S(1)}, u32[]{:S(2)}, u32[]{:S(2)}) collective-permute-start(f32[184,128]{1,0:T(8,128)S(1)} %get-tuple-element.21), channel_id=1, source_target_pairs={{0,4},{4,8},{8,12},{12,0},{1,5},{5,9},{9,13},{13,1},{2,6},{6,10},{... | collective-permute-start | bytes 282632 | tf_op jit(solution)/shard_map/ppermute | solution.py:530
  19.2 0.0 collective-permute-done.left
  19.2 2.1 %collective-permute-start.6 = (f32[184,128]{1,0:T(8,128)S(1)}, f32[184,128]{1,0:T(8,128)S(1)}, u32[]{:S(2)}, u32[]{:S(2)}) collective-permute-start(f32[184,128]{1,0:T(8,128)S(1)} %get-tuple-element.22), channel_id=1, source_target_pairs={{0,12},{4,0},{8,4},{12,8},{1,13},{5,1},{9,5},{13,9},{2,14},{6,2},{... | collective-permute-start | bytes 282632 | tf_op jit(solution)/shard_map/ppermute | solution.py:531
  21.3 1.5 %collective-permute-done.1.right = f32[576,128]{1,0:T(8,128)S(1)} collective-permute-done((f32[576,128]{1,0:T(8,128)S(1)}, f32[576,128]{1,0:T(8,128)S(1)}, u32[]{:S(2)}, u32[]{:S(2)}) %collective-permute-start.1) | collective-permute-done | bytes 294944 | tf_op jit(solution)/shard_map/ppermute | solution.py:519
  22.7 1.9 %collective-permute-done.5.fleft = f32[184,128]{1,0:T(8,128)S(1)} collective-permute-done((f32[184,128]{1,0:T(8,128)S(1)}, f32[184,128]{1,0:T(8,128)S(1)}, u32[]{:S(2)}, u32[]{:S(2)}) %collective-permute-start.5) | collective-permute-done | bytes 94240 | tf_op jit(solution)/shard_map/ppermute | solution.py:530
  24.6 1.7 %collective-permute-done.6.fright = f32[184,128]{1,0:T(8,128)S(1)} collective-permute-done((f32[184,128]{1,0:T(8,128)S(1)}, f32[184,128]{1,0:T(8,128)S(1)}, u32[]{:S(2)}, u32[]{:S(2)}) %collective-permute-start.6) | collective-permute-done | bytes 94240 | tf_op jit(solution)/shard_map/ppermute | solution.py:531
  26.3 0.0 collective-permute-done.7.fnear
  26.3 0.0 collective-permute-done.8.ffar
  26.3 0.1 shard_map.48
  26.4 1.6 %collective-permute-start.9 = (f32[504,128]{1,0:T(8,128)S(1)}, f32[504,128]{1,0:T(8,128)S(1)}, u32[]{:S(2)}, u32[]{:S(2)}) collective-permute-start(f32[504,128]{1,0:T(8,128)S(1)} %get-tuple-element.25), channel_id=1, source_target_pairs={{0,1},{1,0},{2,3},{3,2},{4,5},{5,4},{6,7},{7,6},{8,9},{9,8},{10,11... | collective-permute-start | bytes 774152 | tf_op jit(solution)/shard_map/ppermute | solution.py:543
  28.1 0.0 copy-start.1
  28.1 2.0 %collective-permute-start.10 = (f32[504,128]{1,0:T(8,128)S(1)}, f32[504,128]{1,0:T(8,128)S(1)}, u32[]{:S(2)}, u32[]{:S(2)}) collective-permute-start(f32[504,128]{1,0:T(8,128)S(1)} %get-tuple-element.26), channel_id=1, source_target_pairs={{0,0},{1,2},{2,1},{3,3},{4,4},{5,6},{6,5},{7,7},{8,8},{9,10},{10,9... | collective-permute-start | bytes 774152 | tf_op jit(solution)/shard_map/ppermute | solution.py:542
  30.1 2.0 %shard_map.49.count = f32[4,16,24,128]{3,2,1,0:T(8,128)S(1)} custom-call(f32[1160,128]{1,0:T(8,128)S(1)} %get-tuple-element.19.own, f32[1160,128]{1,0:T(8,128)S(1)} %collective-permute-done.3.near, f32[1160,128]{1,0:T(8,128)S(1)} %collective-permute-done.4.far, f32[184,128]{1,0:T(8,128)S(1)} %collective-permute-done.5.fleft, ...), custom_call_target="tpu_custom_call" | custom-call | flops 8000000 | bytes 8000000 | tf_op jit(solution)/shard_map/pallas_call | solution.py:38
  32.2 0.0 collective-permute-done.9.cnear
  32.2 3.7 %collective-permute-done.10.cfar = f32[504,128]{1,0:T(8,128)S(1)} collective-permute-done((f32[504,128]{1,0:T(8,128)S(1)}, f32[504,128]{1,0:T(8,128)S(1)}, u32[]{:S(2)}, u32[]{:S(2)}) %collective-permute-start.10) | collective-permute-done | bytes 258080 | tf_op jit(solution)/shard_map/ppermute | solution.py:542
  35.8 0.0 copy-done.1
  35.8 15.0 %shard_map.50 = f32[3,8,16,512]{3,2,1,0:T(8,128)} custom-call(s32[1]{0:T(128)S(6)} %copy.6.start.first_column, f32[3,8,16,512]{3,2,1,0:T(8,128)S(1)} %bitcast.3, f32[576,128]{1,0:T(8,128)S(1)} %collective-permute-done.left, f32[576,128]{1,0:T(8,128)S(1)} %collective-permute-done.1.right, f32[448,128]{1,0:T(8,128)S(1)} %collective-permute-done.2.fringe, ...), custom_call_target="tpu_custom_call" | custom-call | flops 8000000 | bytes 8000000 | tf_op jit(solution)/shard_map/pallas_call | solution.py:38
Async XLA Ops:
  0.7 0.7 %copy-start.2 = (s32[1,1,512]{2,1,0:T(1,128)S(1)}, s32[1,1,512]{2,1,0:T(1,128)}, u32[]{:S(2)}) copy-start(s32[1,1,512]{2,1,0:T(1,128)} %cells.1) | copy-start | bytes 6148
  1.3 1.1 %copy-start = (f32[1,3,8,16,512]{4,3,2,1,0:T(8,128)S(1)}, f32[1,3,8,16,512]{4,3,2,1,0:T(8,128)}, u32[]{:S(2)}) copy-start(f32[1,3,8,16,512]{4,3,2,1,0:T(8,128)} %param.4) | copy-start | bytes 2359300
  2.8 11.5 %collective-permute-start.4 = (f32[1160,128]{1,0:T(8,128)S(1)}, f32[1160,128]{1,0:T(8,128)S(1)}, u32[]{:S(2)}, u32[]{:S(2)}) collective-permute-start(f32[1160,128]{1,0:T(8,128)S(1)} %get-tuple-element.20), channel_id=1, source_target_pairs={{0,0},{1,2},{2,1},{3,3},{4,4},{5,6},{6,5},{7,7},{8,8},{9,10},{10,9... | collective-permute-start | bytes 1781768 | tf_op jit(solution)/shard_map/ppermute | solution.py:521
  6.4 7.9 %collective-permute-start.3 = (f32[1160,128]{1,0:T(8,128)S(1)}, f32[1160,128]{1,0:T(8,128)S(1)}, u32[]{:S(2)}, u32[]{:S(2)}) collective-permute-start(f32[1160,128]{1,0:T(8,128)S(1)} %get-tuple-element.19.own), channel_id=1, source_target_pairs={{0,1},{1,0},{2,3},{3,2},{4,5},{5,4},{6,7},{7,6},{8,9},{9,8},{10,11... | collective-permute-start | bytes 1781768 | tf_op jit(solution)/shard_map/ppermute | solution.py:520
  6.5 6.8 %collective-permute-start.2 = (f32[448,128]{1,0:T(8,128)S(1)}, f32[448,128]{1,0:T(8,128)S(1)}, u32[]{:S(2)}, u32[]{:S(2)}) collective-permute-start(f32[448,128]{1,0:T(8,128)S(1)} %get-tuple-element.18), channel_id=1, source_target_pairs={{0,16},{16,0},{1,17},{17,1},{2,18},{18,2},{3,19},{19,3},{4,20},{20... | collective-permute-start | bytes 688136 | tf_op jit(solution)/shard_map/ppermute | solution.py:517
  6.8 12.4 %collective-permute-start = (f32[576,128]{1,0:T(8,128)S(1)}, f32[576,128]{1,0:T(8,128)S(1)}, u32[]{:S(2)}, u32[]{:S(2)}) collective-permute-start(f32[576,128]{1,0:T(8,128)S(1)} %get-tuple-element.16), channel_id=1, source_target_pairs={{0,4},{4,8},{8,12},{12,0},{1,5},{5,9},{9,13},{13,1},{2,6},{6,10},{... | collective-permute-start | bytes 884744 | tf_op jit(solution)/shard_map/ppermute | solution.py:518
  8.1 14.6 %collective-permute-start.1 = (f32[576,128]{1,0:T(8,128)S(1)}, f32[576,128]{1,0:T(8,128)S(1)}, u32[]{:S(2)}, u32[]{:S(2)}) collective-permute-start(f32[576,128]{1,0:T(8,128)S(1)} %get-tuple-element.17), channel_id=1, source_target_pairs={{0,12},{4,0},{8,4},{12,8},{1,13},{5,1},{9,5},{13,9},{2,14},{6,2},{... | collective-permute-start | bytes 884744 | tf_op jit(solution)/shard_map/ppermute | solution.py:519
  14.4 11.9 %collective-permute-start.7 = (f32[352,128]{1,0:T(8,128)S(1)}, f32[352,128]{1,0:T(8,128)S(1)}, u32[]{:S(2)}, u32[]{:S(2)}) collective-permute-start(f32[352,128]{1,0:T(8,128)S(1)} %get-tuple-element.23), channel_id=1, source_target_pairs={{0,1},{1,0},{2,3},{3,2},{4,5},{5,4},{6,7},{7,6},{8,9},{9,8},{10,11... | collective-permute-start | bytes 540680 | tf_op jit(solution)/shard_map/ppermute | solution.py:532
  14.7 11.6 %collective-permute-start.8 = (f32[352,128]{1,0:T(8,128)S(1)}, f32[352,128]{1,0:T(8,128)S(1)}, u32[]{:S(2)}, u32[]{:S(2)}) collective-permute-start(f32[352,128]{1,0:T(8,128)S(1)} %get-tuple-element.24), channel_id=1, source_target_pairs={{0,0},{1,2},{2,1},{3,3},{4,4},{5,6},{6,5},{7,7},{8,8},{9,10},{10,9... | collective-permute-start | bytes 540680 | tf_op jit(solution)/shard_map/ppermute | solution.py:533
  17.8 6.8 %collective-permute-start.5 = (f32[184,128]{1,0:T(8,128)S(1)}, f32[184,128]{1,0:T(8,128)S(1)}, u32[]{:S(2)}, u32[]{:S(2)}) collective-permute-start(f32[184,128]{1,0:T(8,128)S(1)} %get-tuple-element.21), channel_id=1, source_target_pairs={{0,4},{4,8},{8,12},{12,0},{1,5},{5,9},{9,13},{13,1},{2,6},{6,10},{... | collective-permute-start | bytes 282632 | tf_op jit(solution)/shard_map/ppermute | solution.py:530
  19.2 7.2 %collective-permute-start.6 = (f32[184,128]{1,0:T(8,128)S(1)}, f32[184,128]{1,0:T(8,128)S(1)}, u32[]{:S(2)}, u32[]{:S(2)}) collective-permute-start(f32[184,128]{1,0:T(8,128)S(1)} %get-tuple-element.22), channel_id=1, source_target_pairs={{0,12},{4,0},{8,4},{12,8},{1,13},{5,1},{9,5},{13,9},{2,14},{6,2},{... | collective-permute-start | bytes 282632 | tf_op jit(solution)/shard_map/ppermute | solution.py:531
  26.4 5.7 %collective-permute-start.9 = (f32[504,128]{1,0:T(8,128)S(1)}, f32[504,128]{1,0:T(8,128)S(1)}, u32[]{:S(2)}, u32[]{:S(2)}) collective-permute-start(f32[504,128]{1,0:T(8,128)S(1)} %get-tuple-element.25), channel_id=1, source_target_pairs={{0,1},{1,0},{2,3},{3,2},{4,5},{5,4},{6,7},{7,6},{8,9},{9,8},{10,11... | collective-permute-start | bytes 774152 | tf_op jit(solution)/shard_map/ppermute | solution.py:543
  28.1 7.8 %copy-start.1 = (f32[1,3,8,16,512]{4,3,2,1,0:T(8,128)S(1)}, f32[1,3,8,16,512]{4,3,2,1,0:T(8,128)}, u32[]{:S(2)}) copy-start(f32[1,3,8,16,512]{4,3,2,1,0:T(8,128)} %param.4) | copy-start | bytes 2359300
  28.1 7.8 %collective-permute-start.10 = (f32[504,128]{1,0:T(8,128)S(1)}, f32[504,128]{1,0:T(8,128)S(1)}, u32[]{:S(2)}, u32[]{:S(2)}) collective-permute-start(f32[504,128]{1,0:T(8,128)S(1)} %get-tuple-element.26), channel_id=1, source_target_pairs={{0,0},{1,2},{2,1},{3,3},{4,4},{5,6},{6,5},{7,7},{8,8},{9,10},{10,9... | collective-permute-start | bytes 774152 | tf_op jit(solution)/shard_map/ppermute | solution.py:542

commit v4 on v3

--- a/solution.py
+++ b/solution.py
@@ -249,13 +249,13 @@
 
 def tau_level(src, tau, part, z, inner, ring, count, span, seam, inside, outermost):
     first, last, nleft, nright = seam
-    u = [[src[c, span, z, rows_of(k), :] for k in range(ring)] for c in range(3)]
+    u = [[src(z)[c, span, z, rows_of(k), :] for k in range(ring)] for c in range(3)]
     dy = [ydiff(v, count) for v in u]
     for k in range(count):
         here = rows_of(k)
         gx = [xdiff(u[c][k], first, last, nleft, nright) for c in range(3)]
         gy = [dy[c][k] for c in range(3)]
-        gz = [src[c, span, z + 1, here, :] - src[c, span, z - 1, here, :] for c in range(3)]
+        gz = [src(z + 1)[c, span, z + 1, here, :] - src(z - 1)[c, span, z - 1, here, :] for c in range(3)]
         xy = gx[1] + gy[0]
         xz = gx[2] + gz[0]
         yz = gy[2] + gz[1]
@@ -294,30 +294,44 @@
             )
             value = part[c, span, z, here, :] * take + div * (take * time_step * 0.5 * smag_coef)
             if keep:
-                value = value + keep * base[c, span, z, here, :]
+                value = value + keep * base(z)[c, span, z, here, :]
             results[k].append(value)
     return results
 
 
-def assemble(dims, u, left, right, fringe, fleft, fright, near, far, fnear, ffar, cnear, cfar, u0):
+def side_rows(width, dst, side, value):
+    n = value.shape[0]
+    if side == 1:
+        dst[pl.ds(RING + width, n), :] = value
+    else:
+        keep = min(n, RING)
+        dst[pl.ds(RING - keep, keep), :] = value[n - keep :]
+        if n > RING:
+            dst[pl.ds(width + 2 * RING + 8 - (n - RING), n - RING), :] = value[: n - RING]
+
+
+def unpacked(source, at, n, group):
+    value = source[pl.ds(at, n), :]
+    return pltpu.roll(value, LANES - GROUP * group, 1) if group else value
+
+
+def interleave(u0, levels):
+    def step(i, carry):
+        z = levels(i)
+        for c in range(3):
+            for t in range(u0.shape[1]):
+                values = [u0[c, t, z, pl.ds(k, 8, stride=3), :] for k in range(3)]
+                for k in range(3):
+                    u0[c, t, z, rows_of(k), :] = values[k]
+        return carry
+
+    return step
+
+
+def assemble(dims, u, left, right, fringe, fleft, fright, near, far, fnear, ffar, u0):
     tiles, depth, width = dims
-    table, total = corner_rows()
-    half, rows = depth // 2, width + 2 * RING
+    half = depth // 2
     own = pl.ds(RING, width)
-
-    def side_rows(dst, side, value):
-        n = value.shape[0]
-        if side == 1:
-            dst[pl.ds(RING + width, n), :] = value
-        else:
-            keep = min(n, RING)
-            dst[pl.ds(RING - keep, keep), :] = value[n - keep :]
-            if n > RING:
-                dst[pl.ds(rows + 8 - (n - RING), n - RING), :] = value[: n - RING]
-
-    def unpacked(source, at, n, group):
-        value = source[pl.ds(at, n), :]
-        return pltpu.roll(value, LANES - GROUP * group, 1) if group else value
 
     for c in range(3):
         for z in range(depth):
@@ -325,24 +339,21 @@
                 dst = u0.at[c, t, z + HALO]
                 dst[own, :] = u[c, z, :, pl.ds(t * LANES, LANES)]
                 at = pl.ds(((c * tiles + t) * depth + z) * HALO, HALO)
-                side_rows(dst, 0, left[at, :])
-                side_rows(dst, 1, right[at, :])
+                side_rows(width, dst, 0, left[at, :])
+                side_rows(width, dst, 1, right[at, :])
             dst = u0.at[c, tiles, z + HALO]
             at = c * depth + z
             dst[own, :] = fringe[pl.ds(at * width, width), :]
-            side_rows(dst, 0, fleft[pl.ds(at * HALO, HALO), :])
-            side_rows(dst, 1, fright[pl.ds(at * HALO, HALO), :])
+            side_rows(width, dst, 0, fleft[pl.ds(at * HALO, HALO), :])
+            side_rows(width, dst, 1, fright[pl.ds(at * HALO, HALO), :])
             dst = u0.at[c, tiles + 1, z + HALO]
             group, at = c * 2 + z // half, 3 * depth + z % half
             dst[own, :] = unpacked(fringe, at * width, width, group)
-            side_rows(dst, 0, unpacked(fleft, at * HALO, HALO, group))
-            side_rows(dst, 1, unpacked(fright, at * HALO, HALO, group))
+            side_rows(width, dst, 0, unpacked(fleft, at * HALO, HALO, group))
+            side_rows(width, dst, 1, unpacked(fright, at * HALO, HALO, group))
 
     def vertical(even):
-        for over, levels, window, corners in (
-            (even, near, fnear, cnear),
-            (not even, far, ffar, cfar),
-        ):
+        for over, levels, window in ((even, near, fnear), (not even, far, ffar)):
             for c in range(3):
                 for h in range(HALO):
                     z = HALO + depth + h if over else h
@@ -353,33 +364,53 @@
                     level = h if over else depth - HALO + h
                     at = (3 * HALO + level % half) * width
                     u0[c, tiles + 1, z, own, :] = unpacked(window, at, width, c * 2 + level // half)
+
+    parity(vertical)
+    step = interleave(u0, lambda i: jnp.where(i < depth, HALO + i, (i - depth) * (depth + 2 * HALO - 1)))
+    lax.fori_loop(0, depth + 2, step, 0)
+
+
+def corner_levels(depth):
+    return list(range(1, HALO)) + list(range(HALO + depth, 2 * HALO + depth - 1))
+
+
+def add_corners(dims, cnear, cfar, given, u0):
+    tiles, depth, width = dims
+    table, total = corner_rows()
+    half = depth // 2
+    for z in corner_levels(depth):
+        for c in range(3):
+            u0[c, :, z] = given[c, :, z]
+
+    def vertical(even):
+        for over, corners in ((even, cnear), (not even, cfar)):
+            for c in range(3):
                 for distance, n, offset in table:
                     z = HALO + depth + distance - 1 if over else HALO - distance
                     for side in range(2):
                         for t in range(tiles + 1):
                             at = (c * tiles + t) if t < tiles else 3 * tiles + c
                             at = (at * 2 + side) * total + offset
-                            side_rows(u0.at[c, t, z], side, corners[pl.ds(at, n), :])
+                            side_rows(width, u0.at[c, t, z], side, corners[pl.ds(at, n), :])
                         level = distance - 1 if over else depth - distance
                         at = 3 * (tiles + 1) * 2 * total + (side * half + level % half) * HALO
                         at = at + (HALO - n if side == 0 else 0)
                         value = unpacked(corners, at, n, c * 2 + level // half)
-                        side_rows(u0.at[c, tiles + 1, z], side, value)
+                        side_rows(width, u0.at[c, tiles + 1, z], side, value)
 
     parity(vertical)
-
-
-def step_kernel(
-    dims, first_column, u, left, right, fringe, fleft, fright, near, far, fnear, ffar,
-    cnear, cfar, count, out, u0, u1, u2, tau, part,
-):
+    step = interleave(u0, lambda i: jnp.where(i < HALO - 1, 1 + i, depth + 1 + i))
+    lax.fori_loop(0, 2 * (HALO - 1), step, 0)
+
+
+def step_kernel(dims, first_column, cfar, cnear, count, given, out, u0, u1, u2, tau, part):
     tiles, depth, width = dims
     start = first_column[0]
     _, lane0 = place(start, tiles * LANES)
     main = lax.axis_index("box")
     bottom = (lax.axis_index("gz") == 0).astype(jnp.int32)
     top = (lax.axis_index("gz") == lax.axis_size("gz") - 1).astype(jnp.int32)
-    assemble(dims, u, left, right, fringe, fleft, fright, near, far, fnear, ffar, cnear, cfar, u0)
+    add_corners(dims, cnear, cfar, given, u0)
 
     def clear(z):
         for c in range(3):
@@ -387,21 +418,11 @@
 
     @pl.when(bottom == 1)
     def _():
-        lax.fori_loop(0, HALO, lambda i, _: clear(i), None)
+        lax.fori_loop(1, HALO, lambda i, _: clear(i), None)
 
     @pl.when(top == 1)
     def _():
-        lax.fori_loop(0, HALO, lambda i, _: clear(HALO + depth + i), None)
-
-    def interleave(z, carry):
-        for c in range(3):
-            for t in range(tiles + 2):
-                values = [u0[c, t, z, pl.ds(k, 8, stride=3), :] for k in range(3)]
-                for k in range(3):
-                    u0[c, t, z, rows_of(k), :] = values[k]
-        return carry
-
-    lax.fori_loop(0, depth + 2 * HALO, interleave, 0)
+        lax.fori_loop(0, HALO - 1, lambda i, _: clear(HALO + depth + i), None)
 
     lane = lax.broadcasted_iota(jnp.int32, (8, LANES), 1)
     order = list(range(tiles))
@@ -409,6 +430,10 @@
     window_seam = (lane == lane0, lane == lax.rem(lane0 + LANES - 1, LANES), [1, 0], [1, 0])
     main_span, window_span = slice(0, tiles), slice(tiles, tiles + 2)
     inner = (width + 2 * RING) // 8
+    touched = corner_levels(depth)
+
+    def first_field(z):
+        return u0 if z in touched else given
 
     def inside_of(z):
         if HALO <= z < HALO + depth:
@@ -433,12 +458,12 @@
     def new_level(src, dst, margin, weights, span, seam, blended, z):
         if True:
             ring = inner + 1 if margin - outside(z) >= RING else inner
-            level = out_level(u0, tau, part, z, ring, inner, span, seam, weights)
+            level = out_level(first_field, tau, part, z, ring, inner, span, seam, weights)
             for k in range(inner):
                 here = rows_of(k)
                 values = level[k]
                 if blended:
-                    ux = src[0, span, z, here, :]
+                    ux = src(z)[0, span, z, here, :]
                     times = count[:, z - HALO + RING, here, :]
                     factor = jnp.where(main == 1, -drag_coef * time_step * weights[1], 0.0)
                     values[0] = values[0] + (times * factor) * (ux * jnp.abs(ux))
@@ -459,9 +484,9 @@
                     dst[c, span, z, here, :] = value
 
     stages = (
-        (u0, u1, HALO - 1, (0.0, 1.0)),
-        (u1, u2, HALO - 3, (0.75, 0.25)),
-        (u2, u1, HALO - 5, (1.0 / 3.0, 2.0 / 3.0)),
+        (first_field, u1, HALO - 1, (0.0, 1.0)),
+        (lambda z: u1, u2, HALO - 3, (0.75, 0.25)),
+        (lambda z: u2, u1, HALO - 5, (1.0 / 3.0, 2.0 / 3.0)),
     )
     for src, dst, margin, weights in stages:
 
@@ -551,12 +576,20 @@
         8_000_000,
     )
     ext = (tiles + 2, depth + 2 * HALO, width + 2 * RING + 8, LANES)
+    (given,) = call(
+        functools.partial(assemble, dims),
+        [(3,) + ext],
+        (u, left, right, fringe, fleft, fright, near, far, fnear, ffar),
+        0,
+        16,
+        8_000_000,
+    )
     (out,) = call(
         functools.partial(step_kernel, dims),
         [u.shape],
-        (fringe_start, u, left, right, fringe, fleft, fright, near, far, fnear, ffar, cnear, cfar, count),
+        (fringe_start, cfar, cnear, count, given),
         1,
-        48,
+        46,
         8_000_000,
         [pltpu.VMEM((n,) + ext, jnp.float32) for n in (3, 3, 3, 6, 3)],
     )

time: 51.1 us -> 49.8 us (0.975)
  waiting for transfers between devices: 12.9 us -> 11 us
  local copies, waits for them, and re-layouts: 1.15 us -> 1.81 us
    ppermute x1, waiting for transfers between devices: 1 us -> 2.66 us  [per_device(): far = lax.ppermute(second, 'gz', swaps('gz', 1))]
    ppermute x1, starting transfers between devices: 2.1 us -> 3.51 us  [per_device(): fright = lax.ppermute(fdown, 'gy', around('gy', -1))]
    ppermute x1, starting transfers between devices: 1.62 us -> 0.46 us  [per_device(): cnear = lax.ppermute(cfirst, 'gz', swaps('gz', 0))]
    ppermute x1, waiting for transfers between devices: 1.45 us -> 0.43 us  [per_device(): right = lax.ppermute(down, 'gy', around('gy', -1))]
    ppermute x1, waiting for transfers between devices: 3.19 us -> 2.23 us  [per_device(): fringe = lax.ppermute(fringe, 'box', [(0, 1), (1, 0)])]
    ppermute x1, waiting for transfers between devices: 3.66 us -> 2.83 us  [per_device(): cfar = lax.ppermute(csecond, 'gz', swaps('gz', 1))]
    unnamed x6, local copies, waits for them, and re-layouts: 1.15 us -> 1.81 us
    ppermute x1, starting transfers between devices: 0.07 us -> 0.7 us  [per_device(): near = lax.ppermute(first, 'gz', swaps('gz', 0))]
  transfers between devices with their start and end apart: 11 -> 11, of which waited for: 6 -> 6; matrix products, arithmetic and copies ran while one was open for 0% -> 0% of each run, Pallas kernels for 4% -> 5%
where the time goes in v4:
time: 49.8 us; the launch traced here: 49.6 us
  Pallas kernels  17.8 us (36%)
  starting transfers between devices  17.6 us (35%)
  waiting for transfers between devices  11 us (22%)
  local copies, waits for them, and re-layouts  1.81 us (4%)
  between operations  1.4 us (3%)
    pallas_call x6, Pallas kernels, call(): pl.pallas_call(kernel, out_shape=[jax.ShapeDtypeStruct(shape, jnp.float32...  17.8 us
    ppermute x1, starting transfers between devices, per_device(): fright = lax.ppermute(fdown, 'gy', around('gy', -1))  3.51 us
    ppermute x1, starting transfers between devices, per_device(): far = lax.ppermute(second, 'gz', swaps('gz', 1))  3.02 us
    ppermute x1, waiting for transfers between devices, per_device(): cfar = lax.ppermute(csecond, 'gz', swaps('gz', 1))  2.83 us
    ppermute x1, starting transfers between devices, per_device(): ffar = lax.ppermute(fsecond, 'gz', swaps('gz', 1))  2.74 us
    ppermute x1, waiting for transfers between devices, per_device(): far = lax.ppermute(second, 'gz', swaps('gz', 1))  2.66 us
    ppermute x1, waiting for transfers between devices, per_device(): fringe = lax.ppermute(fringe, 'box', [(0, 1), (1, 0)])  2.23 us
    ppermute x1, starting transfers between devices, per_device(): cfar = lax.ppermute(csecond, 'gz', swaps('gz', 1))  2.14 us
  transfers between devices with their start and end apart: 11, of which 6 were waited for; matrix products, arithmetic and copies ran while one was open for 0% of the time, Pallas kernels for 5%

profile of v4, /device:TPU:5, one launch (start us, length us, event | category | flops | bytes accessed | tf_op | source)
XLA Modules:
  0.0 49.6 jit_solution(16543144262247280494)
XLA Ops:
  1.3 0.0 copy-start
  1.3 1.1 %copy-done = f32[1,3,8,16,512]{4,3,2,1,0:T(8,128)S(1)} copy-done((f32[1,3,8,16,512]{4,3,2,1,0:T(8,128)S(1)}, f32[1,3,8,16,512]{4,3,2,1,0:T(8,128)}, u32[]{:S(2)}) %copy-start) | copy-done | bytes 786456
  2.4 0.0 copy-start.2
  2.4 0.7 %copy-done.2 = s32[1,1,512]{2,1,0:T(1,128)S(1)} copy-done((s32[1,1,512]{2,1,0:T(1,128)S(1)}, s32[1,1,512]{2,1,0:T(1,128)}, u32[]{:S(2)}) %copy-start.2) | copy-done | bytes 2072
  3.1 0.0 copy-start.1
  3.1 0.3 shard_map.46
  3.4 0.7 %collective-permute-start.2 = (f32[1160,128]{1,0:T(8,128)S(1)}, f32[1160,128]{1,0:T(8,128)S(1)}, u32[]{:S(2)}, u32[]{:S(2)}) collective-permute-start(f32[1160,128]{1,0:T(8,128)S(1)} %get-tuple-element.18.own), channel_id=1, source_target_pairs={{0,1},{1,0},{2,3},{3,2},{4,5},{5,4},{6,7},{7,6},{8,9},{9,8},{10,11... | collective-permute-start | bytes 1781768 | tf_op jit(solution)/shard_map/ppermute | solution.py:545
  4.1 3.0 %collective-permute-start.3 = (f32[1160,128]{1,0:T(8,128)S(1)}, f32[1160,128]{1,0:T(8,128)S(1)}, u32[]{:S(2)}, u32[]{:S(2)}) collective-permute-start(f32[1160,128]{1,0:T(8,128)S(1)} %get-tuple-element.19), channel_id=1, source_target_pairs={{0,0},{1,2},{2,1},{3,3},{4,4},{5,6},{6,5},{7,7},{8,8},{9,10},{10,9... | collective-permute-start | bytes 1781768 | tf_op jit(solution)/shard_map/ppermute | solution.py:546
  7.1 0.3 collective-permute-start.4
  7.4 1.3 %collective-permute-start = (f32[576,128]{1,0:T(8,128)S(1)}, f32[576,128]{1,0:T(8,128)S(1)}, u32[]{:S(2)}, u32[]{:S(2)}) collective-permute-start(f32[576,128]{1,0:T(8,128)S(1)} %get-tuple-element.16), channel_id=1, source_target_pairs={{0,4},{4,8},{8,12},{12,0},{1,5},{5,9},{9,13},{13,1},{2,6},{6,10},{... | collective-permute-start | bytes 884744 | tf_op jit(solution)/shard_map/ppermute | solution.py:543
  8.7 2.0 %collective-permute-start.1 = (f32[576,128]{1,0:T(8,128)S(1)}, f32[576,128]{1,0:T(8,128)S(1)}, u32[]{:S(2)}, u32[]{:S(2)}) collective-permute-start(f32[576,128]{1,0:T(8,128)S(1)} %get-tuple-element.17), channel_id=1, source_target_pairs={{0,12},{4,0},{8,4},{12,8},{1,13},{5,1},{9,5},{13,9},{2,14},{6,2},{... | collective-permute-start | bytes 884744 | tf_op jit(solution)/shard_map/ppermute | solution.py:544
  10.8 2.2 %collective-permute-done.4.fringe = f32[448,128]{1,0:T(8,128)S(1)} collective-permute-done((f32[448,128]{1,0:T(8,128)S(1)}, f32[448,128]{1,0:T(8,128)S(1)}, u32[]{:S(2)}, u32[]{:S(2)}) %collective-permute-start.4) | collective-permute-done | bytes 229408 | tf_op jit(solution)/shard_map/ppermute | solution.py:542
  13.0 0.0 collective-permute-done.2.near
  13.0 2.7 %collective-permute-done.3.far = f32[1160,128]{1,0:T(8,128)S(1)} collective-permute-done((f32[1160,128]{1,0:T(8,128)S(1)}, f32[1160,128]{1,0:T(8,128)S(1)}, u32[]{:S(2)}, u32[]{:S(2)}) %collective-permute-start.3) | collective-permute-done | bytes 593952 | tf_op jit(solution)/shard_map/ppermute | solution.py:546
  15.7 0.1 collective-permute-start.7
  15.8 2.7 %collective-permute-start.8 = (f32[352,128]{1,0:T(8,128)S(1)}, f32[352,128]{1,0:T(8,128)S(1)}, u32[]{:S(2)}, u32[]{:S(2)}) collective-permute-start(f32[352,128]{1,0:T(8,128)S(1)} %get-tuple-element.24), channel_id=1, source_target_pairs={{0,0},{1,2},{2,1},{3,3},{4,4},{5,6},{6,5},{7,7},{8,8},{9,10},{10,9... | collective-permute-start | bytes 540680 | tf_op jit(solution)/shard_map/ppermute | solution.py:558
  18.5 1.3 %collective-permute-start.5 = (f32[184,128]{1,0:T(8,128)S(1)}, f32[184,128]{1,0:T(8,128)S(1)}, u32[]{:S(2)}, u32[]{:S(2)}) collective-permute-start(f32[184,128]{1,0:T(8,128)S(1)} %get-tuple-element.21), channel_id=1, source_target_pairs={{0,4},{4,8},{8,12},{12,0},{1,5},{5,9},{9,13},{13,1},{2,6},{6,10},{... | collective-permute-start | bytes 282632 | tf_op jit(solution)/shard_map/ppermute | solution.py:555
  19.9 0.0 collective-permute-done.left
  19.9 3.5 %collective-permute-start.6 = (f32[184,128]{1,0:T(8,128)S(1)}, f32[184,128]{1,0:T(8,128)S(1)}, u32[]{:S(2)}, u32[]{:S(2)}) collective-permute-start(f32[184,128]{1,0:T(8,128)S(1)} %get-tuple-element.22), channel_id=1, source_target_pairs={{0,12},{4,0},{8,4},{12,8},{1,13},{5,1},{9,5},{13,9},{2,14},{6,2},{... | collective-permute-start | bytes 282632 | tf_op jit(solution)/shard_map/ppermute | solution.py:556
  23.4 0.4 collective-permute-done.1.right
  23.8 1.7 %collective-permute-done.5.fleft = f32[184,128]{1,0:T(8,128)S(1)} collective-permute-done((f32[184,128]{1,0:T(8,128)S(1)}, f32[184,128]{1,0:T(8,128)S(1)}, u32[]{:S(2)}, u32[]{:S(2)}) %collective-permute-start.5) | collective-permute-done | bytes 94240 | tf_op jit(solution)/shard_map/ppermute | solution.py:555
  25.5 1.2 %collective-permute-done.6.fright = f32[184,128]{1,0:T(8,128)S(1)} collective-permute-done((f32[184,128]{1,0:T(8,128)S(1)}, f32[184,128]{1,0:T(8,128)S(1)}, u32[]{:S(2)}, u32[]{:S(2)}) %collective-permute-start.6) | collective-permute-done | bytes 94240 | tf_op jit(solution)/shard_map/ppermute | solution.py:556
  26.7 0.0 collective-permute-done.7.fnear
  26.7 0.0 collective-permute-done.8.ffar
  26.7 0.1 shard_map.48
  26.8 0.5 collective-permute-start.10
  27.3 2.1 %collective-permute-start.9 = (f32[504,128]{1,0:T(8,128)S(1)}, f32[504,128]{1,0:T(8,128)S(1)}, u32[]{:S(2)}, u32[]{:S(2)}) collective-permute-start(f32[504,128]{1,0:T(8,128)S(1)} %get-tuple-element.25), channel_id=1, source_target_pairs={{0,0},{1,2},{2,1},{3,3},{4,4},{5,6},{6,5},{7,7},{8,8},{9,10},{10,9... | collective-permute-start | bytes 774152 | tf_op jit(solution)/shard_map/ppermute | solution.py:567
  29.4 2.0 %shard_map.49.count = f32[4,16,24,128]{3,2,1,0:T(8,128)S(1)} custom-call(f32[1160,128]{1,0:T(8,128)S(1)} %get-tuple-element.18.own, f32[1160,128]{1,0:T(8,128)S(1)} %collective-permute-done.2.near, f32[1160,128]{1,0:T(8,128)S(1)} %collective-permute-done.3.far, f32[184,128]{1,0:T(8,128)S(1)} %collective-permute-done.5.fleft, ...), custom_call_target="tpu_custom_call" | custom-call | flops 8000000 | bytes 8000000 | tf_op jit(solution)/shard_map/pallas_call | solution.py:38
  31.4 0.0 copy-done.1
  31.5 0.6 %shard_map.50.given = f32[3,6,20,32,128]{4,3,2,1,0:T(8,128)S(1)} custom-call(f32[3,8,16,512]{3,2,1,0:T(8,128)S(1)} %bitcast.3, f32[576,128]{1,0:T(8,128)S(1)} %collective-permute-done.left, f32[576,128]{1,0:T(8,128)S(1)} %collective-permute-done.1.right, f32[448,128]{1,0:T(8,128)S(1)} %collective-permute-done.4.fringe, ...), custom_call_target="tpu_custom_call" | custom-call | flops 8000000 | bytes 8000000 | tf_op jit(solution)/shard_map/pallas_call | solution.py:38
  32.1 0.0 collective-permute-done.10.cnear
  32.1 2.8 %collective-permute-done.9.cfar = f32[504,128]{1,0:T(8,128)S(1)} collective-permute-done((f32[504,128]{1,0:T(8,128)S(1)}, f32[504,128]{1,0:T(8,128)S(1)}, u32[]{:S(2)}, u32[]{:S(2)}) %collective-permute-start.9) | collective-permute-done | bytes 258080 | tf_op jit(solution)/shard_map/ppermute | solution.py:567
  34.9 14.7 %shard_map.51 = f32[3,8,16,512]{3,2,1,0:T(8,128)} custom-call(s32[1]{0:T(128)S(6)} %copy.6.start.first_column, f32[504,128]{1,0:T(8,128)S(1)} %collective-permute-done.9.cfar, f32[504,128]{1,0:T(8,128)S(1)} %collective-permute-done.10.cnear, f32[4,16,24,128]{3,2,1,0:T(8,128)S(1)} %shard_map.49.count, f32[3,6,20,32,128]{4,3,2,1,0:T(8,128)S(1)} %shard_map.50.given), custom_call_target="tpu_custom_call" | custom-call | flops 8000000 | bytes 8000000 | tf_op jit(solution)/shard_map/pallas_call | solution.py:38
  (1 shorter events, 0.0 us)
Async XLA Ops:
  1.3 1.1 %copy-start = (f32[1,3,8,16,512]{4,3,2,1,0:T(8,128)S(1)}, f32[1,3,8,16,512]{4,3,2,1,0:T(8,128)}, u32[]{:S(2)}) copy-start(f32[1,3,8,16,512]{4,3,2,1,0:T(8,128)} %param.4) | copy-start | bytes 2359300
  2.4 0.7 %copy-start.2 = (s32[1,1,512]{2,1,0:T(1,128)S(1)}, s32[1,1,512]{2,1,0:T(1,128)}, u32[]{:S(2)}) copy-start(s32[1,1,512]{2,1,0:T(1,128)} %cells.1) | copy-start | bytes 6148
  3.1 28.3 %copy-start.1 = (f32[1,3,8,16,512]{4,3,2,1,0:T(8,128)S(1)}, f32[1,3,8,16,512]{4,3,2,1,0:T(8,128)}, u32[]{:S(2)}) copy-start(f32[1,3,8,16,512]{4,3,2,1,0:T(8,128)} %param.4) | copy-start | bytes 2359300
  3.4 9.6 %collective-permute-start.2 = (f32[1160,128]{1,0:T(8,128)S(1)}, f32[1160,128]{1,0:T(8,128)S(1)}, u32[]{:S(2)}, u32[]{:S(2)}) collective-permute-start(f32[1160,128]{1,0:T(8,128)S(1)} %get-tuple-element.18.own), channel_id=1, source_target_pairs={{0,1},{1,0},{2,3},{3,2},{4,5},{5,4},{6,7},{7,6},{8,9},{9,8},{10,11... | collective-permute-start | bytes 1781768 | tf_op jit(solution)/shard_map/ppermute | solution.py:545
  4.1 11.5 %collective-permute-start.3 = (f32[1160,128]{1,0:T(8,128)S(1)}, f32[1160,128]{1,0:T(8,128)S(1)}, u32[]{:S(2)}, u32[]{:S(2)}) collective-permute-start(f32[1160,128]{1,0:T(8,128)S(1)} %get-tuple-element.19), channel_id=1, source_target_pairs={{0,0},{1,2},{2,1},{3,3},{4,4},{5,6},{6,5},{7,7},{8,8},{9,10},{10,9... | collective-permute-start | bytes 1781768 | tf_op jit(solution)/shard_map/ppermute | solution.py:546
  7.1 5.8 %collective-permute-start.4 = (f32[448,128]{1,0:T(8,128)S(1)}, f32[448,128]{1,0:T(8,128)S(1)}, u32[]{:S(2)}, u32[]{:S(2)}) collective-permute-start(f32[448,128]{1,0:T(8,128)S(1)} %get-tuple-element.20), channel_id=1, source_target_pairs={{0,16},{16,0},{1,17},{17,1},{2,18},{18,2},{3,19},{19,3},{4,20},{20... | collective-permute-start | bytes 688136 | tf_op jit(solution)/shard_map/ppermute | solution.py:542
  7.4 12.4 %collective-permute-start = (f32[576,128]{1,0:T(8,128)S(1)}, f32[576,128]{1,0:T(8,128)S(1)}, u32[]{:S(2)}, u32[]{:S(2)}) collective-permute-start(f32[576,128]{1,0:T(8,128)S(1)} %get-tuple-element.16), channel_id=1, source_target_pairs={{0,4},{4,8},{8,12},{12,0},{1,5},{5,9},{9,13},{13,1},{2,6},{6,10},{... | collective-permute-start | bytes 884744 | tf_op jit(solution)/shard_map/ppermute | solution.py:543
  8.7 15.1 %collective-permute-start.1 = (f32[576,128]{1,0:T(8,128)S(1)}, f32[576,128]{1,0:T(8,128)S(1)}, u32[]{:S(2)}, u32[]{:S(2)}) collective-permute-start(f32[576,128]{1,0:T(8,128)S(1)} %get-tuple-element.17), channel_id=1, source_target_pairs={{0,12},{4,0},{8,4},{12,8},{1,13},{5,1},{9,5},{13,9},{2,14},{6,2},{... | collective-permute-start | bytes 884744 | tf_op jit(solution)/shard_map/ppermute | solution.py:544
  15.7 11.0 %collective-permute-start.7 = (f32[352,128]{1,0:T(8,128)S(1)}, f32[352,128]{1,0:T(8,128)S(1)}, u32[]{:S(2)}, u32[]{:S(2)}) collective-permute-start(f32[352,128]{1,0:T(8,128)S(1)} %get-tuple-element.23), channel_id=1, source_target_pairs={{0,1},{1,0},{2,3},{3,2},{4,5},{5,4},{6,7},{7,6},{8,9},{9,8},{10,11... | collective-permute-start | bytes 540680 | tf_op jit(solution)/shard_map/ppermute | solution.py:557
  15.8 10.9 %collective-permute-start.8 = (f32[352,128]{1,0:T(8,128)S(1)}, f32[352,128]{1,0:T(8,128)S(1)}, u32[]{:S(2)}, u32[]{:S(2)}) collective-permute-start(f32[352,128]{1,0:T(8,128)S(1)} %get-tuple-element.24), channel_id=1, source_target_pairs={{0,0},{1,2},{2,1},{3,3},{4,4},{5,6},{6,5},{7,7},{8,8},{9,10},{10,9... | collective-permute-start | bytes 540680 | tf_op jit(solution)/shard_map/ppermute | solution.py:558
  18.5 6.9 %collective-permute-start.5 = (f32[184,128]{1,0:T(8,128)S(1)}, f32[184,128]{1,0:T(8,128)S(1)}, u32[]{:S(2)}, u32[]{:S(2)}) collective-permute-start(f32[184,128]{1,0:T(8,128)S(1)} %get-tuple-element.21), channel_id=1, source_target_pairs={{0,4},{4,8},{8,12},{12,0},{1,5},{5,9},{9,13},{13,1},{2,6},{6,10},{... | collective-permute-start | bytes 282632 | tf_op jit(solution)/shard_map/ppermute | solution.py:555
  19.9 6.8 %collective-permute-start.6 = (f32[184,128]{1,0:T(8,128)S(1)}, f32[184,128]{1,0:T(8,128)S(1)}, u32[]{:S(2)}, u32[]{:S(2)}) collective-permute-start(f32[184,128]{1,0:T(8,128)S(1)} %get-tuple-element.22), channel_id=1, source_target_pairs={{0,12},{4,0},{8,4},{12,8},{1,13},{5,1},{9,5},{13,9},{2,14},{6,2},{... | collective-permute-start | bytes 282632 | tf_op jit(solution)/shard_map/ppermute | solution.py:556
  26.8 5.3 %collective-permute-start.10 = (f32[504,128]{1,0:T(8,128)S(1)}, f32[504,128]{1,0:T(8,128)S(1)}, u32[]{:S(2)}, u32[]{:S(2)}) collective-permute-start(f32[504,128]{1,0:T(8,128)S(1)} %get-tuple-element.26), channel_id=1, source_target_pairs={{0,1},{1,0},{2,3},{3,2},{4,5},{5,4},{6,7},{7,6},{8,9},{9,8},{10,11... | collective-permute-start | bytes 774152 | tf_op jit(solution)/shard_map/ppermute | solution.py:568
  27.3 7.6 %collective-permute-start.9 = (f32[504,128]{1,0:T(8,128)S(1)}, f32[504,128]{1,0:T(8,128)S(1)}, u32[]{:S(2)}, u32[]{:S(2)}) collective-permute-start(f32[504,128]{1,0:T(8,128)S(1)} %get-tuple-element.25), channel_id=1, source_target_pairs={{0,0},{1,2},{2,1},{3,3},{4,4},{5,6},{6,5},{7,7},{8,8},{9,10},{10,9... | collective-permute-start | bytes 774152 | tf_op jit(solution)/shard_map/ppermute | solution.py:567

commit v5 on v4

--- a/solution.py
+++ b/solution.py
@@ -108,7 +108,7 @@
     parity(levels)
 
 
-def pack_window(dims, own, near, far, fringe, fup, fdown, first, second):
+def pack_window_rows(dims, own, near, far, fringe, fup, fdown):
     tiles, depth, width = dims
     half = depth // 2
     listed, list_at = 3 * tiles * HALO * width, (3 * depth + half) * HALO
@@ -118,6 +118,11 @@
     for at in range(3 * depth + half):
         fup[pl.ds(at * HALO, HALO), :] = fringe[pl.ds(at * width + width - HALO, HALO), :]
         fdown[pl.ds(at * HALO, HALO), :] = fringe[pl.ds(at * width, HALO), :]
+
+
+def pack_window_levels(dims, fringe, first, second):
+    tiles, depth, width = dims
+    half = depth // 2
     for out in (first, second):
         for zz in range(half):
             out[pl.ds((3 * HALO + zz) * width, width), :] = fringe[
@@ -544,9 +549,17 @@
     right = lax.ppermute(down, "gy", around("gy", -1))
     near = lax.ppermute(first, "gz", swaps("gz", 0))
     far = lax.ppermute(second, "gz", swaps("gz", 1))
-    fup, fdown, ffirst, fsecond = call(
-        functools.partial(pack_window, dims),
-        shapes(window_halo, window_halo, window_level, window_level),
+    ffirst, fsecond = call(
+        functools.partial(pack_window_levels, dims),
+        shapes(window_level, window_level),
+        (fringe,),
+        0,
+        12,
+        1,
+    )
+    fup, fdown = call(
+        functools.partial(pack_window_rows, dims),
+        shapes(window_halo, window_halo),
         (first, near, far, fringe),
         0,
         12,

time: 49.8 us -> 49.8 us (level)
  waiting for transfers between devices: 11 us -> 8.27 us
  starting transfers between devices: 17.6 us -> 19.2 us
  local copies, waits for them, and re-layouts: 1.81 us -> 2.94 us
    ppermute x1, waiting for transfers between devices: 2.66 us -> 0.01 us  [per_device(): far = lax.ppermute(second, 'gz', swaps('gz', 1))]
    ppermute x1, starting transfers between devices: 3.51 us -> 4.9 us  [per_device(): fright = lax.ppermute(fdown, 'gy', around('gy', -1))]
    unnamed x6, local copies, waits for them, and re-layouts: 1.81 us -> 2.94 us
    ppermute x1, waiting for transfers between devices: 2.83 us -> 1.7 us  [per_device(): cfar = lax.ppermute(csecond, 'gz', swaps('gz', 1))]
    ppermute x1, waiting for transfers between devices: 0.01 us -> 0.76 us  [per_device(): left = lax.ppermute(up, 'gy', around('gy', 1))]
    pallas_call x6 -> x7, Pallas kernels: 17.8 us -> 17.8 us  [call(): pl.pallas_call(kernel, out_shape=[jax.ShapeDtypeStruct(shape, jnp.float32...]
where the time goes in v5:
time: 49.8 us; the launch traced here: 49.6 us
  starting transfers between devices  19.2 us (39%)
  Pallas kernels  17.8 us (36%)
  waiting for transfers between devices  8.27 us (17%)
  local copies, waits for them, and re-layouts  2.94 us (6%)
  between operations  1.41 us (3%)
    pallas_call x7, Pallas kernels, call(): pl.pallas_call(kernel, out_shape=[jax.ShapeDtypeStruct(shape, jnp.float32...  17.8 us
    ppermute x1, starting transfers between devices, per_device(): fright = lax.ppermute(fdown, 'gy', around('gy', -1))  4.9 us
    ppermute x1, starting transfers between devices, per_device(): far = lax.ppermute(second, 'gz', swaps('gz', 1))  3.02 us
    unnamed x6, local copies, waits for them, and re-layouts  2.94 us
    ppermute x1, starting transfers between devices, per_device(): ffar = lax.ppermute(fsecond, 'gz', swaps('gz', 1))  2.92 us
    ppermute x1, waiting for transfers between devices, per_device(): fringe = lax.ppermute(fringe, 'box', [(0, 1), (1, 0)])  2.23 us
    ppermute x1, starting transfers between devices, per_device(): cfar = lax.ppermute(csecond, 'gz', swaps('gz', 1))  2.14 us
    ppermute x1, starting transfers between devices, per_device(): right = lax.ppermute(down, 'gy', around('gy', -1))  2.03 us
  transfers between devices with their start and end apart: 11, of which 6 were waited for; matrix products, arithmetic and copies ran while one was open for 0% of the time, Pallas kernels for 5%

profile of v5, /device:TPU:5, one launch (start us, length us, event | category | flops | bytes accessed | tf_op | source)
XLA Modules:
  0.0 49.6 jit_solution(8231714086755830976)
XLA Ops:
  1.3 0.0 copy-start
  1.3 1.1 %copy-done = f32[1,3,8,16,512]{4,3,2,1,0:T(8,128)S(1)} copy-done((f32[1,3,8,16,512]{4,3,2,1,0:T(8,128)S(1)}, f32[1,3,8,16,512]{4,3,2,1,0:T(8,128)}, u32[]{:S(2)}) %copy-start) | copy-done | bytes 786456
  2.4 0.0 copy-start.2
  2.4 0.7 %copy-done.2 = s32[1,1,512]{2,1,0:T(1,128)S(1)} copy-done((s32[1,1,512]{2,1,0:T(1,128)S(1)}, s32[1,1,512]{2,1,0:T(1,128)}, u32[]{:S(2)}) %copy-start.2) | copy-done | bytes 2072
  3.1 0.3 shard_map.46
  3.4 0.7 %collective-permute-start.2 = (f32[1160,128]{1,0:T(8,128)S(1)}, f32[1160,128]{1,0:T(8,128)S(1)}, u32[]{:S(2)}, u32[]{:S(2)}) collective-permute-start(f32[1160,128]{1,0:T(8,128)S(1)} %get-tuple-element.18.own), channel_id=1, source_target_pairs={{0,1},{1,0},{2,3},{3,2},{4,5},{5,4},{6,7},{7,6},{8,9},{9,8},{10,11... | collective-permute-start | bytes 1781768 | tf_op jit(solution)/shard_map/ppermute | solution.py:550
  4.1 3.0 %collective-permute-start.3 = (f32[1160,128]{1,0:T(8,128)S(1)}, f32[1160,128]{1,0:T(8,128)S(1)}, u32[]{:S(2)}, u32[]{:S(2)}) collective-permute-start(f32[1160,128]{1,0:T(8,128)S(1)} %get-tuple-element.19), channel_id=1, source_target_pairs={{0,0},{1,2},{2,1},{3,3},{4,4},{5,6},{6,5},{7,7},{8,8},{9,10},{10,9... | collective-permute-start | bytes 1781768 | tf_op jit(solution)/shard_map/ppermute | solution.py:551
  7.1 0.3 collective-permute-start.4
  7.4 1.3 %collective-permute-start = (f32[576,128]{1,0:T(8,128)S(1)}, f32[576,128]{1,0:T(8,128)S(1)}, u32[]{:S(2)}, u32[]{:S(2)}) collective-permute-start(f32[576,128]{1,0:T(8,128)S(1)} %get-tuple-element.16), channel_id=1, source_target_pairs={{0,4},{4,8},{8,12},{12,0},{1,5},{5,9},{9,13},{13,1},{2,6},{6,10},{... | collective-permute-start | bytes 884744 | tf_op jit(solution)/shard_map/ppermute | solution.py:548
  8.7 2.0 %collective-permute-start.1 = (f32[576,128]{1,0:T(8,128)S(1)}, f32[576,128]{1,0:T(8,128)S(1)}, u32[]{:S(2)}, u32[]{:S(2)}) collective-permute-start(f32[576,128]{1,0:T(8,128)S(1)} %get-tuple-element.17), channel_id=1, source_target_pairs={{0,12},{4,0},{8,4},{12,8},{1,13},{5,1},{9,5},{13,9},{2,14},{6,2},{... | collective-permute-start | bytes 884744 | tf_op jit(solution)/shard_map/ppermute | solution.py:549
  10.8 2.2 %collective-permute-done.4.fringe = f32[448,128]{1,0:T(8,128)S(1)} collective-permute-done((f32[448,128]{1,0:T(8,128)S(1)}, f32[448,128]{1,0:T(8,128)S(1)}, u32[]{:S(2)}, u32[]{:S(2)}) %collective-permute-start.4) | collective-permute-done | bytes 229408 | tf_op jit(solution)/shard_map/ppermute | solution.py:547
  13.0 0.1 collective-permute-start.7
  13.1 0.0 collective-permute-done.2.near
  13.1 2.9 %collective-permute-start.8 = (f32[352,128]{1,0:T(8,128)S(1)}, f32[352,128]{1,0:T(8,128)S(1)}, u32[]{:S(2)}, u32[]{:S(2)}) collective-permute-start(f32[352,128]{1,0:T(8,128)S(1)} %get-tuple-element.24), channel_id=1, source_target_pairs={{0,0},{1,2},{2,1},{3,3},{4,4},{5,6},{6,5},{7,7},{8,8},{9,10},{10,9... | collective-permute-start | bytes 540680 | tf_op jit(solution)/shard_map/ppermute | solution.py:571
  16.0 0.0 collective-permute-done.3.far
  16.1 1.3 %collective-permute-start.5 = (f32[184,128]{1,0:T(8,128)S(1)}, f32[184,128]{1,0:T(8,128)S(1)}, u32[]{:S(2)}, u32[]{:S(2)}) collective-permute-start(f32[184,128]{1,0:T(8,128)S(1)} %get-tuple-element.21), channel_id=1, source_target_pairs={{0,4},{4,8},{8,12},{12,0},{1,5},{5,9},{9,13},{13,1},{2,6},{6,10},{... | collective-permute-start | bytes 282632 | tf_op jit(solution)/shard_map/ppermute | solution.py:568
  17.4 0.8 %collective-permute-done.left = f32[576,128]{1,0:T(8,128)S(1)} collective-permute-done((f32[576,128]{1,0:T(8,128)S(1)}, f32[576,128]{1,0:T(8,128)S(1)}, u32[]{:S(2)}, u32[]{:S(2)}) %collective-permute-start) | collective-permute-done | bytes 294944 | tf_op jit(solution)/shard_map/ppermute | solution.py:548
  18.2 4.9 %collective-permute-start.6 = (f32[184,128]{1,0:T(8,128)S(1)}, f32[184,128]{1,0:T(8,128)S(1)}, u32[]{:S(2)}, u32[]{:S(2)}) collective-permute-start(f32[184,128]{1,0:T(8,128)S(1)} %get-tuple-element.22), channel_id=1, source_target_pairs={{0,12},{4,0},{8,4},{12,8},{1,13},{5,1},{9,5},{13,9},{2,14},{6,2},{... | collective-permute-start | bytes 282632 | tf_op jit(solution)/shard_map/ppermute | solution.py:569
  23.1 0.9 %collective-permute-done.1.right = f32[576,128]{1,0:T(8,128)S(1)} collective-permute-done((f32[576,128]{1,0:T(8,128)S(1)}, f32[576,128]{1,0:T(8,128)S(1)}, u32[]{:S(2)}, u32[]{:S(2)}) %collective-permute-start.1) | collective-permute-done | bytes 294944 | tf_op jit(solution)/shard_map/ppermute | solution.py:549
  24.0 0.0 collective-permute-done.7.fnear
  24.0 0.0 collective-permute-done.8.ffar
  24.0 1.8 %collective-permute-done.5.fleft = f32[184,128]{1,0:T(8,128)S(1)} collective-permute-done((f32[184,128]{1,0:T(8,128)S(1)}, f32[184,128]{1,0:T(8,128)S(1)}, u32[]{:S(2)}, u32[]{:S(2)}) %collective-permute-start.5) | collective-permute-done | bytes 94240 | tf_op jit(solution)/shard_map/ppermute | solution.py:568
  25.8 0.9 %collective-permute-done.6.fright = f32[184,128]{1,0:T(8,128)S(1)} collective-permute-done((f32[184,128]{1,0:T(8,128)S(1)}, f32[184,128]{1,0:T(8,128)S(1)}, u32[]{:S(2)}, u32[]{:S(2)}) %collective-permute-start.6) | collective-permute-done | bytes 94240 | tf_op jit(solution)/shard_map/ppermute | solution.py:569
  26.7 0.1 shard_map.49
  26.8 0.5 collective-permute-start.10
  27.2 2.1 %collective-permute-start.9 = (f32[504,128]{1,0:T(8,128)S(1)}, f32[504,128]{1,0:T(8,128)S(1)}, u32[]{:S(2)}, u32[]{:S(2)}) collective-permute-start(f32[504,128]{1,0:T(8,128)S(1)} %get-tuple-element.25), channel_id=1, source_target_pairs={{0,0},{1,2},{2,1},{3,3},{4,4},{5,6},{6,5},{7,7},{8,8},{9,10},{10,9... | collective-permute-start | bytes 774152 | tf_op jit(solution)/shard_map/ppermute | solution.py:580
  29.4 0.0 copy-start.1
  29.4 1.1 %copy-done.1 = f32[1,3,8,16,512]{4,3,2,1,0:T(8,128)S(1)} copy-done((f32[1,3,8,16,512]{4,3,2,1,0:T(8,128)S(1)}, f32[1,3,8,16,512]{4,3,2,1,0:T(8,128)}, u32[]{:S(2)}) %copy-start.1) | copy-done | bytes 786456
  30.5 0.6 %shard_map.51.given = f32[3,6,20,32,128]{4,3,2,1,0:T(8,128)S(1)} custom-call(f32[3,8,16,512]{3,2,1,0:T(8,128)S(1)} %bitcast.3, f32[576,128]{1,0:T(8,128)S(1)} %collective-permute-done.left, f32[576,128]{1,0:T(8,128)S(1)} %collective-permute-done.1.right, f32[448,128]{1,0:T(8,128)S(1)} %collective-permute-done.4.fringe, ...), custom_call_target="tpu_custom_call" | custom-call | flops 8000000 | bytes 8000000 | tf_op jit(solution)/shard_map/pallas_call | solution.py:38
  31.1 2.0 %shard_map.50.count = f32[4,16,24,128]{3,2,1,0:T(8,128)S(1)} custom-call(f32[1160,128]{1,0:T(8,128)S(1)} %get-tuple-element.18.own, f32[1160,128]{1,0:T(8,128)S(1)} %collective-permute-done.2.near, f32[1160,128]{1,0:T(8,128)S(1)} %collective-permute-done.3.far, f32[184,128]{1,0:T(8,128)S(1)} %collective-permute-done.5.fleft, ...), custom_call_target="tpu_custom_call" | custom-call | flops 8000000 | bytes 8000000 | tf_op jit(solution)/shard_map/pallas_call | solution.py:38
  33.2 0.0 collective-permute-done.10.cnear
  33.2 1.7 %collective-permute-done.9.cfar = f32[504,128]{1,0:T(8,128)S(1)} collective-permute-done((f32[504,128]{1,0:T(8,128)S(1)}, f32[504,128]{1,0:T(8,128)S(1)}, u32[]{:S(2)}, u32[]{:S(2)}) %collective-permute-start.9) | collective-permute-done | bytes 258080 | tf_op jit(solution)/shard_map/ppermute | solution.py:580
  34.9 14.7 %shard_map.52 = f32[3,8,16,512]{3,2,1,0:T(8,128)} custom-call(s32[1]{0:T(128)S(6)} %copy.6.start.first_column, f32[504,128]{1,0:T(8,128)S(1)} %collective-permute-done.9.cfar, f32[504,128]{1,0:T(8,128)S(1)} %collective-permute-done.10.cnear, f32[4,16,24,128]{3,2,1,0:T(8,128)S(1)} %shard_map.50.count, f32[3,6,20,32,128]{4,3,2,1,0:T(8,128)S(1)} %shard_map.51.given), custom_call_target="tpu_custom_call" | custom-call | flops 8000000 | bytes 8000000 | tf_op jit(solution)/shard_map/pallas_call | solution.py:38
  (2 shorter events, 0.0 us)
Async XLA Ops:
  1.3 1.1 %copy-start = (f32[1,3,8,16,512]{4,3,2,1,0:T(8,128)S(1)}, f32[1,3,8,16,512]{4,3,2,1,0:T(8,128)}, u32[]{:S(2)}) copy-start(f32[1,3,8,16,512]{4,3,2,1,0:T(8,128)} %param.4) | copy-start | bytes 2359300
  2.4 0.7 %copy-start.2 = (s32[1,1,512]{2,1,0:T(1,128)S(1)}, s32[1,1,512]{2,1,0:T(1,128)}, u32[]{:S(2)}) copy-start(s32[1,1,512]{2,1,0:T(1,128)} %cells.1) | copy-start | bytes 6148
  3.4 9.7 %collective-permute-start.2 = (f32[1160,128]{1,0:T(8,128)S(1)}, f32[1160,128]{1,0:T(8,128)S(1)}, u32[]{:S(2)}, u32[]{:S(2)}) collective-permute-start(f32[1160,128]{1,0:T(8,128)S(1)} %get-tuple-element.18.own), channel_id=1, source_target_pairs={{0,1},{1,0},{2,3},{3,2},{4,5},{5,4},{6,7},{7,6},{8,9},{9,8},{10,11... | collective-permute-start | bytes 1781768 | tf_op jit(solution)/shard_map/ppermute | solution.py:550
  4.1 11.9 %collective-permute-start.3 = (f32[1160,128]{1,0:T(8,128)S(1)}, f32[1160,128]{1,0:T(8,128)S(1)}, u32[]{:S(2)}, u32[]{:S(2)}) collective-permute-start(f32[1160,128]{1,0:T(8,128)S(1)} %get-tuple-element.19), channel_id=1, source_target_pairs={{0,0},{1,2},{2,1},{3,3},{4,4},{5,6},{6,5},{7,7},{8,8},{9,10},{10,9... | collective-permute-start | bytes 1781768 | tf_op jit(solution)/shard_map/ppermute | solution.py:551
  7.1 5.8 %collective-permute-start.4 = (f32[448,128]{1,0:T(8,128)S(1)}, f32[448,128]{1,0:T(8,128)S(1)}, u32[]{:S(2)}, u32[]{:S(2)}) collective-permute-start(f32[448,128]{1,0:T(8,128)S(1)} %get-tuple-element.20), channel_id=1, source_target_pairs={{0,16},{16,0},{1,17},{17,1},{2,18},{18,2},{3,19},{19,3},{4,20},{20... | collective-permute-start | bytes 688136 | tf_op jit(solution)/shard_map/ppermute | solution.py:547
  7.4 10.8 %collective-permute-start = (f32[576,128]{1,0:T(8,128)S(1)}, f32[576,128]{1,0:T(8,128)S(1)}, u32[]{:S(2)}, u32[]{:S(2)}) collective-permute-start(f32[576,128]{1,0:T(8,128)S(1)} %get-tuple-element.16), channel_id=1, source_target_pairs={{0,4},{4,8},{8,12},{12,0},{1,5},{5,9},{9,13},{13,1},{2,6},{6,10},{... | collective-permute-start | bytes 884744 | tf_op jit(solution)/shard_map/ppermute | solution.py:548
  8.7 15.2 %collective-permute-start.1 = (f32[576,128]{1,0:T(8,128)S(1)}, f32[576,128]{1,0:T(8,128)S(1)}, u32[]{:S(2)}, u32[]{:S(2)}) collective-permute-start(f32[576,128]{1,0:T(8,128)S(1)} %get-tuple-element.17), channel_id=1, source_target_pairs={{0,12},{4,0},{8,4},{12,8},{1,13},{5,1},{9,5},{13,9},{2,14},{6,2},{... | collective-permute-start | bytes 884744 | tf_op jit(solution)/shard_map/ppermute | solution.py:549
  13.0 10.9 %collective-permute-start.7 = (f32[352,128]{1,0:T(8,128)S(1)}, f32[352,128]{1,0:T(8,128)S(1)}, u32[]{:S(2)}, u32[]{:S(2)}) collective-permute-start(f32[352,128]{1,0:T(8,128)S(1)} %get-tuple-element.23), channel_id=1, source_target_pairs={{0,1},{1,0},{2,3},{3,2},{4,5},{5,4},{6,7},{7,6},{8,9},{9,8},{10,11... | collective-permute-start | bytes 540680 | tf_op jit(solution)/shard_map/ppermute | solution.py:570
  13.1 10.9 %collective-permute-start.8 = (f32[352,128]{1,0:T(8,128)S(1)}, f32[352,128]{1,0:T(8,128)S(1)}, u32[]{:S(2)}, u32[]{:S(2)}) collective-permute-start(f32[352,128]{1,0:T(8,128)S(1)} %get-tuple-element.24), channel_id=1, source_target_pairs={{0,0},{1,2},{2,1},{3,3},{4,4},{5,6},{6,5},{7,7},{8,8},{9,10},{10,9... | collective-permute-start | bytes 540680 | tf_op jit(solution)/shard_map/ppermute | solution.py:571
  16.1 9.7 %collective-permute-start.5 = (f32[184,128]{1,0:T(8,128)S(1)}, f32[184,128]{1,0:T(8,128)S(1)}, u32[]{:S(2)}, u32[]{:S(2)}) collective-permute-start(f32[184,128]{1,0:T(8,128)S(1)} %get-tuple-element.21), channel_id=1, source_target_pairs={{0,4},{4,8},{8,12},{12,0},{1,5},{5,9},{9,13},{13,1},{2,6},{6,10},{... | collective-permute-start | bytes 282632 | tf_op jit(solution)/shard_map/ppermute | solution.py:568
  18.2 8.5 %collective-permute-start.6 = (f32[184,128]{1,0:T(8,128)S(1)}, f32[184,128]{1,0:T(8,128)S(1)}, u32[]{:S(2)}, u32[]{:S(2)}) collective-permute-start(f32[184,128]{1,0:T(8,128)S(1)} %get-tuple-element.22), channel_id=1, source_target_pairs={{0,12},{4,0},{8,4},{12,8},{1,13},{5,1},{9,5},{13,9},{2,14},{6,2},{... | collective-permute-start | bytes 282632 | tf_op jit(solution)/shard_map/ppermute | solution.py:569
  26.8 6.4 %collective-permute-start.10 = (f32[504,128]{1,0:T(8,128)S(1)}, f32[504,128]{1,0:T(8,128)S(1)}, u32[]{:S(2)}, u32[]{:S(2)}) collective-permute-start(f32[504,128]{1,0:T(8,128)S(1)} %get-tuple-element.26), channel_id=1, source_target_pairs={{0,1},{1,0},{2,3},{3,2},{4,5},{5,4},{6,7},{7,6},{8,9},{9,8},{10,11... | collective-permute-start | bytes 774152 | tf_op jit(solution)/shard_map/ppermute | solution.py:581
  27.2 7.6 %collective-permute-start.9 = (f32[504,128]{1,0:T(8,128)S(1)}, f32[504,128]{1,0:T(8,128)S(1)}, u32[]{:S(2)}, u32[]{:S(2)}) collective-permute-start(f32[504,128]{1,0:T(8,128)S(1)} %get-tuple-element.25), channel_id=1, source_target_pairs={{0,0},{1,2},{2,1},{3,3},{4,4},{5,6},{6,5},{7,7},{8,8},{9,10},{10,9... | collective-permute-start | bytes 774152 | tf_op jit(solution)/shard_map/ppermute | solution.py:580
  29.4 1.1 %copy-start.1 = (f32[1,3,8,16,512]{4,3,2,1,0:T(8,128)S(1)}, f32[1,3,8,16,512]{4,3,2,1,0:T(8,128)}, u32[]{:S(2)}) copy-start(f32[1,3,8,16,512]{4,3,2,1,0:T(8,128)} %param.4) | copy-start | bytes 2359300
